TPU v7x, 256 devices: a whole 4x4x8 slice. The times are simulated.
256 devices in a mesh: rep: 32 (over y, x, core), head: 8 (over z).
Axes of the slice: x: 4, y: 4, z: 8, core: 2. Of those that a mesh axis runs over, the one named last changes fastest.
Arguments:
- states: float32 [256, 32, 128, 128], P('rep', 'head'), may hold values from -6 to 6
- alive_flag: int32 [256], P('rep'), may hold values from 0 to 1, as said below
- plan_source: int32 [32, 3], replicated, may hold values from 0 to 7, as said below
- plan_target: int32 [32, 3], replicated, may hold values from 0 to 255, as said below
- move_count: int32 [32], replicated, may hold values from 2 to 3, as said below
- query_proj: bfloat16 [256, 4, 4096], P('rep', None, 'head'), may hold values from -6 to 6
- key_proj: bfloat16 [256, 4, 4096], P('rep', None, 'head'), may hold values from -6 to 6
- value_proj: bfloat16 [256, 4, 4096], P('rep', None, 'head'), may hold values from -6 to 6
- gate_proj: bfloat16 [256, 4, 4096], P('rep', None, 'head'), may hold values from -8 to 8
- decay_rate: float32 [32], P('head'), may hold values from 0.02 to 2
- norm_gain: float32 [4096], P('head'), may hold values from 0.1 to 1.9
Outputs:
- attended: bfloat16 [256, 4, 4096], P('rep', None, 'head')
- new_states: float32 [256, 32, 128, 128], P('rep', 'head')
Inputs may be any that keep to these rules, and one draw needn't show every extreme that they name: `alive_flag`: 1 marks a slot whose row is unfinished before the moves. `plan_source`: for a move in force, the anchor slot is alive and differs from the replica's other anchors in force; other entries are in range and meaningless. `plan_target`: for a move (r, m) in force with g = m // 2, the target is a slot whose alive_flag is 0 on replica (r + d) mod 32, where d = 16 for g = 0 and d = g otherwise; no slot is the target of two moves in force. Other entries are in range and meaningless. `move_count`: the value 3 is reached on some replica in every draw.
All inputs are finite; a program needn't handle non-finite values.
Results may differ from a plain program's by a relative error of at most 0.0011.
Values sent between devices are 32-bit elements; how exact they have to be, the bound alone decides.
No kernel may reach another device: no remote copies, remote signals or barrier semaphores. Data moves between devices by JAX's collectives and lax.ppermute only.
A program may use at most 128 MiB of HBM per device.

v0:
```python
import jax
import jax.numpy as jnp
from jax import lax
from jax.sharding import PartitionSpec as P

HEADS = 32
DK = 128


epsilon = 1e-06


def local(
    states,
    alive_flag,
    plan_source,
    plan_target,
    move_count,
    query_proj,
    key_proj,
    value_proj,
    gate_proj,
    decay_rate,
    norm_gain,
):
    per_device = alive_flag.shape[0]
    head_count = states.shape[1]
    width = states.shape[2]
    move_slots = plan_source.shape[1]
    step_count = query_proj.shape[1]
    my_replica = lax.axis_index("rep")
    move_ids = jnp.arange(move_slots, dtype=jnp.int32)
    slot_ids = jnp.arange(per_device, dtype=jnp.int32)
    is_valid = move_ids[None, :] < move_count[:, None]
    target_dev = plan_target // per_device
    target_slot = plan_target % per_device
    my_valid = lax.dynamic_index_in_dim(is_valid, my_replica, 0, keepdims=False)
    my_source = lax.dynamic_index_in_dim(plan_source, my_replica, 0, keepdims=False)
    leaving = jnp.any(my_valid[:, None] & (my_source[:, None] == slot_ids[None, :]), axis=0)
    staying = (alive_flag == 1) & jnp.logical_not(leaving)
    inbound = is_valid & (target_dev == my_replica)
    hit_table = inbound[:, :, None] & (target_slot[:, :, None] == slot_ids[None, None, :])
    arrives = jnp.any(hit_table, axis=(0, 1))
    outbox = jnp.take(states, my_source, axis=0)
    hit_rows = hit_table.reshape(-1, per_device)
    found_any = jnp.any(hit_rows, axis=0)
    picked = jnp.argmax(hit_rows, axis=0)
    received = jnp.where(
        found_any[:, None, None, None],
        jnp.take(lax.all_gather(outbox, "rep", axis=0, tiled=True), picked, axis=0),
        jnp.zeros(states.shape, jnp.float32),
    )
    current = jnp.where(
        arrives[:, None, None, None], received, jnp.where(staying[:, None, None, None], states, 0.0)
    )

    def activate(projection):
        return jax.nn.silu(projection.astype(jnp.float32)).reshape(
            per_device, step_count, head_count, width
        )

    queries = activate(query_proj)
    keys_now = activate(key_proj)
    values_now = activate(value_proj)
    factor = jnp.exp(-decay_rate)[None, :, None, None]
    feature_total = HEADS * DK
    readouts = []
    for step_index in range(step_count):
        current = (
            factor * current
            + keys_now[:, step_index, :, :, None] * values_now[:, step_index, :, None, :]
        )
        readout = jnp.einsum(
            "bhd,bhde->bhe", queries[:, step_index], current, precision=lax.Precision.HIGHEST
        ).reshape(per_device, head_count * width)
        square_sum = lax.psum(jnp.sum(readout * readout, axis=1), "head")
        readout = readout * lax.rsqrt(square_sum / feature_total + epsilon)[:, None]
        readouts.append(readout)
    stacked = jnp.stack(readouts, 1)
    gated_rows = stacked * norm_gain * jax.nn.sigmoid(gate_proj.astype(jnp.float32))
    live_rows = arrives | staying
    attended = jnp.where(live_rows[:, None, None], gated_rows, 0.0).astype(jnp.bfloat16)
    new_states = jnp.where(live_rows[:, None, None, None], current, 0.0)
    return (attended, new_states)


def solution(mesh):
    return jax.shard_map(
        local,
        mesh=mesh,
        in_specs=(
            P("rep", "head", None, None),
            P("rep"),
            P(),
            P(),
            P(),
            P("rep", None, "head"),
            P("rep", None, "head"),
            P("rep", None, "head"),
            P("rep", None, "head"),
            P("head"),
            P("head"),
        ),
        out_specs=(P("rep", None, "head"), P("rep", "head", None, None)),
        check_vma=False,
    )
```

profile of v0, /device:TPU:32, one launch (start us, length us, event | category | flops | bytes accessed | tf_op | source)
XLA Modules:
  0.0 160.0 jit_solution(9789419022595262156)
XLA Ops:
  7.2 0.0 copy-start
  7.2 0.0 copy-start.5
  7.2 0.0 copy-start.8
  7.2 0.0 copy-start.1
  7.2 0.0 all-gather.2.cloned.1.call-start
  7.3 0.6 copy-done
  7.9 0.2 dynamic-slice_reduce_fusion
  8.1 0.0 copy-start.2
  8.1 0.0 copy-start.3
  8.1 0.0 copy-start.9
  8.1 0.0 copy-start.7
  8.1 2.2 %gather_fusion = f32[3,4,128,128]{3,2,1,0:T(8,128)S(1)} fusion(f32[8,4,128,128]{3,2,1,0:T(8,128)} %param.11, s32[1024]{0:T(1024)S(1)} %pad_clamp_fusion.1), kind=kCustom, calls=%fused_computation | custom fusion | bytes 1572876 | tf_op jit(solution)/shard_map/jit(_take)/gather | solution.py:44
  10.3 1.0 broadcast_select_fusion
  11.4 0.0 all-gather.2.cloned.1.call-update
  11.4 0.0 copy-done.5
  11.4 0.0 copy-done.8
  11.4 0.2 dynamic-slice_reduce_fusion.1
  11.6 0.1 copy.49
  11.7 0.1 and.65
  11.8 0.1 copy.50
  11.9 0.1 eq.60
  12.0 0.0 copy-done.1
  12.2 0.0 copy-done.2
  12.3 0.0 copy-done.3
  12.4 0.6 iota_reduce_fusion
  13.0 0.1 fusion.18
  13.1 0.1 fusion.16
  13.3 0.1 fusion.22
  13.4 0.0 copy-done.9
  13.4 0.0 copy-done.7
  13.5 97.8 %all-gather.2.cloned.1.call-done = f32[96,4,128,128]{3,2,1,0:T(8,128)} async-done(((f32[3,4,128,128]{3,2,1,0:T(8,128)}), f32[96,4,128,128]{3,2,1,0:T(8,128)}) %all-gather.2.cloned.1.call-update) | async-done | bytes 25165840 | tf_op jit(solution)/shard_map/all_gather | solution.py:50
  111.3 8.8 %gather_fusion.1 = f32[8,4,128,128]{3,2,1,0:T(8,128)S(1)} fusion(f32[96,4,128,128]{3,2,1,0:T(8,128)} %all-gather.2.cloned.1.call-done, s32[1024]{0:T(1024)S(1)} %pad_clamp_fusion), kind=kCustom, calls=%fused_computation.1 | custom fusion | bytes 4194336 | tf_op jit(solution)/shard_map/jit(_take)/gather | solution.py:50
  120.1 5.1 %fusion.1 = (f32[8,4,128,128]{3,2,1,0:T(8,128)}, f32[8,4,128,128]{3,2,1,0:T(8,128)S(1)}) fusion(f32[8,4,128]{2,1,0:T(4,128)S(1)} %get-tuple-element.23, f32[8,4,128]{2,1,0:T(4,128)S(1)} %get-tuple-element.26, f32[4]{0:T(128)S(1)} %negate_exponential_fusion, pred[8]{0:T(512)(128)(4,1)S(1)} %get-tuple-element.10, f32[8,4,128]{2,1,0:T(4,128)S(1)} %get-tuple-element.21, ...), kind=kLoop, calls=%fused_computation.7 | loop fusion | flops 8912896 | bytes 8519736 | tf_op jit(solution)/shard_map/jit(_where)/select_n | solution.py:83
  125.2 1.9 %fusion.28 = f32[8,4,1,128]{3,2,1,0:T(1,128)S(1)} fusion(f32[8,4,128,1]{2,3,1,0:T(1,128)S(1)} %bitcast.80, f32[8,4,128,128]{3,2,1,0:T(8,128)S(1)} %get-tuple-element.9), kind=kOutput, calls=%fused_computation.87 | convolution fusion | flops 6291456 | bytes 2129920 | tf_op jit(solution)/shard_map/bhd,bhde->bhe/dot_general | solution.py:73
  127.1 0.1 multiply_reduce_fusion.3
  127.2 2.1 %fusion = f32[8,4,1,128]{3,2,1,0:T(1,128)S(1)} fusion(f32[8,4,128,1]{2,3,1,0:T(1,128)S(1)} %bitcast.79, f32[8,4,128,128]{3,2,1,0:T(8,128)S(1)} %get-tuple-element.9, f32[8,4,128]{2,1,0:T(4,128)S(1)} %get-tuple-element.22, f32[8,4,128]{2,1,0:T(4,128)S(1)} %get-tuple-element.27, f32[4]{0:T(128)S(1)} %negate_exponential_fusion), kind=kOutput, calls=%fused_computation.6 | convolution fusion | flops 7864320 | bytes 2162704 | tf_op jit(solution)/shard_map/bhd,bhde->bhe/dot_general | solution.py:73
  129.3 0.1 multiply_reduce_fusion.2
  129.4 2.8 %fusion.25 = f32[8,4,1,128]{3,2,1,0:T(1,128)S(1)} fusion(f32[8,4,128,1]{2,3,1,0:T(1,128)S(1)} %bitcast.84, f32[8,4,128,128]{3,2,1,0:T(8,128)S(1)} %get-tuple-element.9, f32[8,4,128]{2,1,0:T(4,128)S(1)} %get-tuple-element.21, f32[8,4,128]{2,1,0:T(4,128)S(1)} %get-tuple-element.28, f32[8,4,128]{2,1,0:T(4,128)S(1)} %get-tuple-element.22, ...), kind=kOutput, calls=%fused_computation.84 | convolution fusion | flops 9437184 | bytes 2195472 | tf_op jit(solution)/shard_map/bhd,bhde->bhe/dot_general | solution.py:73
  132.3 0.1 multiply_reduce_fusion.1
  132.4 0.0 copy-start.4
  132.4 0.0 copy-start.6
  132.4 3.4 %fusion.2 = f32[8,4,1,128]{3,2,1,0:T(1,128)S(1)} fusion(f32[8,4,128,1]{2,3,1,0:T(1,128)S(1)} %bitcast.83, f32[8,4,128]{2,1,0:T(4,128)S(1)} %get-tuple-element.23, f32[8,4,128]{2,1,0:T(4,128)S(1)} %get-tuple-element.26, f32[4]{0:T(128)S(1)} %negate_exponential_fusion, f32[8,4,128,128]{3,2,1,0:T(8,128)S(1)} %get-tuple-element.9, ...), kind=kOutput, calls=%fused_computation.8 | convolution fusion | flops 11010048 | bytes 2228240 | tf_op jit(solution)/shard_map/bhd,bhde->bhe/dot_general | solution.py:73
  135.8 0.1 multiply_reduce_fusion
  135.9 16.1 %all-reduce = (f32[8]{0:T(128)S(1)}, f32[8]{0:T(128)S(1)}, f32[8]{0:T(128)S(1)}, f32[8]{0:T(128)S(1)}) all-reduce(f32[8]{0:T(128)S(1)} %multiply_reduce_fusion, f32[8]{0:T(128)S(1)} %multiply_reduce_fusion.1, f32[8]{0:T(128)S(1)} %multiply_reduce_fusion.2, f32[8]{0:T(128)S(1)} %multiply_reduce_fusion.3), channel_id=1, replica_groups=mesh['rep'=32,'head'=8] {'head'}, use_global_device_ids=true, to_apply=%region_11.12 | all-reduce | flops 32 | bytes 256 | tf_op jit(solution)/shard_map/psum | solution.py:76
  152.0 0.1 bitcast_multiply_fusion.3
  152.1 0.1 bitcast_multiply_fusion.2
  152.2 0.1 bitcast_multiply_fusion.1
  152.3 0.1 bitcast_multiply_fusion
  152.4 0.0 copy-done.4
  152.4 0.0 copy-done.6
  152.4 0.7 select_convert_fusion
  (21 shorter events, 0.4 us)
Async XLA Ops:
  7.2 0.7 copy-start
  7.2 4.2 %copy-start.5 = (s32[32,3]{0,1:T(4,128)S(1)}, s32[32,3]{0,1:T(4,128)}, u32[]{:S(2)}) copy-start(s32[32,3]{0,1:T(4,128)} %param.14) | copy-start | bytes 1156
  7.2 4.2 %copy-start.8 = (s32[32]{0:T(128)S(1)}, s32[32]{0:T(128)}, u32[]{:S(2)}) copy-start(s32[32]{0:T(128)} %param.15) | copy-start | bytes 388
  7.2 4.8 %copy-start.1 = (bf16[8,4,512]{2,1,0:T(4,128)(2,1)S(1)}, bf16[8,4,512]{2,1,0:T(4,128)(2,1)}, u32[]{:S(2)}) copy-start(bf16[8,4,512]{2,1,0:T(4,128)(2,1)} %param.17) | copy-start | bytes 98308
  7.2 104.1 %all-gather.2.cloned.1.call-start = ((), (), s32[]{:S(2)}) async-start(), calls=%async_computation | async-start | bytes 25952256 | tf_op jit(solution)/shard_map/all_gather | solution.py:50
  8.1 4.1 %copy-start.2 = (bf16[8,4,512]{2,1,0:T(4,128)(2,1)S(1)}, bf16[8,4,512]{2,1,0:T(4,128)(2,1)}, u32[]{:S(2)}) copy-start(bf16[8,4,512]{2,1,0:T(4,128)(2,1)} %param.18) | copy-start | bytes 98308
  8.1 4.2 %copy-start.3 = (bf16[8,4,512]{2,1,0:T(4,128)(2,1)S(1)}, bf16[8,4,512]{2,1,0:T(4,128)(2,1)}, u32[]{:S(2)}) copy-start(bf16[8,4,512]{2,1,0:T(4,128)(2,1)} %param.16) | copy-start | bytes 98308
  8.1 5.3 %copy-start.9 = (f32[4]{0:T(128)S(1)}, f32[4]{0:T(128)}, u32[]{:S(2)}) copy-start(f32[4]{0:T(128)} %param.20) | copy-start | bytes 52
  8.1 5.3 %copy-start.7 = (s32[8]{0:T(128)S(1)}, s32[8]{0:T(128)}, u32[]{:S(2)}) copy-start(s32[8]{0:T(128)} %param.12) | copy-start | bytes 100
  132.4 20.0 %copy-start.4 = (bf16[8,4,512]{2,1,0:T(4,128)(2,1)S(1)}, bf16[8,4,512]{2,1,0:T(4,128)(2,1)}, u32[]{:S(2)}) copy-start(bf16[8,4,512]{2,1,0:T(4,128)(2,1)} %param.19) | copy-start | bytes 98308
  132.4 20.0 %copy-start.6 = (f32[512]{0:T(512)S(1)}, f32[512]{0:T(512)}, u32[]{:S(2)}) copy-start(f32[512]{0:T(512)} %param.21) | copy-start | bytes 6148
Sparse Core Ops, SparseCore 0:
  11.5 99.7 all-gather.1
where the time goes:
time: 162 us; the launch traced here: 160 us
  waiting for transfers between devices  97.8 us (60%)
  blocking collectives  16.1 us (10%)
  between operations  14.3 us (9%)
  local copies, waits for them, and re-layouts  12.6 us (8%)
  matrix products  10.2 us (6%)
  other arithmetic  8.92 us (6%)
    all_gather x1, waiting for transfers between devices, local(): lax.all_gather(outbox, 'rep', axis=0, tiled=True)  97.8 us
    psum x1, blocking collectives, local(): square_sum = lax.psum(jnp.sum(readout * readout, axis=1), 'head')  16.1 us
    dot_general x4, matrix products, local(): jnp.einsum('bhd,bhde->bhe', queries[:, step_index], current, precision=la...  10.2 us
    gather x1, local copies, waits for them, and re-layouts, local(): jnp.take(lax.all_gather(outbox, 'rep', axis=0, tiled=True), picked, axis=0)  8.84 us
    select_n x1, other arithmetic, local(): new_states = jnp.where(live_rows[:, None, None, None], current, 0.0)  5.07 us
  transfers between devices with their start and end apart: 1, of which 1 were waited for; matrix products, arithmetic and copies ran while one was open for 1% of the time, Pallas kernels for 0%

commit v1 on v0

v1 whole, which is shorter than its diff:
```python
import jax
import jax.numpy as jnp
from jax import lax
from jax.experimental import pallas as pl
from jax.experimental.pallas import tpu as pltpu
from jax.sharding import PartitionSpec as P

SLOTS_DEV = 8
MOVE = 3
STEPS = 4
N_REP = 32
N_HEAD = 8
HEADS = 32
DK = 128
HEADS_DEV = HEADS // N_HEAD
WIDTH = HEADS_DEV * DK
FAR = N_REP // 2
epsilon = 1e-06

HIGHEST = lax.Precision.HIGHEST
VMEM = pl.BlockSpec(memory_space=pltpu.VMEM)
SMEM = pl.BlockSpec(memory_space=pltpu.SMEM)
ANY = pl.BlockSpec(memory_space=pl.ANY)


def silu(x):
    x = x.astype(jnp.float32)
    return x / (1.0 + jnp.exp(-x))


def sender_of(move):
    me = lax.axis_index("rep")
    return lax.rem(me + (FAR if move < 2 else N_REP - 1), N_REP)


def comes_to(move, target_ref, count_ref):
    sender = sender_of(move)
    return count_ref[sender] > move, lax.rem(target_ref[sender, move], SLOTS_DEV)


def slot_flags(slot, alive_ref, source_ref, target_ref, count_ref):
    me = lax.axis_index("rep")
    leaves = False
    arrives = False
    for move in range(MOVE):
        leaves |= (count_ref[me] > move) & (source_ref[me, move] == slot)
        valid, at = comes_to(move, target_ref, count_ref)
        arrives |= valid & (at == slot)
    return (alive_ref[slot] == 1) & jnp.logical_not(leaves), arrives


def step_column(height=STEPS):
    return lax.broadcasted_iota(jnp.int32, (height, DK), 0).astype(jnp.float32)


def head_slice(head):
    return slice(head * DK, (head + 1) * DK)


def ask_kernel(target_ref, count_ref, query_ref, out_ref):
    for move in range(2):
        _, slot = comes_to(move, target_ref, count_ref)
        out_ref[move] = silu(query_ref[slot])


def outbox_kernel(source_ref, states_ref, far_ref, near_ref, sems):
    me = lax.axis_index("rep")
    copies = []
    for move in range(MOVE):
        out = far_ref.at[move] if move < 2 else near_ref.at[0]
        copies.append(pltpu.make_async_copy(states_ref.at[source_ref[me, move]], out, sems.at[move]))
    for copy in copies:
        copy.start()
    for copy in copies:
        copy.wait()


def answer_kernel(query_ref, far_ref, out_ref):
    for move in range(2):
        for head in range(HEADS_DEV):
            out_ref[move, :, head_slice(head)] = jnp.dot(
                query_ref[move, :, head_slice(head)], far_ref[move, head],
                precision=HIGHEST, preferred_element_type=jnp.float32)


def main_kernel(alive_ref, source_ref, target_ref, count_ref, rate_ref, query_ref, key_ref, value_ref, states_ref, out_ref, new_ref):
    slot = pl.program_id(0)
    stays, arrives = slot_flags(slot, alive_ref, source_ref, target_ref, count_ref)
    live = (stays | arrives).astype(jnp.float32)
    stays = stays.astype(jnp.float32)
    queries, keys, values = silu(query_ref[slot]), silu(key_ref[slot]), silu(value_ref[slot])
    steps = step_column()
    later = lax.broadcasted_iota(jnp.int32, (STEPS, STEPS), 0) - lax.broadcasted_iota(jnp.int32, (STEPS, STEPS), 1)
    for head in range(HEADS_DEV):
        rate = rate_ref[head]
        query, key, value = (x[:, head_slice(head)] for x in (queries, keys, values))
        state = states_ref[0, head] * stays
        weights = lax.dot_general(query, key, (((1,), (1,)), ((), ())), precision=HIGHEST, preferred_element_type=jnp.float32)
        weights = jnp.where(later >= 0, weights * jnp.exp(-rate * jnp.maximum(later, 0).astype(jnp.float32)), 0.0)
        inside = jnp.dot(weights, value, precision=HIGHEST, preferred_element_type=jnp.float32)
        before = jnp.dot(query, state, precision=HIGHEST, preferred_element_type=jnp.float32)
        out_ref[slot, :, head_slice(head)] = inside + before * jnp.exp(-rate * (steps + 1.0))
        faded = key * jnp.exp(-rate * (STEPS - 1.0 - steps))
        added = lax.dot_general(faded, value, (((0,), (0,)), ((), ())), precision=HIGHEST, preferred_element_type=jnp.float32)
        fade = jnp.exp(jnp.full((8, DK), -STEPS * rate, jnp.float32))[:1]
        new_ref[0, head] = (state * fade + added) * live


def combine_kernel(target_ref, count_ref, rate_ref, query_ref, answer_ref, near_ref, part_ref, out_ref, square_ref):
    out_ref[...] = part_ref[...]
    steps = step_column()
    for move in range(MOVE):
        valid, slot = comes_to(move, target_ref, count_ref)

        @pl.when(valid)
        def _(move=move, slot=slot):
            for head in range(HEADS_DEV):
                at = head_slice(head)
                if move < 2:
                    before = answer_ref[move, :, at]
                else:
                    before = jnp.dot(silu(query_ref[slot, :, at]), near_ref[0, head], precision=HIGHEST, preferred_element_type=jnp.float32)
                out_ref[slot, :, at] += before * jnp.exp(-rate_ref[head] * (steps + 1.0))

    total = jnp.zeros((SLOTS_DEV, STEPS, DK), jnp.float32)
    for head in range(HEADS_DEV):
        row = out_ref[:, :, head_slice(head)]
        total += row * row
    square_ref[...] = total


def final_kernel(alive_ref, source_ref, target_ref, count_ref, gain_ref, gate_ref, out_ref, square_a_ref, square_b_ref, attended_ref):
    gain = gain_ref[...]
    for slot in range(SLOTS_DEV):
        stays, arrives = slot_flags(slot, alive_ref, source_ref, target_ref, count_ref)
        live = (stays | arrives).astype(jnp.float32)
        total = jnp.sum(square_a_ref[slot] + square_b_ref[slot], axis=1, keepdims=True)
        scale = lax.rsqrt(total * (1.0 / (HEADS * DK)) + epsilon) * live
        gate = gate_ref[slot].astype(jnp.float32)
        row = out_ref[slot] * scale * gain / (1.0 + jnp.exp(-gate))
        attended_ref[slot] = row.astype(jnp.bfloat16)


def place_of(target_ref, count_ref, move):
    slots = [comes_to(m, target_ref, count_ref) for m in range(MOVE)]
    at = slots[0][1]
    for m in range(1, MOVE):
        at = jnp.where((move >= m) & slots[m][0], slots[m][1], at)
    return at


def update_kernel(target_ref, count_ref, rate_ref, far_ref, near_ref, old_ref, new_ref):
    move = pl.program_id(0)
    for m in range(MOVE):
        valid, _ = comes_to(m, target_ref, count_ref)

        @pl.when((move == m) & valid)
        def _(m=m):
            for head in range(HEADS_DEV):
                fade = jnp.exp(jnp.full((8, DK), -STEPS * rate_ref[head], jnp.float32))[:1]
                came = far_ref[0, head] if m < 2 else near_ref[0, head]
                new_ref[0, head] = old_ref[0, head] + came * fade


def call(kernel, outs, in_specs, args, cost=100_000, **more):
    if in_specs is not None:
        more["in_specs"] = in_specs
    return pl.pallas_call(
        kernel, out_shape=outs,
        cost_estimate=pl.CostEstimate(flops=cost, bytes_accessed=cost, transcendentals=0), **more,
    )(*args)


def f32(*shape):
    return jax.ShapeDtypeStruct(shape, jnp.float32)


def over_rep(x, distance):
    return lax.ppermute(x, "rep", [(i, (i + distance) % N_REP) for i in range(N_REP)])


def over_head(x, flip):
    return lax.ppermute(x, "head", [(i, i ^ flip) for i in range(N_HEAD)])


def local(states, alive_flag, plan_source, plan_target, move_count, query_proj, key_proj, value_proj, gate_proj, decay_rate, norm_gain):
    row = (HEADS_DEV, DK, DK)
    plan = (plan_target, move_count)
    flags = (alive_flag, plan_source, plan_target, move_count)
    asked = call(ask_kernel, f32(2, STEPS, WIDTH), [SMEM, SMEM, VMEM], (*plan, query_proj), out_specs=VMEM)
    asked = over_rep(asked, FAR)
    far, near = call(
        outbox_kernel, (f32(2, *row), f32(1, *row)), [SMEM, ANY], (plan_source, states), out_specs=(ANY, ANY),
        scratch_shapes=[pltpu.SemaphoreType.DMA((MOVE,))])
    near_in = over_rep(near, 1)
    far_in = over_rep(far, FAR)
    answer = call(answer_kernel, f32(2, STEPS, WIDTH), [VMEM, VMEM], (asked, far), out_specs=VMEM)
    answer = over_rep(answer, FAR)

    whole = pl.BlockSpec((SLOTS_DEV, STEPS, WIDTH), lambda i: (0, 0, 0))
    by_slot = pl.BlockSpec((1, *row), lambda i: (i, 0, 0, 0))
    part, new_states = call(
        main_kernel, (f32(SLOTS_DEV, STEPS, WIDTH), f32(SLOTS_DEV, *row)), [SMEM] * 5 + [whole] * 3 + [by_slot],
        (*flags, decay_rate, query_proj, key_proj, value_proj, states), out_specs=(whole, by_slot), grid=(SLOTS_DEV,), cost=4_000_000)
    out, square = call(
        combine_kernel, (f32(SLOTS_DEV, STEPS, WIDTH), f32(SLOTS_DEV, STEPS, DK)), [SMEM] * 3 + [VMEM] * 4,
        (*plan, decay_rate, query_proj, answer, near_in, part), out_specs=(VMEM, VMEM))
    square = square + over_head(square, 1)
    square = square + over_head(square, 2)
    other = over_head(square, 6)
    attended = call(
        final_kernel, jax.ShapeDtypeStruct((SLOTS_DEV, STEPS, WIDTH), jnp.bfloat16), [SMEM] * 4 + [VMEM] * 5,
        (*flags, norm_gain.reshape(1, WIDTH), gate_proj, out, square, other), out_specs=VMEM)
    placed = pl.BlockSpec((1, *row), lambda i, target, count: (place_of(target, count, i), 0, 0, 0))
    new_states = call(
        update_kernel, f32(SLOTS_DEV, *row), None, (*plan, decay_rate, far_in, near_in, new_states),
        cost=1_000_000, input_output_aliases={5: 0},
        grid_spec=pltpu.PrefetchScalarGridSpec(
            num_scalar_prefetch=2, grid=(MOVE,),
            in_specs=[
                SMEM,
                pl.BlockSpec((1, *row), lambda i, target, count: (jnp.minimum(i, 1), 0, 0, 0)),
                pl.BlockSpec((1, *row), lambda i, target, count: (0, 0, 0, 0)),
                placed,
            ],
            out_specs=placed))
    return attended, new_states


def solution(mesh):
    return jax.shard_map(
        local,
        mesh=mesh,
        in_specs=(
            P("rep", "head", None, None),
            P("rep"),
            P(),
            P(),
            P(),
            P("rep", None, "head"),
            P("rep", None, "head"),
            P("rep", None, "head"),
            P("rep", None, "head"),
            P("head"),
            P("head"),
        ),
        out_specs=(P("rep", None, "head"), P("rep", "head", None, None)),
        check_vma=False,
    )
```

time: 162 us -> 90.2 us (0.56)
  waiting for transfers between devices: 97.8 us -> 20.7 us
  Pallas kernels: 0 us -> 47.2 us
  blocking collectives: 16.1 us -> 0 us
  starting transfers between devices: 0.04 us -> 15 us
  between operations: 14.3 us -> 0.69 us
  matrix products: 10.2 us -> 0 us
  other arithmetic: 8.92 us -> 0.73 us
  local copies, waits for them, and re-layouts: 12.6 us -> 4.75 us
    all_gather x1 -> x0, waiting for transfers between devices: 97.8 us -> none  [local(): lax.all_gather(outbox, 'rep', axis=0, tiled=True)]
    pallas_call x0 -> x7, Pallas kernels: none -> 47.2 us  [call(): pl.pallas_call(kernel, out_shape=outs, cost_estimate=pl.CostEstimate(flop...]
    ppermute x0 -> x7, waiting for transfers between devices: none -> 20.7 us  [the longest x4 13.4 us: over_rep(): lax.ppermute(x, 'rep', [(i, (i + distance) % N_REP) for i in range(N_REP)])]
    psum x1 -> x0, blocking collectives: 16.1 us -> none  [local(): square_sum = lax.psum(jnp.sum(readout * readout, axis=1), 'head')]
    ppermute x0 -> x7, starting transfers between devices: none -> 15 us  [the longest x3 8.41 us: over_head(): return lax.ppermute(x, 'head', [(i, i ^ flip) for i in range(N_HEAD)])]
    gather x2 -> x0, local copies, waits for them, and re-layouts: 11 us -> none  [the longest x1 8.84 us: local(): jnp.take(lax.all_gather(outbox, 'rep', axis=0, tiled=True), picked, axis=0)]
    dot_general x4 -> x0, matrix products: 10.2 us -> none  [local(): jnp.einsum('bhd,bhde->bhe', queries[:, step_index], current, precision=la...]
    select_n x5 -> x0, other arithmetic: 6.12 us -> none  [the longest x1 5.07 us: local(): new_states = jnp.where(live_rows[:, None, None, None], current, 0.0)]
  transfers between devices with their start and end apart: 1 -> 7, of which waited for: 1 -> 4; matrix products, arithmetic and copies ran while one was open for 1% -> 2% of each run, Pallas kernels for 0% -> 20%
where the time goes in v1:
time: 90.2 us; the launch traced here: 89.1 us
  Pallas kernels  47.2 us (52%)
  waiting for transfers between devices  20.7 us (23%)
  starting transfers between devices  15 us (17%)
  local copies, waits for them, and re-layouts  4.75 us (5%)
    pallas_call x7, Pallas kernels, call(): pl.pallas_call(kernel, out_shape=outs, cost_estimate=pl.CostEstimate(flop...  47.2 us
    ppermute x4, waiting for transfers between devices, over_rep(): lax.ppermute(x, 'rep', [(i, (i + distance) % N_REP) for i in range(N_REP)])  13.4 us
    ppermute x3, starting transfers between devices, over_head(): return lax.ppermute(x, 'head', [(i, i ^ flip) for i in range(N_HEAD)])  8.41 us
    ppermute x3, waiting for transfers between devices, over_head(): return lax.ppermute(x, 'head', [(i, i ^ flip) for i in range(N_HEAD)])  7.38 us
    ppermute x4, starting transfers between devices, over_rep(): lax.ppermute(x, 'rep', [(i, (i + distance) % N_REP) for i in range(N_REP)])  6.62 us
    unnamed x16, local copies, waits for them, and re-layouts  4.75 us
  transfers between devices with their start and end apart: 7, of which 4 were waited for; matrix products, arithmetic and copies ran while one was open for 2% of the time, Pallas kernels for 20%

profile of v1, /device:TPU:32, one launch (start us, length us, event | category | flops | bytes accessed | tf_op | source)
XLA Modules:
  0.0 89.1 jit_solution(601282945680482880)
XLA Ops:
  0.6 0.0 copy-start.6
  0.6 1.4 %copy.19.source_ref = s32[32,3]{1,0:T(8,128)} copy(s32[32,3]{0,1:T(4,128)} %param.13) | data formatting | bytes 768 | tf_op args[2]
  2.0 25.9 %shard_map.123 = (f32[2,4,128,128]{3,2,1,0:T(8,128)}, f32[1,4,128,128]{3,2,1,0:T(8,128)}) custom-call(s32[32,3]{1,0:T(8,128)} %copy.19.source_ref, f32[8,4,128,128]{3,2,1,0:T(8,128)} %states_ref.3), custom_call_target="tpu_custom_call" | custom-call | flops 100000 | bytes 100000 | tf_op jit(solution)/shard_map/pallas_call | solution.py:168
  27.9 3.3 %collective-permute-start.6 = (f32[2,4,128,128]{3,2,1,0:T(8,128)}, f32[2,4,128,128]{3,2,1,0:T(8,128)S(1)}, u32[]{:S(2)}, u32[]{:S(2)}) collective-permute-start(f32[2,4,128,128]{3,2,1,0:T(8,128)} %get-tuple-element.8.far_ref), channel_id=1, source_target_pairs={{0,128},{8,136},{16,144},{24,152},{32,160},{40,168},{48,176},{56,1... | collective-permute-start | bytes 1572872 | tf_op jit(solution)/shard_map/ppermute | solution.py:179
  31.2 0.0 collective-permute-start.2
  31.2 0.0 copy-done.6
  31.2 0.7 copy.20.target_ref
  31.9 1.6 %shard_map.122 = f32[2,4,512]{2,1,0:T(4,128)} custom-call(s32[32,3]{1,0:T(8,128)} %copy.20.target_ref, s32[32]{0:T(128)} %count_ref.9, bf16[8,4,512]{2,1,0:T(4,128)(2,1)} %query_ref.5), custom_call_target="tpu_custom_call" | custom-call | flops 100000 | bytes 100000 | tf_op jit(solution)/shard_map/pallas_call | solution.py:168
  33.4 0.3 collective-permute-start
  33.8 13.4 %collective-permute-done.query_ref = f32[2,4,512]{2,1,0:T(4,128)S(1)} collective-permute-done((f32[2,4,512]{2,1,0:T(4,128)}, f32[2,4,512]{2,1,0:T(4,128)S(1)}, u32[]{:S(2)}, u32[]{:S(2)}) %collective-permute-start) | collective-permute-done | bytes 16416 | tf_op jit(solution)/shard_map/ppermute | solution.py:179
  47.1 0.0 copy-start.5
  47.1 0.6 copy-done.5
  47.7 2.2 %shard_map.124 = f32[2,4,512]{2,1,0:T(4,128)} custom-call(f32[2,4,512]{2,1,0:T(4,128)} %copy-done.5, f32[2,4,128,128]{3,2,1,0:T(8,128)} %get-tuple-element.8.far_ref), custom_call_target="tpu_custom_call" | custom-call | flops 100000 | bytes 100000 | tf_op jit(solution)/shard_map/pallas_call | solution.py:168
  49.9 3.0 %collective-permute-start.1 = (f32[2,4,512]{2,1,0:T(4,128)}, f32[2,4,512]{2,1,0:T(4,128)S(1)}, u32[]{:S(2)}, u32[]{:S(2)}) collective-permute-start(f32[2,4,512]{2,1,0:T(4,128)} %shard_map.124), channel_id=1, source_target_pairs={{0,128},{8,136},{16,144},{24,152},{32,160},{40,168},{48,176},{56,1... | collective-permute-start | bytes 49160 | tf_op jit(solution)/shard_map/ppermute | solution.py:179
  52.9 9.9 %shard_map.125 = (f32[8,4,512]{2,1,0:T(4,128)}, f32[8,4,128,128]{3,2,1,0:T(8,128)}) custom-call(s32[8]{0:T(128)} %alive_ref.3, s32[32,3]{1,0:T(8,128)} %copy.19.source_ref, s32[32,3]{1,0:T(8,128)} %copy.20.target_ref, s32[32]{0:T(128)} %count_ref.9, f32[4]{0:T(128)} %rate_ref.5, bf16[8,4,512]{2,1,0:T(4,128)(2,1)} %query_ref.5, bf16[8,4,512]{2,1,0:T(4,128)(2,1)} %key_ref.1, ...), custom_call_target="tpu_custom_call" | custom-call | flops 4000000 | bytes 4000000 | tf_op jit(solution)/shard_map/pallas_call | solution.py:168
  62.8 0.0 collective-permute-done.1.answer_ref
  62.8 0.0 copy-start.3
  62.8 0.0 collective-permute-done.2.near_ref
  62.9 0.0 copy-start
  62.9 0.6 copy-done.3
  63.4 0.1 copy-done
  63.6 1.8 %shard_map.126 = (f32[8,4,512]{2,1,0:T(4,128)}, f32[8,4,128]{2,1,0:T(4,128)}) custom-call(s32[32,3]{1,0:T(8,128)} %copy.20.target_ref, s32[32]{0:T(128)} %count_ref.9, f32[4]{0:T(128)} %rate_ref.5, bf16[8,4,512]{2,1,0:T(4,128)(2,1)} %query_ref.5, f32[2,4,512]{2,1,0:T(4,128)} %copy-done.3, f32[1,4,128,128]{3,2,1,0:T(8,128)} %copy-done, ...), custom_call_target="tpu_custom_call" | custom-call | flops 100000 | bytes 100000 | tf_op jit(solution)/shard_map/pallas_call | solution.py:168
  65.3 0.0 collective-permute-start.3
  65.3 3.9 %collective-permute-done.3 = f32[8,4,128]{2,1,0:T(4,128)S(1)} collective-permute-done((f32[8,4,128]{2,1,0:T(4,128)}, f32[8,4,128]{2,1,0:T(4,128)S(1)}, u32[]{:S(2)}, u32[]{:S(2)}) %collective-permute-start.3) | collective-permute-done | bytes 16416 | tf_op jit(solution)/shard_map/ppermute | solution.py:183
  69.3 0.7 add.6
  70.0 3.3 %collective-permute-start.4 = (f32[8,4,128]{2,1,0:T(4,128)S(1)}, f32[8,4,128]{2,1,0:T(4,128)S(1)}, u32[]{:S(2)}, u32[]{:S(2)}) collective-permute-start(f32[8,4,128]{2,1,0:T(4,128)S(1)} %add.6), channel_id=1, source_target_pairs={{0,2},{1,3},{2,0},{3,1},{4,6},{5,7},{6,4},{7,5},{8,10},{9,11},{10,... | collective-permute-start | bytes 49160 | tf_op jit(solution)/shard_map/ppermute | solution.py:183
  73.3 1.7 %collective-permute-done.4 = f32[8,4,128]{2,1,0:T(4,128)S(1)} collective-permute-done((f32[8,4,128]{2,1,0:T(4,128)S(1)}, f32[8,4,128]{2,1,0:T(4,128)S(1)}, u32[]{:S(2)}, u32[]{:S(2)}) %collective-permute-start.4) | collective-permute-done | bytes 16416 | tf_op jit(solution)/shard_map/ppermute | solution.py:183
  75.0 0.0 copy-start.2
  75.0 5.1 %collective-permute-start.5 = (f32[8,4,128]{2,1,0:T(4,128)S(1)}, f32[8,4,128]{2,1,0:T(4,128)S(1)}, u32[]{:S(2)}, u32[]{:S(2)}) collective-permute-start(f32[8,4,128]{2,1,0:T(4,128)S(1)} %add.7.square_a_ref), channel_id=1, source_target_pairs={{0,6},{1,7},{2,4},{3,5},{4,2},{5,3},{6,0},{7,1},{8,14},{9,15},{10,... | collective-permute-start | bytes 49160 | tf_op jit(solution)/shard_map/ppermute | solution.py:183
  80.2 1.7 %collective-permute-done.5.square_b_ref = f32[8,4,128]{2,1,0:T(4,128)S(1)} collective-permute-done((f32[8,4,128]{2,1,0:T(4,128)S(1)}, f32[8,4,128]{2,1,0:T(4,128)S(1)}, u32[]{:S(2)}, u32[]{:S(2)}) %collective-permute-start.5) | collective-permute-done | bytes 16416 | tf_op jit(solution)/shard_map/ppermute | solution.py:183
  81.9 0.0 copy-start.4
  81.9 0.0 copy-done.2
  81.9 0.6 copy-done.4
  82.5 2.1 %shard_map.127 = bf16[8,4,512]{2,1,0:T(4,128)(2,1)} custom-call(s32[8]{0:T(128)} %alive_ref.3, s32[32,3]{1,0:T(8,128)} %copy.19.source_ref, s32[32,3]{1,0:T(8,128)} %copy.20.target_ref, s32[32]{0:T(128)} %count_ref.9, f32[1,512]{1,0:T(1,128)} %bitcast.1, bf16[8,4,512]{2,1,0:T(4,128)(2,1)} %gate_ref.1, f32[8,4,512]{2,1,0:T(4,128)} %get-tuple-element.11.out_ref, ...), custom_call_target="tpu_custom_call" | custom-call | flops 100000 | bytes 100000 | tf_op jit(solution)/shard_map/pallas_call | solution.py:168
  84.6 0.0 collective-permute-done.6.far_ref
  84.6 0.0 copy-start.1
  84.6 0.8 copy-done.1
  85.4 3.7 %shard_map.128 = f32[8,4,128,128]{3,2,1,0:T(8,128)} custom-call(s32[32,3]{1,0:T(8,128)} %copy.20.target_ref, s32[32]{0:T(128)} %count_ref.9, f32[4]{0:T(128)} %rate_ref.5, f32[2,4,128,128]{3,2,1,0:T(8,128)} %copy-done.1, f32[1,4,128,128]{3,2,1,0:T(8,128)} %copy-done, f32[8,4,128,128]{3,2,1,0:T(8,128)} %get-tuple-element.13.old_ref), custom_call_target="tpu_custom_call", output_to_operand_aliasing={{}: (5, {})} | custom-call | flops 1000000 | bytes 1000000 | tf_op jit(solution)/shard_map/pallas_call | solution.py:168
  (1 shorter events, 0.0 us)
Async XLA Ops:
  0.6 30.6 %copy-start.6 = (s32[32,3]{0,1:T(4,128)S(1)}, s32[32,3]{0,1:T(4,128)}, u32[]{:S(2)}) copy-start(s32[32,3]{0,1:T(4,128)} %param.14) | copy-start | bytes 1156
  27.9 56.7 %collective-permute-start.6 = (f32[2,4,128,128]{3,2,1,0:T(8,128)}, f32[2,4,128,128]{3,2,1,0:T(8,128)S(1)}, u32[]{:S(2)}, u32[]{:S(2)}) collective-permute-start(f32[2,4,128,128]{3,2,1,0:T(8,128)} %get-tuple-element.8.far_ref), channel_id=1, source_target_pairs={{0,128},{8,136},{16,144},{24,152},{32,160},{40,168},{48,176},{56,1... | collective-permute-start | bytes 1572872 | tf_op jit(solution)/shard_map/ppermute | solution.py:179
  31.2 31.7 %collective-permute-start.2 = (f32[1,4,128,128]{3,2,1,0:T(8,128)}, f32[1,4,128,128]{3,2,1,0:T(8,128)S(1)}, u32[]{:S(2)}, u32[]{:S(2)}) collective-permute-start(f32[1,4,128,128]{3,2,1,0:T(8,128)} %get-tuple-element.9), channel_id=1, source_target_pairs={{0,8},{8,16},{16,24},{24,32},{32,40},{40,48},{48,56},{56,64},{64,7... | collective-permute-start | bytes 786440 | tf_op jit(solution)/shard_map/ppermute | solution.py:179
  33.4 13.7 %collective-permute-start = (f32[2,4,512]{2,1,0:T(4,128)}, f32[2,4,512]{2,1,0:T(4,128)S(1)}, u32[]{:S(2)}, u32[]{:S(2)}) collective-permute-start(f32[2,4,512]{2,1,0:T(4,128)} %shard_map.122), channel_id=1, source_target_pairs={{0,128},{8,136},{16,144},{24,152},{32,160},{40,168},{48,176},{56,1... | collective-permute-start | bytes 49160 | tf_op jit(solution)/shard_map/ppermute | solution.py:179
  47.1 0.6 copy-start.5
  49.9 12.9 %collective-permute-start.1 = (f32[2,4,512]{2,1,0:T(4,128)}, f32[2,4,512]{2,1,0:T(4,128)S(1)}, u32[]{:S(2)}, u32[]{:S(2)}) collective-permute-start(f32[2,4,512]{2,1,0:T(4,128)} %shard_map.124), channel_id=1, source_target_pairs={{0,128},{8,136},{16,144},{24,152},{32,160},{40,168},{48,176},{56,1... | collective-permute-start | bytes 49160 | tf_op jit(solution)/shard_map/ppermute | solution.py:179
  62.8 0.6 copy-start.3
  62.9 0.7 copy-start
  65.3 3.9 %collective-permute-start.3 = (f32[8,4,128]{2,1,0:T(4,128)}, f32[8,4,128]{2,1,0:T(4,128)S(1)}, u32[]{:S(2)}, u32[]{:S(2)}) collective-permute-start(f32[8,4,128]{2,1,0:T(4,128)} %get-tuple-element.12), channel_id=1, source_target_pairs={{0,1},{1,0},{2,3},{3,2},{4,5},{5,4},{6,7},{7,6},{8,9},{9,8},{10,11... | collective-permute-start | bytes 49160 | tf_op jit(solution)/shard_map/ppermute | solution.py:183
  70.0 5.0 %collective-permute-start.4 = (f32[8,4,128]{2,1,0:T(4,128)S(1)}, f32[8,4,128]{2,1,0:T(4,128)S(1)}, u32[]{:S(2)}, u32[]{:S(2)}) collective-permute-start(f32[8,4,128]{2,1,0:T(4,128)S(1)} %add.6), channel_id=1, source_target_pairs={{0,2},{1,3},{2,0},{3,1},{4,6},{5,7},{6,4},{7,5},{8,10},{9,11},{10,... | collective-permute-start | bytes 49160 | tf_op jit(solution)/shard_map/ppermute | solution.py:183
  75.0 6.9 %copy-start.2 = (f32[8,4,128]{2,1,0:T(4,128)}, f32[8,4,128]{2,1,0:T(4,128)S(1)}, u32[]{:S(2)}) copy-start(f32[8,4,128]{2,1,0:T(4,128)S(1)} %add.7.square_a_ref) | copy-start | bytes 49156
  75.0 6.9 %collective-permute-start.5 = (f32[8,4,128]{2,1,0:T(4,128)S(1)}, f32[8,4,128]{2,1,0:T(4,128)S(1)}, u32[]{:S(2)}, u32[]{:S(2)}) collective-permute-start(f32[8,4,128]{2,1,0:T(4,128)S(1)} %add.7.square_a_ref), channel_id=1, source_target_pairs={{0,6},{1,7},{2,4},{3,5},{4,2},{5,3},{6,0},{7,1},{8,14},{9,15},{10,... | collective-permute-start | bytes 49160 | tf_op jit(solution)/shard_map/ppermute | solution.py:183
  81.9 0.6 copy-start.4
  84.6 0.8 copy-start.1

commit v2 on v1

v2 whole, which is shorter than its diff:
```python
import jax
import jax.numpy as jnp
from jax import lax
from jax.experimental import pallas as pl
from jax.experimental.pallas import tpu as pltpu
from jax.sharding import PartitionSpec as P

SLOTS_DEV = 8
MOVE = 3
STEPS = 4
N_REP = 32
N_HEAD = 8
HEADS = 32
DK = 128
HEADS_DEV = HEADS // N_HEAD
WIDTH = HEADS_DEV * DK
FAR = N_REP // 2
BLOCK = 2
epsilon = 1e-06

HIGHEST = lax.Precision.HIGHEST
VMEM = pl.BlockSpec(memory_space=pltpu.VMEM)
SMEM = pl.BlockSpec(memory_space=pltpu.SMEM)
ANY = pl.BlockSpec(memory_space=pl.ANY)


def silu(x):
    x = x.astype(jnp.float32)
    return x / (1.0 + jnp.exp(-x))


def sender_of(move):
    me = lax.axis_index("rep")
    return lax.rem(me + (FAR if move < 2 else N_REP - 1), N_REP)


def comes_to(move, target_ref, count_ref):
    sender = sender_of(move)
    return count_ref[sender] > move, lax.rem(target_ref[move, sender], SLOTS_DEV)


def slot_flags(slot, alive_ref, source_ref, target_ref, count_ref):
    me = lax.axis_index("rep")
    leaves = False
    arrives = []
    for move in range(MOVE):
        leaves |= (count_ref[me] > move) & (source_ref[move, me] == slot)
        valid, at = comes_to(move, target_ref, count_ref)
        arrives.append(valid & (at == slot))
    return (alive_ref[slot] == 1) & jnp.logical_not(leaves), arrives


def split(x):
    high = x.astype(jnp.bfloat16)
    return high, (x - high.astype(jnp.float32)).astype(jnp.bfloat16)


def dot(a, b, dims):
    return lax.dot_general(a, b, (dims, ((), ())), preferred_element_type=jnp.float32)


def read_out(query, state):
    rows = jnp.concatenate(split(query), axis=0)
    high, low = split(state)
    by_high = dot(rows, high, ((1,), (0,)))
    by_low = dot(rows, low, ((1,), (0,)))
    return by_high[:STEPS] + by_high[STEPS:] + by_low[:STEPS]


def later_by(x, gap):
    return x if gap == 0 else jnp.concatenate([jnp.zeros((gap, x.shape[1]), x.dtype), x[:-gap]], axis=0)


def head_slice(head):
    return slice(head * DK, (head + 1) * DK)


def ask_kernel(target_ref, count_ref, query_ref, out_ref):
    for move in range(2):
        _, slot = comes_to(move, target_ref, count_ref)
        out_ref[move] = silu(query_ref[slot])


def outbox_kernel(source_ref, states_ref, asked_ref, far_ref, near_ref, sems):
    del asked_ref
    me = lax.axis_index("rep")
    copies = []
    for move in range(MOVE):
        out = far_ref.at[move] if move < 2 else near_ref.at[0]
        copies.append(pltpu.make_async_copy(states_ref.at[source_ref[move, me]], out, sems.at[move]))
    for copy in copies:
        copy.start()
    for copy in copies:
        copy.wait()


def answer_kernel(query_ref, far_ref, out_ref):
    for move in range(2):
        for head in range(HEADS_DEV):
            out_ref[move, :, head_slice(head)] = read_out(query_ref[move, :, head_slice(head)], far_ref[move, head])


def main_kernel(
    alive_ref, source_ref, target_ref, count_ref, rate_ref, query_ref, key_ref, value_ref, states_ref,
    out_ref, new_ref, flag_ref, fade_ref, added_ref, near_query_ref,
):
    step = pl.program_id(0)
    times = lax.broadcasted_iota(jnp.int32, (STEPS, DK), 0).astype(jnp.float32)

    @pl.when(step == 0)
    def _():
        for head in range(HEADS_DEV):
            fade_ref[:, head_slice(head)] = jnp.exp(-rate_ref[head] * (times + 1.0))
        _, slot = comes_to(2, target_ref, count_ref)
        near_query_ref[...] = silu(query_ref[slot])

    for place in range(BLOCK):
        slot = step * BLOCK + place
        stays, arrives = slot_flags(slot, alive_ref, source_ref, target_ref, count_ref)
        live = (stays | arrives[0] | arrives[1] | arrives[2]).astype(jnp.float32)
        for move in range(MOVE):
            flag_ref[move, slot] = jnp.full((STEPS, DK), arrives[move].astype(jnp.float32))
        flag_ref[MOVE, slot] = jnp.full((STEPS, DK), live)
        stays = stays.astype(jnp.float32)
        queries, keys, values = silu(query_ref[slot]), silu(key_ref[slot]), silu(value_ref[slot])
        inside = [jnp.zeros((STEPS, DK), jnp.float32)] * HEADS_DEV
        for gap in range(STEPS):
            older_keys, older_values = later_by(keys, gap), later_by(values, gap)
            for head in range(HEADS_DEV):
                at = head_slice(head)
                inner = jnp.sum(queries[:, at] * older_keys[:, at], axis=1, keepdims=True)
                inside[head] += inner * (older_values[:, at] * jnp.exp(-rate_ref[head] * jnp.full((STEPS, DK), float(gap))))
        for head in range(HEADS_DEV):
            rate = rate_ref[head]
            query, key, value = (x[:, head_slice(head)] for x in (queries, keys, values))
            state = states_ref[place, head]
            out_ref[slot, :, head_slice(head)] = inside[head] + read_out(query, state) * (stays * jnp.exp(-rate * (times + 1.0)))
            value_high, value_low = split(value)
            faded_high, faded_low = split(key * jnp.exp(-rate * (STEPS - 1.0 - times)))
            added = dot(
                jnp.concatenate([faded_high, faded_low, faded_high], axis=0),
                jnp.concatenate([value_high, value_high, value_low], axis=0), ((0,), (0,)))
            fade = jnp.exp(jnp.full((8, DK), -STEPS * rate, jnp.float32))[:1]
            new_ref[place, head] = state * (fade * stays) + added * live
        for move in range(MOVE):
            @pl.when(arrives[move])
            def _(move=move, place=place):
                added_ref[move] = new_ref[place]


def combine_kernel(answer_ref, near_ref, near_query_ref, part_ref, flag_ref, fade_ref, far_in_ref, out_ref, square_ref, far_ref):
    del far_in_ref, far_ref
    moved = [answer_ref[0], answer_ref[1], jnp.concatenate(
        [read_out(near_query_ref[:, head_slice(head)], near_ref[0, head]) for head in range(HEADS_DEV)], axis=1)]
    moved = [x * fade_ref[...] for x in moved]
    for slot in range(SLOTS_DEV):
        total = jnp.zeros((STEPS, DK), jnp.float32)
        for head in range(HEADS_DEV):
            at = head_slice(head)
            row = part_ref[slot, :, at]
            for move in range(MOVE):
                row = jnp.where(flag_ref[move, slot] > 0.0, row + moved[move][:, at], row)
            out_ref[slot, :, at] = row
            total += row * row
        square_ref[slot] = total


def final_kernel(
    target_ref, count_ref, gain_ref, gate_ref, out_ref, square_a_ref, square_b_ref, flag_ref, fade_ref, added_ref, far_ref, near_ref, old_ref,
    attended_ref, new_ref, rows_ref, sems,
):
    del old_ref
    copies = []
    for move in range(MOVE):
        valid, slot = comes_to(move, target_ref, count_ref)
        copies.append((valid, pltpu.make_async_copy(rows_ref.at[move], new_ref.at[slot], sems.at[move])))
        for head in range(HEADS_DEV):
            came = far_ref[move, head] if move < 2 else near_ref[0, head]
            rows_ref[move, head] = came * fade_ref[STEPS - 1:, head_slice(head)] + added_ref[move, head]

        @pl.when(valid)
        def _(copy=copies[-1][1]):
            copy.start()

    for slot in range(SLOTS_DEV):
        total = jnp.sum(square_a_ref[slot] + square_b_ref[slot], axis=1, keepdims=True)
        scale = lax.rsqrt(total * (1.0 / (HEADS * DK)) + epsilon) * flag_ref[MOVE, slot]
        gate = gate_ref[slot].astype(jnp.float32)
        row = out_ref[slot] * gain_ref[...] / (1.0 + jnp.exp(-gate))
        attended_ref[slot] = (row * jnp.concatenate([scale] * HEADS_DEV, axis=1)).astype(jnp.bfloat16)
    for valid, copy in copies:
        @pl.when(valid)
        def _(copy=copy):
            copy.wait()


def call(kernel, outs, in_specs, args, cost=100_000, limit=8, **more):
    return pl.pallas_call(
        kernel, out_shape=outs, in_specs=in_specs,
        compiler_params=pltpu.CompilerParams(vmem_limit_bytes=limit * 1024 * 1024),
        cost_estimate=pl.CostEstimate(flops=cost, bytes_accessed=cost, transcendentals=0), **more,
    )(*args)


def f32(*shape):
    return jax.ShapeDtypeStruct(shape, jnp.float32)


def over_rep(x, distance):
    return lax.ppermute(x, "rep", [(i, (i + distance) % N_REP) for i in range(N_REP)])


def over_head(x, flip):
    return lax.ppermute(x, "head", [(i, i ^ flip) for i in range(N_HEAD)])


def whole(*shape):
    return pl.BlockSpec(shape, lambda i: (0,) * len(shape))


def by_slot(*row):
    return pl.BlockSpec((BLOCK, *row), lambda i: (i, 0, 0, 0))


def run_main(*args):
    row = (HEADS_DEV, DK, DK)
    features = (SLOTS_DEV, STEPS, WIDTH)
    return call(
        main_kernel,
        (f32(*features), f32(SLOTS_DEV, *row), f32(MOVE + 1, SLOTS_DEV, STEPS, DK), f32(STEPS, WIDTH), f32(MOVE, *row), f32(STEPS, WIDTH)),
        [SMEM] * 5 + [whole(*features)] * 3 + [by_slot(*row)], args,
        out_specs=(
            whole(*features), by_slot(*row), whole(MOVE + 1, SLOTS_DEV, STEPS, DK), whole(STEPS, WIDTH), whole(MOVE, *row), whole(STEPS, WIDTH)),
        grid=(SLOTS_DEV // BLOCK,), cost=40_000_000)


def local(states, alive_flag, plan_source, plan_target, move_count, query_proj, key_proj, value_proj, gate_proj, decay_rate, norm_gain):
    row = (HEADS_DEV, DK, DK)
    features = (SLOTS_DEV, STEPS, WIDTH)
    source, target = plan_source.T, plan_target.T
    asked = call(ask_kernel, f32(2, STEPS, WIDTH), [SMEM, SMEM, VMEM], (target, move_count, query_proj), out_specs=VMEM, limit=60)
    far, near = call(
        outbox_kernel, (f32(2, *row), f32(1, *row)), [SMEM, ANY, ANY], (source, states, asked), out_specs=(VMEM, VMEM),
        scratch_shapes=[pltpu.SemaphoreType.DMA((MOVE,))])
    asked = over_rep(asked, FAR)
    near = over_rep(near, 1)
    answer = call(answer_kernel, f32(2, STEPS, WIDTH), [VMEM, VMEM], (asked, far), out_specs=VMEM)
    part, new_states, flags, fade, added, near_query = run_main(
        alive_flag, source, target, move_count, decay_rate, query_proj, key_proj, value_proj, states)
    answer = over_rep(answer, FAR)
    out, square, far = call(
        combine_kernel, (f32(*features), f32(SLOTS_DEV, STEPS, DK), f32(2, *row)), [VMEM] * 6 + [ANY],
        (answer, near, near_query, part, flags, fade, far), out_specs=(VMEM, VMEM, ANY), input_output_aliases={6: 2})
    far = over_rep(far, FAR)
    square = square + over_head(square, 1)
    square = square + over_head(square, 2)
    other = over_head(square, 6)
    return call(
        final_kernel, (jax.ShapeDtypeStruct(features, jnp.bfloat16), f32(SLOTS_DEV, *row)), [SMEM] * 2 + [VMEM] * 10 + [ANY],
        (target, move_count, norm_gain.reshape(1, WIDTH), gate_proj, out, square, other, flags, fade, added, far, near, new_states),
        out_specs=(VMEM, ANY), input_output_aliases={12: 1},
        scratch_shapes=[pltpu.VMEM((MOVE, *row), jnp.float32), pltpu.SemaphoreType.DMA((MOVE,))])


def solution(mesh):
    return jax.shard_map(
        local,
        mesh=mesh,
        in_specs=(
            P("rep", "head", None, None),
            P("rep"),
            P(),
            P(),
            P(),
            P("rep", None, "head"),
            P("rep", None, "head"),
            P("rep", None, "head"),
            P("rep", None, "head"),
            P("head"),
            P("head"),
        ),
        out_specs=(P("rep", None, "head"), P("rep", "head", None, None)),
        check_vma=False,
    )
```

time: 90.2 us -> 41.1 us (0.46)
  Pallas kernels: 47.2 us -> 8.76 us
  waiting for transfers between devices: 20.7 us -> 9.12 us
  starting transfers between devices: 15 us -> 19.1 us
  local copies, waits for them, and re-layouts: 4.75 us -> 3.04 us
    pallas_call x7 -> x6, Pallas kernels: 47.2 us -> 8.76 us  [call(): pl.pallas_call(kernel, out_shape=outs, in_specs=in_specs, compiler_params...]
    ppermute x4, waiting for transfers between devices: 13.4 us -> 2.06 us  [over_rep(): lax.ppermute(x, 'rep', [(i, (i + distance) % N_REP) for i in range(N_REP)])]
    ppermute x4, starting transfers between devices: 6.62 us -> 10.7 us  [over_rep(): lax.ppermute(x, 'rep', [(i, (i + distance) % N_REP) for i in range(N_REP)])]
    unnamed x16 -> x28, local copies, waits for them, and re-layouts: 4.75 us -> 3.04 us
  transfers between devices with their start and end apart: 7 -> 7, of which waited for: 4 -> 4; matrix products, arithmetic and copies ran while one was open for 2% -> 0% of each run, Pallas kernels for 20% -> 11%
where the time goes in v2:
time: 41.1 us; the launch traced here: 40.8 us
  starting transfers between devices  19.1 us (46%)
  waiting for transfers between devices  9.12 us (22%)
  Pallas kernels  8.76 us (21%)
  local copies, waits for them, and re-layouts  3.04 us (7%)
  between operations  0.78 us (2%)
    ppermute x4, starting transfers between devices, over_rep(): lax.ppermute(x, 'rep', [(i, (i + distance) % N_REP) for i in range(N_REP)])  10.7 us
    pallas_call x6, Pallas kernels, call(): pl.pallas_call(kernel, out_shape=outs, in_specs=in_specs, compiler_params...  8.76 us
    ppermute x3, starting transfers between devices, over_head(): return lax.ppermute(x, 'head', [(i, i ^ flip) for i in range(N_HEAD)])  8.43 us
    ppermute x3, waiting for transfers between devices, over_head(): return lax.ppermute(x, 'head', [(i, i ^ flip) for i in range(N_HEAD)])  7.06 us
    unnamed x28, local copies, waits for them, and re-layouts  3.04 us
    ppermute x4, waiting for transfers between devices, over_rep(): lax.ppermute(x, 'rep', [(i, (i + distance) % N_REP) for i in range(N_REP)])  2.06 us
  transfers between devices with their start and end apart: 7, of which 4 were waited for; matrix products, arithmetic and copies ran while one was open for 0% of the time, Pallas kernels for 11%

profile of v2, /device:TPU:32, one launch (start us, length us, event | category | flops | bytes accessed | tf_op | source)
XLA Modules:
  0.0 40.8 jit_solution(15989017249326801770)
XLA Ops:
  0.6 0.0 copy-start.10
  0.6 0.0 copy-start.2
  0.7 0.0 copy-start.7
  0.7 0.0 copy-start.9
  0.7 0.0 copy-start.13
  0.7 0.0 copy-start.12
  0.7 1.5 %shard_map.122.asked_ref = f32[2,4,512]{2,1,0:T(4,128)} custom-call(s32[3,32]{1,0:T(4,128)} %bitcast.3, s32[32]{0:T(128)} %count_ref.5, bf16[8,4,512]{2,1,0:T(4,128)(2,1)} %query_ref.3), custom_call_target="tpu_custom_call" | custom-call | flops 100000 | bytes 100000 | tf_op jit(solution)/shard_map/pallas_call | solution.py:198
  2.2 0.0 copy-start
  2.2 1.6 %copy-done = f32[8,4,128,128]{3,2,1,0:T(8,128)S(1)} copy-done((f32[8,4,128,128]{3,2,1,0:T(8,128)S(1)}, f32[8,4,128,128]{3,2,1,0:T(8,128)}, u32[]{:S(2)}) %copy-start) | copy-done | bytes 2097176
  3.8 0.0 copy-start.3
  3.8 0.7 %copy-done.3 = f32[2,4,512]{2,1,0:T(4,128)S(1)} copy-done((f32[2,4,512]{2,1,0:T(4,128)S(1)}, f32[2,4,512]{2,1,0:T(4,128)}, u32[]{:S(2)}) %copy-start.3) | copy-done | bytes 16408
  4.5 0.0 copy-start.8
  4.5 0.7 %copy-done.8 = s32[32,3]{0,1:T(4,128)S(1)} copy-done((s32[32,3]{0,1:T(4,128)S(1)}, s32[32,3]{0,1:T(4,128)}, u32[]{:S(2)}) %copy-start.8) | copy-done | bytes 408
  5.2 0.0 copy-start.1
  5.2 0.0 copy-start.4
  5.2 0.0 copy-start.5
  5.2 0.7 %shard_map.123 = (f32[2,4,128,128]{3,2,1,0:T(8,128)S(1)}, f32[1,4,128,128]{3,2,1,0:T(8,128)S(1)}) custom-call(s32[3,32]{1,0:T(4,128)S(1)} %bitcast.6, f32[8,4,128,128]{3,2,1,0:T(8,128)S(1)} %copy-done, f32[2,4,512]{2,1,0:T(4,128)S(1)} %copy-done.3), custom_call_target="tpu_custom_call" | custom-call | flops 100000 | bytes 100000 | tf_op jit(solution)/shard_map/pallas_call | solution.py:198
  5.8 0.0 copy-start.6
  5.9 0.0 copy-start.11
  5.9 0.1 collective-permute-start.2
  6.0 3.3 %collective-permute-start = (f32[2,4,512]{2,1,0:T(4,128)S(1)}, f32[2,4,512]{2,1,0:T(4,128)S(1)}, u32[]{:S(2)}, u32[]{:S(2)}) collective-permute-start(f32[2,4,512]{2,1,0:T(4,128)S(1)} %copy-done.3), channel_id=1, source_target_pairs={{0,128},{8,136},{16,144},{24,152},{32,160},{40,168},{48,176},{56,1... | collective-permute-start | bytes 49160 | tf_op jit(solution)/shard_map/ppermute | solution.py:210
  9.2 2.0 %collective-permute-done.query_ref = f32[2,4,512]{2,1,0:T(4,128)S(1)} collective-permute-done((f32[2,4,512]{2,1,0:T(4,128)S(1)}, f32[2,4,512]{2,1,0:T(4,128)S(1)}, u32[]{:S(2)}, u32[]{:S(2)}) %collective-permute-start) | collective-permute-done | bytes 16416 | tf_op jit(solution)/shard_map/ppermute | solution.py:210
  11.3 0.2 shard_map.124
  11.5 6.1 %collective-permute-start.1 = (f32[2,4,512]{2,1,0:T(4,128)S(1)}, f32[2,4,512]{2,1,0:T(4,128)S(1)}, u32[]{:S(2)}, u32[]{:S(2)}) collective-permute-start(f32[2,4,512]{2,1,0:T(4,128)S(1)} %shard_map.124), channel_id=1, source_target_pairs={{0,128},{8,136},{16,144},{24,152},{32,160},{40,168},{48,176},{56,1... | collective-permute-start | bytes 49160 | tf_op jit(solution)/shard_map/ppermute | solution.py:210
  17.7 0.0 copy-done.10
  17.7 0.0 copy-done.2
  17.7 0.0 copy-done.7
  17.7 0.0 copy-done.9
  17.7 0.0 copy-done.13
  17.7 0.0 copy-done.12
  17.7 0.0 copy-done.1
  17.7 0.0 copy-done.4
  17.7 0.0 copy-done.5
  17.7 4.1 %shard_map.125 = (f32[8,4,512]{2,1,0:T(4,128)S(1)}, f32[8,4,128,128]{3,2,1,0:T(8,128)}, f32[4,8,4,128]{3,2,1,0:T(4,128)S(1)}, f32[4,512]{1,0:T(4,128)S(1)}, f32[...) custom-call(s32[8]{0:T(128)S(1)} %copy-done.12, s32[3,32]{1,0:T(4,128)S(1)} %bitcast.7, s32[3,32]{1,0:T(4,128)S(1)} %bitcast.4, ...), custom_call_target="tpu_custom_call" | custom-call | flops 40000000 | bytes 40000000 | tf_op jit(solution)/shard_map/pallas_call | solution.py:198
  21.8 0.0 collective-permute-done.1.answer_ref
  21.8 0.0 collective-permute-done.2.near_ref
  21.8 0.2 shard_map.126
  22.0 1.2 %collective-permute-start.6 = (f32[2,4,128,128]{3,2,1,0:T(8,128)S(1)}, f32[2,4,128,128]{3,2,1,0:T(8,128)S(1)}, u32[]{:S(2)}, u32[]{:S(2)}) collective-permute-start(f32[2,4,128,128]{3,2,1,0:T(8,128)S(1)} %get-tuple-element.22), channel_id=1, source_target_pairs={{0,128},{8,136},{16,144},{24,152},{32,160},{40,168},{48,176},{56,1... | collective-permute-start | bytes 1572872 | tf_op jit(solution)/shard_map/ppermute | solution.py:210
  23.2 0.1 collective-permute-start.3
  23.3 3.6 %collective-permute-done.3 = f32[8,4,128]{2,1,0:T(4,128)S(1)} collective-permute-done((f32[8,4,128]{2,1,0:T(4,128)S(1)}, f32[8,4,128]{2,1,0:T(4,128)S(1)}, u32[]{:S(2)}, u32[]{:S(2)}) %collective-permute-start.3) | collective-permute-done | bytes 16416 | tf_op jit(solution)/shard_map/ppermute | solution.py:214
  26.9 3.3 %collective-permute-start.4 = (f32[8,4,128]{2,1,0:T(4,128)S(1)}, f32[8,4,128]{2,1,0:T(4,128)S(1)}, u32[]{:S(2)}, u32[]{:S(2)}) collective-permute-start(f32[8,4,128]{2,1,0:T(4,128)S(1)} %add.6), channel_id=1, source_target_pairs={{0,2},{1,3},{2,0},{3,1},{4,6},{5,7},{6,4},{7,5},{8,10},{9,11},{10,... | collective-permute-start | bytes 49160 | tf_op jit(solution)/shard_map/ppermute | solution.py:214
  30.2 1.7 %collective-permute-done.4 = f32[8,4,128]{2,1,0:T(4,128)S(1)} collective-permute-done((f32[8,4,128]{2,1,0:T(4,128)S(1)}, f32[8,4,128]{2,1,0:T(4,128)S(1)}, u32[]{:S(2)}, u32[]{:S(2)}) %collective-permute-start.4) | collective-permute-done | bytes 16416 | tf_op jit(solution)/shard_map/ppermute | solution.py:214
  31.9 5.1 %collective-permute-start.5 = (f32[8,4,128]{2,1,0:T(4,128)S(1)}, f32[8,4,128]{2,1,0:T(4,128)S(1)}, u32[]{:S(2)}, u32[]{:S(2)}) collective-permute-start(f32[8,4,128]{2,1,0:T(4,128)S(1)} %add.7.square_a_ref), channel_id=1, source_target_pairs={{0,6},{1,7},{2,4},{3,5},{4,2},{5,3},{6,0},{7,1},{8,14},{9,15},{10,... | collective-permute-start | bytes 49160 | tf_op jit(solution)/shard_map/ppermute | solution.py:214
  37.0 1.7 %collective-permute-done.5.square_b_ref = f32[8,4,128]{2,1,0:T(4,128)S(1)} collective-permute-done((f32[8,4,128]{2,1,0:T(4,128)S(1)}, f32[8,4,128]{2,1,0:T(4,128)S(1)}, u32[]{:S(2)}, u32[]{:S(2)}) %collective-permute-start.5) | collective-permute-done | bytes 16416 | tf_op jit(solution)/shard_map/ppermute | solution.py:214
  38.7 0.0 collective-permute-done.6.far_ref
  38.7 0.0 copy-done.6
  38.7 0.0 copy-done.11
  38.7 2.1 %shard_map.127 = (bf16[8,4,512]{2,1,0:T(4,128)(2,1)}, f32[8,4,128,128]{3,2,1,0:T(8,128)}) custom-call(s32[3,32]{1,0:T(4,128)S(1)} %bitcast.5, s32[32]{0:T(128)S(1)} %copy-done.10, f32[1,512]{1,0:T(1,128)S(1)} %bitcast.8, bf16[8,4,512]{2,1,0:T(4,128)(2,1)S(1)} %copy-done.6, ...), custom_call_target="tpu_custom_call", output_to_operand_aliasing={{1}: (12, {})} | custom-call | flops 100000 | bytes 100000 | tf_op jit(solution)/shard_map/pallas_call | solution.py:198
  (2 shorter events, 0.0 us)
Async XLA Ops:
  0.6 17.0 %copy-start.10 = (s32[32]{0:T(128)S(1)}, s32[32]{0:T(128)}, u32[]{:S(2)}) copy-start(s32[32]{0:T(128)} %count_ref.5) | copy-start | bytes 388
  0.6 17.0 %copy-start.2 = (bf16[8,4,512]{2,1,0:T(4,128)(2,1)S(1)}, bf16[8,4,512]{2,1,0:T(4,128)(2,1)}, u32[]{:S(2)}) copy-start(bf16[8,4,512]{2,1,0:T(4,128)(2,1)} %query_ref.3) | copy-start | bytes 98308
  0.7 17.0 %copy-start.7 = (s32[32,3]{0,1:T(4,128)S(1)}, s32[32,3]{0,1:T(4,128)}, u32[]{:S(2)}) copy-start(s32[32,3]{0,1:T(4,128)} %param.14) | copy-start | bytes 1156
  0.7 17.0 %copy-start.9 = (s32[32,3]{0,1:T(4,128)S(1)}, s32[32,3]{0,1:T(4,128)}, u32[]{:S(2)}) copy-start(s32[32,3]{0,1:T(4,128)} %param.13) | copy-start | bytes 1156
  0.7 17.0 %copy-start.13 = (f32[4]{0:T(128)S(1)}, f32[4]{0:T(128)}, u32[]{:S(2)}) copy-start(f32[4]{0:T(128)} %rate_ref.1) | copy-start | bytes 52
  0.7 17.0 %copy-start.12 = (s32[8]{0:T(128)S(1)}, s32[8]{0:T(128)}, u32[]{:S(2)}) copy-start(s32[8]{0:T(128)} %alive_ref.1) | copy-start | bytes 100
  2.2 1.6 %copy-start = (f32[8,4,128,128]{3,2,1,0:T(8,128)S(1)}, f32[8,4,128,128]{3,2,1,0:T(8,128)}, u32[]{:S(2)}) copy-start(f32[8,4,128,128]{3,2,1,0:T(8,128)} %states_ref.3) | copy-start | bytes 6291460
  3.8 0.7 %copy-start.3 = (f32[2,4,512]{2,1,0:T(4,128)S(1)}, f32[2,4,512]{2,1,0:T(4,128)}, u32[]{:S(2)}) copy-start(f32[2,4,512]{2,1,0:T(4,128)} %shard_map.122.asked_ref) | copy-start | bytes 49156
  4.5 0.7 %copy-start.8 = (s32[32,3]{0,1:T(4,128)S(1)}, s32[32,3]{0,1:T(4,128)}, u32[]{:S(2)}) copy-start(s32[32,3]{0,1:T(4,128)} %param.13) | copy-start | bytes 1156
  5.2 12.5 %copy-start.1 = (f32[8,4,128,128]{3,2,1,0:T(8,128)S(1)}, f32[8,4,128,128]{3,2,1,0:T(8,128)}, u32[]{:S(2)}) copy-start(f32[8,4,128,128]{3,2,1,0:T(8,128)} %states_ref.3) | copy-start | bytes 6291460
  5.2 12.5 %copy-start.4 = (bf16[8,4,512]{2,1,0:T(4,128)(2,1)S(1)}, bf16[8,4,512]{2,1,0:T(4,128)(2,1)}, u32[]{:S(2)}) copy-start(bf16[8,4,512]{2,1,0:T(4,128)(2,1)} %key_ref.1) | copy-start | bytes 98308
  5.2 12.6 %copy-start.5 = (bf16[8,4,512]{2,1,0:T(4,128)(2,1)S(1)}, bf16[8,4,512]{2,1,0:T(4,128)(2,1)}, u32[]{:S(2)}) copy-start(bf16[8,4,512]{2,1,0:T(4,128)(2,1)} %value_ref.1) | copy-start | bytes 98308
  5.8 32.9 %copy-start.6 = (bf16[8,4,512]{2,1,0:T(4,128)(2,1)S(1)}, bf16[8,4,512]{2,1,0:T(4,128)(2,1)}, u32[]{:S(2)}) copy-start(bf16[8,4,512]{2,1,0:T(4,128)(2,1)} %gate_ref.1) | copy-start | bytes 98308
  5.9 32.9 %copy-start.11 = (f32[512]{0:T(512)S(1)}, f32[512]{0:T(512)}, u32[]{:S(2)}) copy-start(f32[512]{0:T(512)} %param.21) | copy-start | bytes 6148
  5.9 15.9 %collective-permute-start.2 = (f32[1,4,128,128]{3,2,1,0:T(8,128)S(1)}, f32[1,4,128,128]{3,2,1,0:T(8,128)S(1)}, u32[]{:S(2)}, u32[]{:S(2)}) collective-permute-start(f32[1,4,128,128]{3,2,1,0:T(8,128)S(1)} %get-tuple-element.14), channel_id=1, source_target_pairs={{0,8},{8,16},{16,24},{24,32},{32,40},{40,48},{48,56},{56,64},{64,7... | collective-permute-start | bytes 786440 | tf_op jit(solution)/shard_map/ppermute | solution.py:210
  6.0 5.3 %collective-permute-start = (f32[2,4,512]{2,1,0:T(4,128)S(1)}, f32[2,4,512]{2,1,0:T(4,128)S(1)}, u32[]{:S(2)}, u32[]{:S(2)}) collective-permute-start(f32[2,4,512]{2,1,0:T(4,128)S(1)} %copy-done.3), channel_id=1, source_target_pairs={{0,128},{8,136},{16,144},{24,152},{32,160},{40,168},{48,176},{56,1... | collective-permute-start | bytes 49160 | tf_op jit(solution)/shard_map/ppermute | solution.py:210
  11.5 10.3 %collective-permute-start.1 = (f32[2,4,512]{2,1,0:T(4,128)S(1)}, f32[2,4,512]{2,1,0:T(4,128)S(1)}, u32[]{:S(2)}, u32[]{:S(2)}) collective-permute-start(f32[2,4,512]{2,1,0:T(4,128)S(1)} %shard_map.124), channel_id=1, source_target_pairs={{0,128},{8,136},{16,144},{24,152},{32,160},{40,168},{48,176},{56,1... | collective-permute-start | bytes 49160 | tf_op jit(solution)/shard_map/ppermute | solution.py:210
  22.0 16.7 %collective-permute-start.6 = (f32[2,4,128,128]{3,2,1,0:T(8,128)S(1)}, f32[2,4,128,128]{3,2,1,0:T(8,128)S(1)}, u32[]{:S(2)}, u32[]{:S(2)}) collective-permute-start(f32[2,4,128,128]{3,2,1,0:T(8,128)S(1)} %get-tuple-element.22), channel_id=1, source_target_pairs={{0,128},{8,136},{16,144},{24,152},{32,160},{40,168},{48,176},{56,1... | collective-permute-start | bytes 1572872 | tf_op jit(solution)/shard_map/ppermute | solution.py:210
  23.2 3.7 %collective-permute-start.3 = (f32[8,4,128]{2,1,0:T(4,128)S(1)}, f32[8,4,128]{2,1,0:T(4,128)S(1)}, u32[]{:S(2)}, u32[]{:S(2)}) collective-permute-start(f32[8,4,128]{2,1,0:T(4,128)S(1)} %get-tuple-element.20), channel_id=1, source_target_pairs={{0,1},{1,0},{2,3},{3,2},{4,5},{5,4},{6,7},{7,6},{8,9},{9,8},{10,11... | collective-permute-start | bytes 49160 | tf_op jit(solution)/shard_map/ppermute | solution.py:214
  26.9 5.0 %collective-permute-start.4 = (f32[8,4,128]{2,1,0:T(4,128)S(1)}, f32[8,4,128]{2,1,0:T(4,128)S(1)}, u32[]{:S(2)}, u32[]{:S(2)}) collective-permute-start(f32[8,4,128]{2,1,0:T(4,128)S(1)} %add.6), channel_id=1, source_target_pairs={{0,2},{1,3},{2,0},{3,1},{4,6},{5,7},{6,4},{7,5},{8,10},{9,11},{10,... | collective-permute-start | bytes 49160 | tf_op jit(solution)/shard_map/ppermute | solution.py:214
  31.9 6.8 %collective-permute-start.5 = (f32[8,4,128]{2,1,0:T(4,128)S(1)}, f32[8,4,128]{2,1,0:T(4,128)S(1)}, u32[]{:S(2)}, u32[]{:S(2)}) collective-permute-start(f32[8,4,128]{2,1,0:T(4,128)S(1)} %add.7.square_a_ref), channel_id=1, source_target_pairs={{0,6},{1,7},{2,4},{3,5},{4,2},{5,3},{6,0},{7,1},{8,14},{9,15},{10,... | collective-permute-start | bytes 49160 | tf_op jit(solution)/shard_map/ppermute | solution.py:214

commit v3 on v2

v3 whole, which is shorter than its diff:
```python
import jax
import jax.numpy as jnp
from jax import lax
from jax.experimental import pallas as pl
from jax.experimental.pallas import tpu as pltpu
from jax.sharding import PartitionSpec as P

SLOTS_DEV = 8
MOVE = 3
STEPS = 4
N_REP = 32
N_HEAD = 8
HEADS = 32
DK = 128
HEADS_DEV = HEADS // N_HEAD
WIDTH = HEADS_DEV * DK
FAR = N_REP // 2
epsilon = 1e-06

HIGHEST = lax.Precision.HIGHEST
VMEM = pl.BlockSpec(memory_space=pltpu.VMEM)
SMEM = pl.BlockSpec(memory_space=pltpu.SMEM)
ANY = pl.BlockSpec(memory_space=pl.ANY)
HBM = pl.BlockSpec(memory_space=pltpu.HBM)
LONG = 10_000_000_000


def silu(x):
    x = x.astype(jnp.float32)
    return x / (1.0 + jnp.exp(-x))


def sender_of(move):
    me = lax.axis_index("rep")
    return lax.rem(me + (FAR if move < 2 else N_REP - 1), N_REP)


SOURCE, VALID, SLOT, STAYS, LIVE, INFO = 0, MOVE, 2 * MOVE, 3 * MOVE, 3 * MOVE + SLOTS_DEV, 3 * MOVE + 2 * SLOTS_DEV


def split(x):
    high = x.astype(jnp.bfloat16)
    return high, (x - high.astype(jnp.float32)).astype(jnp.bfloat16)


def dot(a, b, dims):
    return lax.dot_general(a, b, (dims, ((), ())), preferred_element_type=jnp.float32)


def read_out(query, state):
    rows = jnp.concatenate(split(query), axis=0)
    high, low = split(state)
    by_high = dot(rows, high, ((1,), (0,)))
    by_low = dot(rows, low, ((1,), (0,)))
    return by_high[:STEPS] + by_high[STEPS:] + by_low[:STEPS]


def later_by(x, gap):
    return x if gap == 0 else jnp.concatenate([jnp.zeros((gap, x.shape[1]), x.dtype), x[:-gap]], axis=0)


def head_slice(head):
    return slice(head * DK, (head + 1) * DK)


def times():
    return lax.broadcasted_iota(jnp.int32, (STEPS, DK), 0).astype(jnp.float32)


def ask_kernel(
    alive_ref, source_ref, target_ref, count_ref, rate_ref, query_ref,
    out_ref, near_query_ref, fade_ref, back_ref, info_ref,
):
    me = lax.axis_index("rep")
    for move in range(MOVE):
        sender = sender_of(move)
        slot = lax.rem(target_ref[move, sender], SLOTS_DEV)
        info_ref[SOURCE + move] = source_ref[move, me]
        info_ref[VALID + move] = (count_ref[sender] > move).astype(jnp.int32)
        info_ref[SLOT + move] = slot
        if move < 2:
            out_ref[move] = silu(query_ref[slot])
        else:
            near_query_ref[...] = silu(query_ref[slot])
    for slot in range(SLOTS_DEV):
        stays = alive_ref[slot]
        for move in range(MOVE):
            stays = jnp.where((count_ref[me] > move) & (source_ref[move, me] == slot), 0, stays)
        live = stays
        for move in range(MOVE):
            live = jnp.where((info_ref[VALID + move] == 1) & (info_ref[SLOT + move] == slot), 1, live)
        info_ref[STAYS + slot] = stays
        info_ref[LIVE + slot] = live
    for head in range(HEADS_DEV):
        fade_ref[:, head_slice(head)] = jnp.exp(-rate_ref[head] * (times() + 1.0))
        back_ref[:, head_slice(head)] = jnp.exp(-rate_ref[head] * (STEPS - 1.0 - times()))


def outbox_kernel(info_ref, states_ref, far_ref, near_ref, sems):
    copies = []
    for move in range(MOVE):
        out = far_ref.at[move] if move < 2 else near_ref.at[0]
        copies.append(pltpu.make_async_copy(states_ref.at[info_ref[SOURCE + move]], out, sems.at[move]))
    for copy in copies:
        copy.start()
    for copy in copies:
        copy.wait()


def answer_kernel(query_ref, far_ref, part_ref, out_ref):
    del part_ref
    for move in range(2):
        for head in range(HEADS_DEV):
            out_ref[move, :, head_slice(head)] = read_out(query_ref[move, :, head_slice(head)], far_ref[move, head])


def part_kernel(info_ref, fade_ref, query_ref, key_ref, value_ref, gate_ref, gain_ref, states_ref, out_ref, flag_ref, gate_out_ref):
    for slot in range(SLOTS_DEV):
        for move in range(MOVE):
            arrives = info_ref[VALID + move] * (info_ref[SLOT + move] == slot).astype(jnp.int32)
            flag_ref[move, slot] = jnp.full((STEPS, DK), arrives.astype(jnp.float32))
        live = info_ref[LIVE + slot].astype(jnp.float32)
        stays = info_ref[STAYS + slot].astype(jnp.float32)
        gate_out_ref[slot] = gain_ref[...] * live / (1.0 + jnp.exp(-gate_ref[slot].astype(jnp.float32)))
        queries, keys, values = silu(query_ref[slot]), silu(key_ref[slot]), silu(value_ref[slot])
        inside = [jnp.zeros((STEPS, DK), jnp.float32)] * HEADS_DEV
        for gap in range(STEPS):
            older_keys, older_values = later_by(keys, gap), later_by(values, gap)
            if gap:
                older_values = older_values * fade_ref[gap - 1:gap]
            for head in range(HEADS_DEV):
                at = head_slice(head)
                inside[head] += jnp.sum(queries[:, at] * older_keys[:, at], axis=1, keepdims=True) * older_values[:, at]
        for head in range(HEADS_DEV):
            at = head_slice(head)
            before = read_out(queries[:, at], states_ref[slot, head])
            out_ref[slot, :, at] = inside[head] + before * (fade_ref[:, at] * stays)


def state_kernel(
    info_ref, fade_ref, back_ref, key_ref, value_ref, states_ref, answer_ref, far_in_ref,
    new_ref, added_ref, far_ref, rows_ref, sems,
):
    del answer_ref, far_in_ref, far_ref
    copies = []
    for slot in range(SLOTS_DEV):
        live = info_ref[LIVE + slot].astype(jnp.float32)
        stays = info_ref[STAYS + slot].astype(jnp.float32)
        keys, values = silu(key_ref[slot]) * (back_ref[...] * live), silu(value_ref[slot])
        for head in range(HEADS_DEV):
            at = head_slice(head)
            value_high, value_low = split(values[:, at])
            faded_high, faded_low = split(keys[:, at])
            added = dot(
                jnp.concatenate([faded_high, faded_low, faded_high], axis=0),
                jnp.concatenate([value_high, value_high, value_low], axis=0), ((0,), (0,)))
            rows_ref[slot, head] = states_ref[slot, head] * (fade_ref[STEPS - 1:, at] * stays) + added
        copies.append(pltpu.make_async_copy(rows_ref.at[slot], new_ref.at[slot], sems.at[slot]))
        copies[-1].start()
    for move in range(MOVE):
        @pl.when(info_ref[VALID + move] == 1)
        def _(move=move):
            added_ref[move] = rows_ref[info_ref[SLOT + move]]

    for copy in copies:
        copy.wait()


def combine_kernel(answer_ref, near_ref, near_query_ref, part_ref, flag_ref, fade_ref, added_ref, out_ref, square_ref):
    del added_ref
    moved = [answer_ref[0], answer_ref[1], jnp.concatenate(
        [read_out(near_query_ref[:, head_slice(head)], near_ref[0, head]) for head in range(HEADS_DEV)], axis=1)]
    moved = [x * fade_ref[...] for x in moved]
    for slot in range(SLOTS_DEV):
        total = jnp.zeros((STEPS, DK), jnp.float32)
        for head in range(HEADS_DEV):
            at = head_slice(head)
            row = part_ref[slot, :, at]
            for move in range(MOVE):
                row = jnp.where(flag_ref[move, slot] > 0.0, row + moved[move][:, at], row)
            out_ref[slot, :, at] = row
            total += row * row
        square_ref[slot] = total


def final_kernel(
    info_ref, gate_ref, out_ref, square_a_ref, square_b_ref, fade_ref, added_ref, far_ref, near_ref, old_ref,
    attended_hbm, new_ref, attended_ref, rows_ref, sems,
):
    del old_ref
    copies = []
    for move in range(MOVE):
        valid = info_ref[VALID + move] == 1
        copy = pltpu.make_async_copy(rows_ref.at[move], new_ref.at[info_ref[SLOT + move]], sems.at[move])
        copies.append((valid, copy))
        for head in range(HEADS_DEV):
            came = far_ref[move, head] if move < 2 else near_ref[0, head]
            rows_ref[move, head] = came * fade_ref[STEPS - 1:, head_slice(head)] + added_ref[move, head]

        @pl.when(valid)
        def _(copy=copy):
            copy.start()

    for slot in range(SLOTS_DEV):
        total = jnp.sum(square_a_ref[slot] + square_b_ref[slot], axis=1, keepdims=True)
        scale = lax.rsqrt(total * (1.0 / (HEADS * DK)) + epsilon)
        attended_ref[slot] = (out_ref[slot] * gate_ref[slot] * scale).astype(jnp.bfloat16)
    out_copy = pltpu.make_async_copy(attended_ref, attended_hbm, sems.at[MOVE])
    out_copy.start()
    out_copy.wait()
    for valid, copy in copies:
        @pl.when(valid)
        def _(copy=copy):
            copy.wait()


def call(kernel, outs, in_specs, args, cost=100_000, limit=8, **more):
    return pl.pallas_call(
        kernel, out_shape=outs, in_specs=in_specs,
        compiler_params=pltpu.CompilerParams(vmem_limit_bytes=limit * 1024 * 1024),
        cost_estimate=pl.CostEstimate(flops=cost, bytes_accessed=cost, transcendentals=0), **more,
    )(*args)


def vmem(*shape, dtype=jnp.float32):
    return pltpu.VMEM(shape, dtype)


def in_hbm(*arrays):
    return tuple(pltpu.with_memory_space_constraint(x, pltpu.HBM) for x in arrays)


def over_rep(x, distance):
    return lax.ppermute(x, "rep", [(i, (i + distance) % N_REP) for i in range(N_REP)])


def over_head(x, flip):
    return lax.ppermute(x, "head", [(i, i ^ flip) for i in range(N_HEAD)])


def local(states, alive_flag, plan_source, plan_target, move_count, query_proj, key_proj, value_proj, gate_proj, decay_rate, norm_gain):
    row = (HEADS_DEV, DK, DK)
    features = (SLOTS_DEV, STEPS, WIDTH)
    asked, near_query, fade, back, info = call(
        ask_kernel, (vmem(2, STEPS, WIDTH), vmem(STEPS, WIDTH), vmem(STEPS, WIDTH), vmem(STEPS, WIDTH), pltpu.SMEM((INFO,), jnp.int32)),
        [SMEM] * 5 + [VMEM], in_hbm(alive_flag, plan_source.T, plan_target.T, move_count, decay_rate, query_proj),
        out_specs=(VMEM,) * 4 + (SMEM,))
    asked = over_rep(asked, FAR)
    far, near = call(
        outbox_kernel, (vmem(2, *row), vmem(1, *row)), [SMEM, HBM], (info, *in_hbm(states)), out_specs=(VMEM, VMEM),
        scratch_shapes=[pltpu.SemaphoreType.DMA((MOVE,))], cost=LONG)
    near = over_rep(near, 1)
    part, arrives, gate = call(
        part_kernel, (vmem(*features), vmem(MOVE, SLOTS_DEV, STEPS, DK), vmem(*features)), [SMEM] + [VMEM] * 7,
        (info, fade, query_proj, key_proj, value_proj, gate_proj, norm_gain.reshape(1, WIDTH), states),
        out_specs=(VMEM,) * 3, cost=1_000_000)
    answer = call(answer_kernel, vmem(2, STEPS, WIDTH), [VMEM, VMEM, ANY], (asked, far, part), out_specs=VMEM)
    new_states, added, far = call(
        state_kernel, (pltpu.HBM((SLOTS_DEV, *row), jnp.float32), vmem(MOVE, *row), vmem(2, *row)), [SMEM] + [VMEM] * 5 + [ANY] * 2,
        (info, fade, back, key_proj, value_proj, states, answer, far), out_specs=(HBM, VMEM, VMEM), input_output_aliases={7: 2},
        scratch_shapes=[pltpu.VMEM((SLOTS_DEV, *row), jnp.float32), pltpu.SemaphoreType.DMA((SLOTS_DEV,))], cost=LONG)
    answer = over_rep(answer, FAR)
    far = over_rep(far, FAR)
    out, square = call(
        combine_kernel, (vmem(*features), vmem(SLOTS_DEV, STEPS, DK)), [VMEM] * 6 + [ANY],
        (answer, near, near_query, part, arrives, fade, added), out_specs=(VMEM, VMEM), cost=LONG)
    square = square + over_head(square, 1)
    square = square + over_head(square, 2)
    other = over_head(square, 6)
    return call(
        final_kernel, (jax.ShapeDtypeStruct(features, jnp.bfloat16), jax.ShapeDtypeStruct((SLOTS_DEV, *row), jnp.float32)),
        [SMEM] + [VMEM] * 8 + [ANY], (info, gate, out, square, other, fade, added, far, near, new_states),
        out_specs=(ANY, ANY), input_output_aliases={9: 1},
        scratch_shapes=[
            pltpu.VMEM(features, jnp.bfloat16), pltpu.VMEM((MOVE, *row), jnp.float32), pltpu.SemaphoreType.DMA((MOVE + 1,))])


def solution(mesh):
    return jax.shard_map(
        local,
        mesh=mesh,
        in_specs=(
            P("rep", "head", None, None),
            P("rep"),
            P(),
            P(),
            P(),
            P("rep", None, "head"),
            P("rep", None, "head"),
            P("rep", None, "head"),
            P("rep", None, "head"),
            P("head"),
            P("head"),
        ),
        out_specs=(P("rep", None, "head"), P("rep", "head", None, None)),
        check_vma=False,
    )
```

time: 41.1 us -> 33 us (0.80)
  starting transfers between devices: 19.1 us -> 15.6 us
  Pallas kernels: 8.76 us -> 5.88 us
  local copies, waits for them, and re-layouts: 3.04 us -> 0.44 us
  waiting for transfers between devices: 9.12 us -> 10.2 us
    ppermute x4, starting transfers between devices: 10.7 us -> 7.07 us  [over_rep(): lax.ppermute(x, 'rep', [(i, (i + distance) % N_REP) for i in range(N_REP)])]
    pallas_call x6 -> x7, Pallas kernels: 8.76 us -> 5.88 us  [call(): pl.pallas_call(kernel, out_shape=outs, in_specs=in_specs, compiler_params...]
    unnamed x28 -> x12, local copies, waits for them, and re-layouts: 3.04 us -> 0.44 us
    ppermute x4, waiting for transfers between devices: 2.06 us -> 3.12 us  [over_rep(): lax.ppermute(x, 'rep', [(i, (i + distance) % N_REP) for i in range(N_REP)])]
  transfers between devices with their start and end apart: 7 -> 7, of which waited for: 4 -> 5; matrix products, arithmetic and copies ran while one was open for 0% -> 0% of each run, Pallas kernels for 11% -> 12%
where the time goes in v3:
time: 33 us; the launch traced here: 32.8 us
  starting transfers between devices  15.6 us (47%)
  waiting for transfers between devices  10.2 us (31%)
  Pallas kernels  5.88 us (18%)
  between operations  0.71 us (2%)
  local copies, waits for them, and re-layouts  0.44 us (1%)
    ppermute x3, starting transfers between devices, over_head(): return lax.ppermute(x, 'head', [(i, i ^ flip) for i in range(N_HEAD)])  8.52 us
    ppermute x4, starting transfers between devices, over_rep(): lax.ppermute(x, 'rep', [(i, (i + distance) % N_REP) for i in range(N_REP)])  7.07 us
    ppermute x3, waiting for transfers between devices, over_head(): return lax.ppermute(x, 'head', [(i, i ^ flip) for i in range(N_HEAD)])  7.06 us
    pallas_call x7, Pallas kernels, call(): pl.pallas_call(kernel, out_shape=outs, in_specs=in_specs, compiler_params...  5.88 us
    ppermute x4, waiting for transfers between devices, over_rep(): lax.ppermute(x, 'rep', [(i, (i + distance) % N_REP) for i in range(N_REP)])  3.12 us
  transfers between devices with their start and end apart: 7, of which 5 were waited for; matrix products, arithmetic and copies ran while one was open for 0% of the time, Pallas kernels for 12%

profile of v3, /device:TPU:32, one launch (start us, length us, event | category | flops | bytes accessed | tf_op | source)
XLA Modules:
  0.0 32.8 jit_solution(15708601325435047768)
XLA Ops:
  0.6 0.9 %shard_map.122 = (f32[2,4,512]{2,1,0:T(4,128)S(1)}, f32[4,512]{1,0:T(4,128)S(1)}, f32[4,512]{1,0:T(4,128)S(1)}, f32[4,512]{1,0:T(4,128)S(1)}, s32[25]{0:T(128)S(4)}) custom-call(s32[8]{0:T(128)} %alive_ref.1, s32[3,32]{1,0:T(4,128)} %bitcast.4, s32[3,32]{1,0:T(4,128)} %bitcast.5, s32[32]{0:T(128)} %count_ref.1, f32[4]{0:T(128)} %rate_ref.1, ...), custom_call_target="tpu_custom_call" | custom-call | flops 100000 | bytes 100000 | tf_op jit(solution)/shard_map/pallas_call | solution.py:218
  1.5 3.3 %collective-permute-start = (f32[2,4,512]{2,1,0:T(4,128)S(1)}, f32[2,4,512]{2,1,0:T(4,128)S(1)}, u32[]{:S(2)}, u32[]{:S(2)}) collective-permute-start(f32[2,4,512]{2,1,0:T(4,128)S(1)} %get-tuple-element.20), channel_id=1, source_target_pairs={{0,128},{8,136},{16,144},{24,152},{32,160},{40,168},{48,176},{56,1... | collective-permute-start | bytes 49160 | tf_op jit(solution)/shard_map/ppermute | solution.py:234
  4.8 0.0 copy-start
  4.8 0.0 copy-start.1
  4.8 0.0 copy-start.2
  4.8 0.0 copy-start.3
  4.8 0.0 copy-start.4
  4.9 0.0 copy-start.5
  4.9 1.3 %shard_map.124 = (f32[2,4,128,128]{3,2,1,0:T(8,128)S(1)}, f32[1,4,128,128]{3,2,1,0:T(8,128)S(1)}) custom-call(s32[25]{0:T(128)S(4)} %get-tuple-element.17.info_ref, f32[8,4,128,128]{3,2,1,0:T(8,128)} %states_ref.5), custom_call_target="tpu_custom_call" | custom-call | flops 10000000000 | bytes 10000000000 | tf_op jit(solution)/shard_map/pallas_call | solution.py:218
  6.2 0.1 collective-permute-start.2
  6.2 0.4 %copy-done = f32[8,4,128,128]{3,2,1,0:T(8,128)S(1)} copy-done((f32[8,4,128,128]{3,2,1,0:T(8,128)S(1)}, f32[8,4,128,128]{3,2,1,0:T(8,128)}, u32[]{:S(2)}) %copy-start) | copy-done | bytes 2097176
  6.7 0.0 copy-done.1
  6.7 0.0 copy-done.2
  6.7 0.0 copy-done.3
  6.7 0.0 copy-done.4
  6.7 0.0 copy-done.5
  6.7 0.7 %shard_map.123 = (f32[8,4,512]{2,1,0:T(4,128)S(1)}, f32[3,8,4,128]{3,2,1,0:T(4,128)S(1)}, f32[8,4,512]{2,1,0:T(4,128)S(1)}) custom-call(s32[25]{0:T(128)S(4)} %get-tuple-element.17.info_ref, f32[4,512]{1,0:T(4,128)S(1)} %get-tuple-element.18.fade_ref, bf16[8,4,512]{2,1,0:T(4,128)(2,1)S(1)} %copy-done.1, bf16[8,4,512]{2,1,0:T(4,128)(2,1)S(1)} %copy-done.3, ...), custom_call_target="tpu_custom_call" | custom-call | flops 1000000 | bytes 1000000 | tf_op jit(solution)/shard_map/pallas_call | solution.py:218
  7.4 0.0 collective-permute-done.query_ref
  7.4 0.2 shard_map.125.answer_ref
  7.6 2.8 %collective-permute-start.1 = (f32[2,4,512]{2,1,0:T(4,128)S(1)}, f32[2,4,512]{2,1,0:T(4,128)S(1)}, u32[]{:S(2)}, u32[]{:S(2)}) collective-permute-start(f32[2,4,512]{2,1,0:T(4,128)S(1)} %shard_map.125.answer_ref), channel_id=1, source_target_pairs={{0,128},{8,136},{16,144},{24,152},{32,160},{40,168},{48,176},{56,1... | collective-permute-start | bytes 49160 | tf_op jit(solution)/shard_map/ppermute | solution.py:234
  10.4 1.6 %shard_map.126 = (f32[8,4,128,128]{3,2,1,0:T(8,128)}, f32[3,4,128,128]{3,2,1,0:T(8,128)S(1)}, f32[2,4,128,128]{3,2,1,0:T(8,128)S(1)}) custom-call(s32[25]{0:T(128)S(4)} %get-tuple-element.17.info_ref, f32[4,512]{1,0:T(4,128)S(1)} %get-tuple-element.18.fade_ref, f32[4,512]{1,0:T(4,128)S(1)} %get-tuple-element.26.back_ref, ...), custom_call_target="tpu_custom_call", output_to_operand_aliasing={{2}: (7, {})} | custom-call | flops 10000000000 | bytes 10000000000 | tf_op jit(solution)/shard_map/pallas_call | solution.py:218
  12.0 0.9 %collective-permute-start.6 = (f32[2,4,128,128]{3,2,1,0:T(8,128)S(1)}, f32[2,4,128,128]{3,2,1,0:T(8,128)S(1)}, u32[]{:S(2)}, u32[]{:S(2)}) collective-permute-start(f32[2,4,128,128]{3,2,1,0:T(8,128)S(1)} %get-tuple-element.30), channel_id=1, source_target_pairs={{0,128},{8,136},{16,144},{24,152},{32,160},{40,168},{48,176},{56,1... | collective-permute-start | bytes 1572872 | tf_op jit(solution)/shard_map/ppermute | solution.py:234
  12.9 2.3 %collective-permute-done.1.answer_ref = f32[2,4,512]{2,1,0:T(4,128)S(1)} collective-permute-done((f32[2,4,512]{2,1,0:T(4,128)S(1)}, f32[2,4,512]{2,1,0:T(4,128)S(1)}, u32[]{:S(2)}, u32[]{:S(2)}) %collective-permute-start.1) | collective-permute-done | bytes 16416 | tf_op jit(solution)/shard_map/ppermute | solution.py:234
  15.3 0.8 %collective-permute-done.2.near_ref = f32[1,4,128,128]{3,2,1,0:T(8,128)S(1)} collective-permute-done((f32[1,4,128,128]{3,2,1,0:T(8,128)S(1)}, f32[1,4,128,128]{3,2,1,0:T(8,128)S(1)}, u32[]{:S(2)}, u32[]{:S(2)}) %collective-permute-start.2) | collective-permute-done | bytes 262176 | tf_op jit(solution)/shard_map/ppermute | solution.py:234
  16.1 0.2 shard_map.127
  16.3 0.2 collective-permute-start.3
  16.5 3.6 %collective-permute-done.3 = f32[8,4,128]{2,1,0:T(4,128)S(1)} collective-permute-done((f32[8,4,128]{2,1,0:T(4,128)S(1)}, f32[8,4,128]{2,1,0:T(4,128)S(1)}, u32[]{:S(2)}, u32[]{:S(2)}) %collective-permute-start.3) | collective-permute-done | bytes 16416 | tf_op jit(solution)/shard_map/ppermute | solution.py:238
  20.1 3.3 %collective-permute-start.4 = (f32[8,4,128]{2,1,0:T(4,128)S(1)}, f32[8,4,128]{2,1,0:T(4,128)S(1)}, u32[]{:S(2)}, u32[]{:S(2)}) collective-permute-start(f32[8,4,128]{2,1,0:T(4,128)S(1)} %add.6), channel_id=1, source_target_pairs={{0,2},{1,3},{2,0},{3,1},{4,6},{5,7},{6,4},{7,5},{8,10},{9,11},{10,... | collective-permute-start | bytes 49160 | tf_op jit(solution)/shard_map/ppermute | solution.py:238
  23.4 1.7 %collective-permute-done.4 = f32[8,4,128]{2,1,0:T(4,128)S(1)} collective-permute-done((f32[8,4,128]{2,1,0:T(4,128)S(1)}, f32[8,4,128]{2,1,0:T(4,128)S(1)}, u32[]{:S(2)}, u32[]{:S(2)}) %collective-permute-start.4) | collective-permute-done | bytes 16416 | tf_op jit(solution)/shard_map/ppermute | solution.py:238
  25.1 5.1 %collective-permute-start.5 = (f32[8,4,128]{2,1,0:T(4,128)S(1)}, f32[8,4,128]{2,1,0:T(4,128)S(1)}, u32[]{:S(2)}, u32[]{:S(2)}) collective-permute-start(f32[8,4,128]{2,1,0:T(4,128)S(1)} %add.7.square_a_ref), channel_id=1, source_target_pairs={{0,6},{1,7},{2,4},{3,5},{4,2},{5,3},{6,0},{7,1},{8,14},{9,15},{10,... | collective-permute-start | bytes 49160 | tf_op jit(solution)/shard_map/ppermute | solution.py:238
  30.1 1.7 %collective-permute-done.5.square_b_ref = f32[8,4,128]{2,1,0:T(4,128)S(1)} collective-permute-done((f32[8,4,128]{2,1,0:T(4,128)S(1)}, f32[8,4,128]{2,1,0:T(4,128)S(1)}, u32[]{:S(2)}, u32[]{:S(2)}) %collective-permute-start.5) | collective-permute-done | bytes 16416 | tf_op jit(solution)/shard_map/ppermute | solution.py:238
  31.9 0.0 collective-permute-done.6.far_ref
  31.9 0.9 %shard_map.128 = (bf16[8,4,512]{2,1,0:T(4,128)(2,1)}, f32[8,4,128,128]{3,2,1,0:T(8,128)}) custom-call(s32[25]{0:T(128)S(4)} %get-tuple-element.17.info_ref, f32[8,4,512]{2,1,0:T(4,128)S(1)} %get-tuple-element.19.gate_ref, f32[8,4,512]{2,1,0:T(4,128)S(1)} %get-tuple-element.28.out_ref, ...), custom_call_target="tpu_custom_call", output_to_operand_aliasing={{1}: (9, {})} | custom-call | flops 100000 | bytes 100000 | tf_op jit(solution)/shard_map/pallas_call | solution.py:218
  (2 shorter events, 0.0 us)
Async XLA Ops:
  1.5 5.8 %collective-permute-start = (f32[2,4,512]{2,1,0:T(4,128)S(1)}, f32[2,4,512]{2,1,0:T(4,128)S(1)}, u32[]{:S(2)}, u32[]{:S(2)}) collective-permute-start(f32[2,4,512]{2,1,0:T(4,128)S(1)} %get-tuple-element.20), channel_id=1, source_target_pairs={{0,128},{8,136},{16,144},{24,152},{32,160},{40,168},{48,176},{56,1... | collective-permute-start | bytes 49160 | tf_op jit(solution)/shard_map/ppermute | solution.py:234
  4.8 1.8 %copy-start = (f32[8,4,128,128]{3,2,1,0:T(8,128)S(1)}, f32[8,4,128,128]{3,2,1,0:T(8,128)}, u32[]{:S(2)}) copy-start(f32[8,4,128,128]{3,2,1,0:T(8,128)} %states_ref.5) | copy-start | bytes 6291460
  4.8 1.8 %copy-start.1 = (bf16[8,4,512]{2,1,0:T(4,128)(2,1)S(1)}, bf16[8,4,512]{2,1,0:T(4,128)(2,1)}, u32[]{:S(2)}) copy-start(bf16[8,4,512]{2,1,0:T(4,128)(2,1)} %query_ref.3) | copy-start | bytes 98308
  4.8 1.8 %copy-start.2 = (bf16[8,4,512]{2,1,0:T(4,128)(2,1)S(1)}, bf16[8,4,512]{2,1,0:T(4,128)(2,1)}, u32[]{:S(2)}) copy-start(bf16[8,4,512]{2,1,0:T(4,128)(2,1)} %gate_ref.1) | copy-start | bytes 98308
  4.8 1.8 %copy-start.3 = (bf16[8,4,512]{2,1,0:T(4,128)(2,1)S(1)}, bf16[8,4,512]{2,1,0:T(4,128)(2,1)}, u32[]{:S(2)}) copy-start(bf16[8,4,512]{2,1,0:T(4,128)(2,1)} %key_ref.3) | copy-start | bytes 98308
  4.8 1.8 %copy-start.4 = (bf16[8,4,512]{2,1,0:T(4,128)(2,1)S(1)}, bf16[8,4,512]{2,1,0:T(4,128)(2,1)}, u32[]{:S(2)}) copy-start(bf16[8,4,512]{2,1,0:T(4,128)(2,1)} %value_ref.3) | copy-start | bytes 98308
  4.9 1.8 %copy-start.5 = (f32[512]{0:T(512)S(1)}, f32[512]{0:T(512)}, u32[]{:S(2)}) copy-start(f32[512]{0:T(512)} %param.21) | copy-start | bytes 6148
  6.2 9.9 %collective-permute-start.2 = (f32[1,4,128,128]{3,2,1,0:T(8,128)S(1)}, f32[1,4,128,128]{3,2,1,0:T(8,128)S(1)}, u32[]{:S(2)}, u32[]{:S(2)}) collective-permute-start(f32[1,4,128,128]{3,2,1,0:T(8,128)S(1)} %get-tuple-element.23), channel_id=1, source_target_pairs={{0,8},{8,16},{16,24},{24,32},{32,40},{40,48},{48,56},{56,64},{64,7... | collective-permute-start | bytes 786440 | tf_op jit(solution)/shard_map/ppermute | solution.py:234
  7.6 7.7 %collective-permute-start.1 = (f32[2,4,512]{2,1,0:T(4,128)S(1)}, f32[2,4,512]{2,1,0:T(4,128)S(1)}, u32[]{:S(2)}, u32[]{:S(2)}) collective-permute-start(f32[2,4,512]{2,1,0:T(4,128)S(1)} %shard_map.125.answer_ref), channel_id=1, source_target_pairs={{0,128},{8,136},{16,144},{24,152},{32,160},{40,168},{48,176},{56,1... | collective-permute-start | bytes 49160 | tf_op jit(solution)/shard_map/ppermute | solution.py:234
  12.0 19.8 %collective-permute-start.6 = (f32[2,4,128,128]{3,2,1,0:T(8,128)S(1)}, f32[2,4,128,128]{3,2,1,0:T(8,128)S(1)}, u32[]{:S(2)}, u32[]{:S(2)}) collective-permute-start(f32[2,4,128,128]{3,2,1,0:T(8,128)S(1)} %get-tuple-element.30), channel_id=1, source_target_pairs={{0,128},{8,136},{16,144},{24,152},{32,160},{40,168},{48,176},{56,1... | collective-permute-start | bytes 1572872 | tf_op jit(solution)/shard_map/ppermute | solution.py:234
  16.3 3.8 %collective-permute-start.3 = (f32[8,4,128]{2,1,0:T(4,128)S(1)}, f32[8,4,128]{2,1,0:T(4,128)S(1)}, u32[]{:S(2)}, u32[]{:S(2)}) collective-permute-start(f32[8,4,128]{2,1,0:T(4,128)S(1)} %get-tuple-element.29), channel_id=1, source_target_pairs={{0,1},{1,0},{2,3},{3,2},{4,5},{5,4},{6,7},{7,6},{8,9},{9,8},{10,11... | collective-permute-start | bytes 49160 | tf_op jit(solution)/shard_map/ppermute | solution.py:238
  20.1 5.0 %collective-permute-start.4 = (f32[8,4,128]{2,1,0:T(4,128)S(1)}, f32[8,4,128]{2,1,0:T(4,128)S(1)}, u32[]{:S(2)}, u32[]{:S(2)}) collective-permute-start(f32[8,4,128]{2,1,0:T(4,128)S(1)} %add.6), channel_id=1, source_target_pairs={{0,2},{1,3},{2,0},{3,1},{4,6},{5,7},{6,4},{7,5},{8,10},{9,11},{10,... | collective-permute-start | bytes 49160 | tf_op jit(solution)/shard_map/ppermute | solution.py:238
  25.1 6.8 %collective-permute-start.5 = (f32[8,4,128]{2,1,0:T(4,128)S(1)}, f32[8,4,128]{2,1,0:T(4,128)S(1)}, u32[]{:S(2)}, u32[]{:S(2)}) collective-permute-start(f32[8,4,128]{2,1,0:T(4,128)S(1)} %add.7.square_a_ref), channel_id=1, source_target_pairs={{0,6},{1,7},{2,4},{3,5},{4,2},{5,3},{6,0},{7,1},{8,14},{9,15},{10,... | collective-permute-start | bytes 49160 | tf_op jit(solution)/shard_map/ppermute | solution.py:238

commit v4 on v3

--- a/solution.py
+++ b/solution.py
@@ -107,14 +107,17 @@
         copy.wait()
 
 
-def answer_kernel(query_ref, far_ref, part_ref, out_ref):
-    del part_ref
+def answer_kernel(query_ref, far_ref, out_ref):
     for move in range(2):
         for head in range(HEADS_DEV):
             out_ref[move, :, head_slice(head)] = read_out(query_ref[move, :, head_slice(head)], far_ref[move, head])
 
 
-def part_kernel(info_ref, fade_ref, query_ref, key_ref, value_ref, gate_ref, gain_ref, states_ref, out_ref, flag_ref, gate_out_ref):
+def part_kernel(
+    info_ref, fade_ref, query_ref, key_ref, value_ref, gate_ref, gain_ref, states_ref, answer_ref, far_in_ref,
+    out_ref, flag_ref, gate_out_ref, far_ref,
+):
+    del answer_ref, far_in_ref, far_ref
     for slot in range(SLOTS_DEV):
         for move in range(MOVE):
             arrives = info_ref[VALID + move] * (info_ref[SLOT + move] == slot).astype(jnp.int32)
@@ -138,10 +141,10 @@
 
 
 def state_kernel(
-    info_ref, fade_ref, back_ref, key_ref, value_ref, states_ref, answer_ref, far_in_ref,
-    new_ref, added_ref, far_ref, rows_ref, sems,
+    info_ref, fade_ref, back_ref, key_ref, value_ref, states_ref, square_ref,
+    new_ref, added_ref, rows_ref, sems,
 ):
-    del answer_ref, far_in_ref, far_ref
+    del square_ref
     copies = []
     for slot in range(SLOTS_DEV):
         live = info_ref[LIVE + slot].astype(jnp.float32)
@@ -166,11 +169,12 @@
         copy.wait()
 
 
-def combine_kernel(answer_ref, near_ref, near_query_ref, part_ref, flag_ref, fade_ref, added_ref, out_ref, square_ref):
-    del added_ref
+def combine_kernel(answer_ref, near_ref, near_query_ref, part_ref, flag_ref, fade_ref, out_ref, square_ref):
     moved = [answer_ref[0], answer_ref[1], jnp.concatenate(
         [read_out(near_query_ref[:, head_slice(head)], near_ref[0, head]) for head in range(HEADS_DEV)], axis=1)]
     moved = [x * fade_ref[...] for x in moved]
+    lanes = lax.broadcasted_iota(jnp.int32, (STEPS, DK), 1)
+    squares = jnp.zeros((STEPS, DK), jnp.float32)
     for slot in range(SLOTS_DEV):
         total = jnp.zeros((STEPS, DK), jnp.float32)
         for head in range(HEADS_DEV):
@@ -180,7 +184,8 @@
                 row = jnp.where(flag_ref[move, slot] > 0.0, row + moved[move][:, at], row)
             out_ref[slot, :, at] = row
             total += row * row
-        square_ref[slot] = total
+        squares = jnp.where(lanes == slot, jnp.sum(total, axis=1, keepdims=True), squares)
+    square_ref[...] = squares
 
 
 def final_kernel(
@@ -201,10 +206,9 @@
         def _(copy=copy):
             copy.start()
 
-    for slot in range(SLOTS_DEV):
-        total = jnp.sum(square_a_ref[slot] + square_b_ref[slot], axis=1, keepdims=True)
-        scale = lax.rsqrt(total * (1.0 / (HEADS * DK)) + epsilon)
-        attended_ref[slot] = (out_ref[slot] * gate_ref[slot] * scale).astype(jnp.bfloat16)
+    scales = lax.rsqrt((square_a_ref[...] + square_b_ref[...]) * (1.0 / (HEADS * DK)) + epsilon)
+    for slot in range(SLOTS_DEV):
+        attended_ref[slot] = (out_ref[slot] * gate_ref[slot] * scales[:, slot:slot + 1]).astype(jnp.bfloat16)
     out_copy = pltpu.make_async_copy(attended_ref, attended_hbm, sems.at[MOVE])
     out_copy.start()
     out_copy.wait()
@@ -244,26 +248,27 @@
     asked, near_query, fade, back, info = call(
         ask_kernel, (vmem(2, STEPS, WIDTH), vmem(STEPS, WIDTH), vmem(STEPS, WIDTH), vmem(STEPS, WIDTH), pltpu.SMEM((INFO,), jnp.int32)),
         [SMEM] * 5 + [VMEM], in_hbm(alive_flag, plan_source.T, plan_target.T, move_count, decay_rate, query_proj),
-        out_specs=(VMEM,) * 4 + (SMEM,))
+        out_specs=(VMEM,) * 4 + (SMEM,), cost=LONG)
     asked = over_rep(asked, FAR)
     far, near = call(
-        outbox_kernel, (vmem(2, *row), vmem(1, *row)), [SMEM, HBM], (info, *in_hbm(states)), out_specs=(VMEM, VMEM),
+        outbox_kernel, (vmem(2, *row), vmem(1, *row)), [SMEM, ANY], (info, states), out_specs=(VMEM, VMEM),
         scratch_shapes=[pltpu.SemaphoreType.DMA((MOVE,))], cost=LONG)
     near = over_rep(near, 1)
-    part, arrives, gate = call(
-        part_kernel, (vmem(*features), vmem(MOVE, SLOTS_DEV, STEPS, DK), vmem(*features)), [SMEM] + [VMEM] * 7,
-        (info, fade, query_proj, key_proj, value_proj, gate_proj, norm_gain.reshape(1, WIDTH), states),
-        out_specs=(VMEM,) * 3, cost=1_000_000)
-    answer = call(answer_kernel, vmem(2, STEPS, WIDTH), [VMEM, VMEM, ANY], (asked, far, part), out_specs=VMEM)
-    new_states, added, far = call(
-        state_kernel, (pltpu.HBM((SLOTS_DEV, *row), jnp.float32), vmem(MOVE, *row), vmem(2, *row)), [SMEM] + [VMEM] * 5 + [ANY] * 2,
-        (info, fade, back, key_proj, value_proj, states, answer, far), out_specs=(HBM, VMEM, VMEM), input_output_aliases={7: 2},
-        scratch_shapes=[pltpu.VMEM((SLOTS_DEV, *row), jnp.float32), pltpu.SemaphoreType.DMA((SLOTS_DEV,))], cost=LONG)
+    answer = call(answer_kernel, vmem(2, STEPS, WIDTH), [VMEM, VMEM], (asked, far), out_specs=VMEM)
+    part, arrives, gate, far = call(
+        part_kernel, (vmem(*features), vmem(MOVE, SLOTS_DEV, STEPS, DK), vmem(*features), vmem(2, *row)),
+        [SMEM] + [VMEM] * 7 + [ANY] * 2,
+        (info, fade, query_proj, key_proj, value_proj, gate_proj, norm_gain.reshape(1, WIDTH), states, answer, far),
+        out_specs=(VMEM,) * 4, input_output_aliases={9: 3}, cost=LONG)
     answer = over_rep(answer, FAR)
     far = over_rep(far, FAR)
     out, square = call(
-        combine_kernel, (vmem(*features), vmem(SLOTS_DEV, STEPS, DK)), [VMEM] * 6 + [ANY],
-        (answer, near, near_query, part, arrives, fade, added), out_specs=(VMEM, VMEM), cost=LONG)
+        combine_kernel, (vmem(*features), vmem(STEPS, DK)), [VMEM] * 6,
+        (answer, near, near_query, part, arrives, fade), out_specs=(VMEM, VMEM), cost=LONG)
+    new_states, added = call(
+        state_kernel, (pltpu.HBM((SLOTS_DEV, *row), jnp.float32), vmem(MOVE, *row)), [SMEM] + [VMEM] * 5 + [ANY],
+        (info, fade, back, key_proj, value_proj, states, square), out_specs=(HBM, VMEM),
+        scratch_shapes=[pltpu.VMEM((SLOTS_DEV, *row), jnp.float32), pltpu.SemaphoreType.DMA((SLOTS_DEV,))], cost=1_000_000)
     square = square + over_head(square, 1)
     square = square + over_head(square, 2)
     other = over_head(square, 6)

time: 33 us -> 31.5 us (0.955)
  Pallas kernels: 5.88 us -> 4.93 us
  local copies, waits for them, and re-layouts: 0.44 us -> 0.03 us
    ppermute x3, waiting for transfers between devices: 7.06 us -> 4.91 us  [over_head(): return lax.ppermute(x, 'head', [(i, i ^ flip) for i in range(N_HEAD)])]
    ppermute x4, waiting for transfers between devices: 3.12 us -> 5.17 us  [over_rep(): lax.ppermute(x, 'rep', [(i, (i + distance) % N_REP) for i in range(N_REP)])]
    pallas_call x7, Pallas kernels: 5.88 us -> 4.93 us  [call(): pl.pallas_call(kernel, out_shape=outs, in_specs=in_specs, compiler_params...]
    unnamed x12, local copies, waits for them, and re-layouts: 0.44 us -> 0.03 us
  transfers between devices with their start and end apart: 7 -> 7, of which waited for: 5 -> 5; matrix products, arithmetic and copies ran while one was open for 0% -> 0% of each run, Pallas kernels for 12% -> 9%
where the time goes in v4:
time: 31.5 us; the launch traced here: 31.4 us
  starting transfers between devices  15.7 us (50%)
  waiting for transfers between devices  10.1 us (32%)
  Pallas kernels  4.93 us (16%)
  between operations  0.73 us (2%)
    ppermute x3, starting transfers between devices, over_head(): return lax.ppermute(x, 'head', [(i, i ^ flip) for i in range(N_HEAD)])  8.61 us
    ppermute x4, starting transfers between devices, over_rep(): lax.ppermute(x, 'rep', [(i, (i + distance) % N_REP) for i in range(N_REP)])  7.05 us
    ppermute x4, waiting for transfers between devices, over_rep(): lax.ppermute(x, 'rep', [(i, (i + distance) % N_REP) for i in range(N_REP)])  5.17 us
    pallas_call x7, Pallas kernels, call(): pl.pallas_call(kernel, out_shape=outs, in_specs=in_specs, compiler_params...  4.93 us
    ppermute x3, waiting for transfers between devices, over_head(): return lax.ppermute(x, 'head', [(i, i ^ flip) for i in range(N_HEAD)])  4.91 us
  transfers between devices with their start and end apart: 7, of which 5 were waited for; matrix products, arithmetic and copies ran while one was open for 0% of the time, Pallas kernels for 9%

profile of v4, /device:TPU:32, one launch (start us, length us, event | category | flops | bytes accessed | tf_op | source)
XLA Modules:
  0.0 31.4 jit_solution(2774742275600857527)
XLA Ops:
  0.6 0.0 copy-start
  0.6 1.1 %shard_map.122 = (f32[2,4,512]{2,1,0:T(4,128)S(1)}, f32[4,512]{1,0:T(4,128)S(1)}, f32[4,512]{1,0:T(4,128)S(1)}, f32[4,512]{1,0:T(4,128)S(1)}, s32[25]{0:T(128)S(4)}) custom-call(s32[8]{0:T(128)} %alive_ref.1, s32[3,32]{1,0:T(4,128)} %bitcast.4, s32[3,32]{1,0:T(4,128)} %bitcast.5, s32[32]{0:T(128)} %count_ref.1, f32[4]{0:T(128)} %rate_ref.1, ...), custom_call_target="tpu_custom_call" | custom-call | flops 10000000000 | bytes 10000000000 | tf_op jit(solution)/shard_map/pallas_call | solution.py:222
  1.7 3.3 %collective-permute-start = (f32[2,4,512]{2,1,0:T(4,128)S(1)}, f32[2,4,512]{2,1,0:T(4,128)S(1)}, u32[]{:S(2)}, u32[]{:S(2)}) collective-permute-start(f32[2,4,512]{2,1,0:T(4,128)S(1)} %get-tuple-element.19), channel_id=1, source_target_pairs={{0,128},{8,136},{16,144},{24,152},{32,160},{40,168},{48,176},{56,1... | collective-permute-start | bytes 49160 | tf_op jit(solution)/shard_map/ppermute | solution.py:238
  5.0 0.0 copy-done
  5.0 0.0 copy-start.1
  5.0 0.0 copy-start.2
  5.0 0.0 copy-start.3
  5.0 0.0 copy-start.4
  5.0 0.0 copy-start.5
  5.0 0.1 shard_map.123
  5.1 0.1 collective-permute-start.2
  5.2 1.8 %collective-permute-done.query_ref = f32[2,4,512]{2,1,0:T(4,128)S(1)} collective-permute-done((f32[2,4,512]{2,1,0:T(4,128)S(1)}, f32[2,4,512]{2,1,0:T(4,128)S(1)}, u32[]{:S(2)}, u32[]{:S(2)}) %collective-permute-start) | collective-permute-done | bytes 16416 | tf_op jit(solution)/shard_map/ppermute | solution.py:238
  7.0 0.2 shard_map.124.answer_ref
  7.3 3.3 %collective-permute-start.1 = (f32[2,4,512]{2,1,0:T(4,128)S(1)}, f32[2,4,512]{2,1,0:T(4,128)S(1)}, u32[]{:S(2)}, u32[]{:S(2)}) collective-permute-start(f32[2,4,512]{2,1,0:T(4,128)S(1)} %shard_map.124.answer_ref), channel_id=1, source_target_pairs={{0,128},{8,136},{16,144},{24,152},{32,160},{40,168},{48,176},{56,1... | collective-permute-start | bytes 49160 | tf_op jit(solution)/shard_map/ppermute | solution.py:238
  10.5 0.0 copy-done.1
  10.6 0.0 copy-done.2
  10.6 0.0 copy-done.3
  10.6 0.0 copy-done.4
  10.6 0.0 copy-done.5
  10.6 0.7 %shard_map.125 = (f32[8,4,512]{2,1,0:T(4,128)S(1)}, f32[3,8,4,128]{3,2,1,0:T(4,128)S(1)}, f32[8,4,512]{2,1,0:T(4,128)S(1)}, f32[2,4,128,128]{3,2,1,0:T(8,128)S(1)}) custom-call(s32[25]{0:T(128)S(4)} %get-tuple-element.17.info_ref, f32[4,512]{1,0:T(4,128)S(1)} %get-tuple-element.18.fade_ref, ...), custom_call_target="tpu_custom_call", output_to_operand_aliasing={{3}: (9, {})} | custom-call | flops 10000000000 | bytes 10000000000 | tf_op jit(solution)/shard_map/pallas_call | solution.py:222
  11.3 0.4 %collective-permute-start.6 = (f32[2,4,128,128]{3,2,1,0:T(8,128)S(1)}, f32[2,4,128,128]{3,2,1,0:T(8,128)S(1)}, u32[]{:S(2)}, u32[]{:S(2)}) collective-permute-start(f32[2,4,128,128]{3,2,1,0:T(8,128)S(1)} %get-tuple-element.30), channel_id=1, source_target_pairs={{0,128},{8,136},{16,144},{24,152},{32,160},{40,168},{48,176},{56,1... | collective-permute-start | bytes 1572872 | tf_op jit(solution)/shard_map/ppermute | solution.py:238
  11.7 2.8 %collective-permute-done.1.answer_ref = f32[2,4,512]{2,1,0:T(4,128)S(1)} collective-permute-done((f32[2,4,512]{2,1,0:T(4,128)S(1)}, f32[2,4,512]{2,1,0:T(4,128)S(1)}, u32[]{:S(2)}, u32[]{:S(2)}) %collective-permute-start.1) | collective-permute-done | bytes 16416 | tf_op jit(solution)/shard_map/ppermute | solution.py:238
  14.5 0.6 %collective-permute-done.2.near_ref = f32[1,4,128,128]{3,2,1,0:T(8,128)S(1)} collective-permute-done((f32[1,4,128,128]{3,2,1,0:T(8,128)S(1)}, f32[1,4,128,128]{3,2,1,0:T(8,128)S(1)}, u32[]{:S(2)}, u32[]{:S(2)}) %collective-permute-start.2) | collective-permute-done | bytes 262176 | tf_op jit(solution)/shard_map/ppermute | solution.py:238
  15.0 0.3 shard_map.126
  15.3 0.3 collective-permute-start.3
  15.6 3.4 %collective-permute-done.3 = f32[4,128]{1,0:T(4,128)S(1)} collective-permute-done((f32[4,128]{1,0:T(4,128)S(1)}, f32[4,128]{1,0:T(4,128)S(1)}, u32[]{:S(2)}, u32[]{:S(2)}) %collective-permute-start.3) | collective-permute-done | bytes 2080 | tf_op jit(solution)/shard_map/ppermute | solution.py:242
  18.9 3.3 %collective-permute-start.4 = (f32[4,128]{1,0:T(4,128)S(1)}, f32[4,128]{1,0:T(4,128)S(1)}, u32[]{:S(2)}, u32[]{:S(2)}) collective-permute-start(f32[4,128]{1,0:T(4,128)S(1)} %add.6), channel_id=1, source_target_pairs={{0,2},{1,3},{2,0},{3,1},{4,6},{5,7},{6,4},{7,5},{8,10},{9,11},{10,... | collective-permute-start | bytes 6152 | tf_op jit(solution)/shard_map/ppermute | solution.py:242
  22.2 1.6 %collective-permute-done.4 = f32[4,128]{1,0:T(4,128)S(1)} collective-permute-done((f32[4,128]{1,0:T(4,128)S(1)}, f32[4,128]{1,0:T(4,128)S(1)}, u32[]{:S(2)}, u32[]{:S(2)}) %collective-permute-start.4) | collective-permute-done | bytes 2080 | tf_op jit(solution)/shard_map/ppermute | solution.py:242
  23.8 5.1 %collective-permute-start.5 = (f32[4,128]{1,0:T(4,128)S(1)}, f32[4,128]{1,0:T(4,128)S(1)}, u32[]{:S(2)}, u32[]{:S(2)}) collective-permute-start(f32[4,128]{1,0:T(4,128)S(1)} %add.7.square_a_ref), channel_id=1, source_target_pairs={{0,6},{1,7},{2,4},{3,5},{4,2},{5,3},{6,0},{7,1},{8,14},{9,15},{10,... | collective-permute-start | bytes 6152 | tf_op jit(solution)/shard_map/ppermute | solution.py:242
  28.8 1.6 %shard_map.127 = (f32[8,4,128,128]{3,2,1,0:T(8,128)}, f32[3,4,128,128]{3,2,1,0:T(8,128)S(1)}) custom-call(s32[25]{0:T(128)S(4)} %get-tuple-element.17.info_ref, f32[4,512]{1,0:T(4,128)S(1)} %get-tuple-element.18.fade_ref, f32[4,512]{1,0:T(4,128)S(1)} %get-tuple-element.28.back_ref, bf16[8,4,512]{2,1,0:T(4,128)(2,1)S(1)} %copy-done.1, ...), custom_call_target="tpu_custom_call" | custom-call | flops 1000000 | bytes 1000000 | tf_op jit(solution)/shard_map/pallas_call | solution.py:222
  30.5 0.0 collective-permute-done.5.square_b_ref
  30.5 0.0 collective-permute-done.6.far_ref
  30.5 1.0 %shard_map.128 = (bf16[8,4,512]{2,1,0:T(4,128)(2,1)}, f32[8,4,128,128]{3,2,1,0:T(8,128)}) custom-call(s32[25]{0:T(128)S(4)} %get-tuple-element.17.info_ref, f32[8,4,512]{2,1,0:T(4,128)S(1)} %get-tuple-element.21.gate_ref, f32[8,4,512]{2,1,0:T(4,128)S(1)} %get-tuple-element.26.out_ref, ...), custom_call_target="tpu_custom_call", output_to_operand_aliasing={{1}: (9, {})} | custom-call | flops 100000 | bytes 100000 | tf_op jit(solution)/shard_map/pallas_call | solution.py:222
  (2 shorter events, 0.0 us)
Async XLA Ops:
  0.6 4.4 %copy-start = (f32[8,4,128,128]{3,2,1,0:T(8,128)S(1)}, f32[8,4,128,128]{3,2,1,0:T(8,128)}, u32[]{:S(2)}) copy-start(f32[8,4,128,128]{3,2,1,0:T(8,128)} %states_ref.5) | copy-start | bytes 6291460
  1.7 5.3 %collective-permute-start = (f32[2,4,512]{2,1,0:T(4,128)S(1)}, f32[2,4,512]{2,1,0:T(4,128)S(1)}, u32[]{:S(2)}, u32[]{:S(2)}) collective-permute-start(f32[2,4,512]{2,1,0:T(4,128)S(1)} %get-tuple-element.19), channel_id=1, source_target_pairs={{0,128},{8,136},{16,144},{24,152},{32,160},{40,168},{48,176},{56,1... | collective-permute-start | bytes 49160 | tf_op jit(solution)/shard_map/ppermute | solution.py:238
  5.0 5.6 %copy-start.1 = (bf16[8,4,512]{2,1,0:T(4,128)(2,1)S(1)}, bf16[8,4,512]{2,1,0:T(4,128)(2,1)}, u32[]{:S(2)}) copy-start(bf16[8,4,512]{2,1,0:T(4,128)(2,1)} %key_ref.3) | copy-start | bytes 98308
  5.0 5.6 %copy-start.2 = (bf16[8,4,512]{2,1,0:T(4,128)(2,1)S(1)}, bf16[8,4,512]{2,1,0:T(4,128)(2,1)}, u32[]{:S(2)}) copy-start(bf16[8,4,512]{2,1,0:T(4,128)(2,1)} %value_ref.3) | copy-start | bytes 98308
  5.0 5.6 %copy-start.3 = (bf16[8,4,512]{2,1,0:T(4,128)(2,1)S(1)}, bf16[8,4,512]{2,1,0:T(4,128)(2,1)}, u32[]{:S(2)}) copy-start(bf16[8,4,512]{2,1,0:T(4,128)(2,1)} %query_ref.3) | copy-start | bytes 98308
  5.0 5.6 %copy-start.4 = (bf16[8,4,512]{2,1,0:T(4,128)(2,1)S(1)}, bf16[8,4,512]{2,1,0:T(4,128)(2,1)}, u32[]{:S(2)}) copy-start(bf16[8,4,512]{2,1,0:T(4,128)(2,1)} %gate_ref.1) | copy-start | bytes 98308
  5.0 5.6 %copy-start.5 = (f32[512]{0:T(512)S(1)}, f32[512]{0:T(512)}, u32[]{:S(2)}) copy-start(f32[512]{0:T(512)} %param.21) | copy-start | bytes 6148
  5.1 9.9 %collective-permute-start.2 = (f32[1,4,128,128]{3,2,1,0:T(8,128)S(1)}, f32[1,4,128,128]{3,2,1,0:T(8,128)S(1)}, u32[]{:S(2)}, u32[]{:S(2)}) collective-permute-start(f32[1,4,128,128]{3,2,1,0:T(8,128)S(1)} %get-tuple-element.22), channel_id=1, source_target_pairs={{0,8},{8,16},{16,24},{24,32},{32,40},{40,48},{48,56},{56,64},{64,7... | collective-permute-start | bytes 786440 | tf_op jit(solution)/shard_map/ppermute | solution.py:238
  7.3 7.2 %collective-permute-start.1 = (f32[2,4,512]{2,1,0:T(4,128)S(1)}, f32[2,4,512]{2,1,0:T(4,128)S(1)}, u32[]{:S(2)}, u32[]{:S(2)}) collective-permute-start(f32[2,4,512]{2,1,0:T(4,128)S(1)} %shard_map.124.answer_ref), channel_id=1, source_target_pairs={{0,128},{8,136},{16,144},{24,152},{32,160},{40,168},{48,176},{56,1... | collective-permute-start | bytes 49160 | tf_op jit(solution)/shard_map/ppermute | solution.py:238
  11.3 19.2 %collective-permute-start.6 = (f32[2,4,128,128]{3,2,1,0:T(8,128)S(1)}, f32[2,4,128,128]{3,2,1,0:T(8,128)S(1)}, u32[]{:S(2)}, u32[]{:S(2)}) collective-permute-start(f32[2,4,128,128]{3,2,1,0:T(8,128)S(1)} %get-tuple-element.30), channel_id=1, source_target_pairs={{0,128},{8,136},{16,144},{24,152},{32,160},{40,168},{48,176},{56,1... | collective-permute-start | bytes 1572872 | tf_op jit(solution)/shard_map/ppermute | solution.py:238
  15.3 3.6 %collective-permute-start.3 = (f32[4,128]{1,0:T(4,128)S(1)}, f32[4,128]{1,0:T(4,128)S(1)}, u32[]{:S(2)}, u32[]{:S(2)}) collective-permute-start(f32[4,128]{1,0:T(4,128)S(1)} %get-tuple-element.27.square_ref), channel_id=1, source_target_pairs={{0,1},{1,0},{2,3},{3,2},{4,5},{5,4},{6,7},{7,6},{8,9},{9,8},{10,11... | collective-permute-start | bytes 6152 | tf_op jit(solution)/shard_map/ppermute | solution.py:242
  18.9 4.8 %collective-permute-start.4 = (f32[4,128]{1,0:T(4,128)S(1)}, f32[4,128]{1,0:T(4,128)S(1)}, u32[]{:S(2)}, u32[]{:S(2)}) collective-permute-start(f32[4,128]{1,0:T(4,128)S(1)} %add.6), channel_id=1, source_target_pairs={{0,2},{1,3},{2,0},{3,1},{4,6},{5,7},{6,4},{7,5},{8,10},{9,11},{10,... | collective-permute-start | bytes 6152 | tf_op jit(solution)/shard_map/ppermute | solution.py:242
  23.8 6.7 %collective-permute-start.5 = (f32[4,128]{1,0:T(4,128)S(1)}, f32[4,128]{1,0:T(4,128)S(1)}, u32[]{:S(2)}, u32[]{:S(2)}) collective-permute-start(f32[4,128]{1,0:T(4,128)S(1)} %add.7.square_a_ref), channel_id=1, source_target_pairs={{0,6},{1,7},{2,4},{3,5},{4,2},{5,3},{6,0},{7,1},{8,14},{9,15},{10,... | collective-permute-start | bytes 6152 | tf_op jit(solution)/shard_map/ppermute | solution.py:242

commit v5 on v4

--- a/solution.py
+++ b/solution.py
@@ -186,6 +186,11 @@
             total += row * row
         squares = jnp.where(lanes == slot, jnp.sum(total, axis=1, keepdims=True), squares)
     square_ref[...] = squares
+
+
+def add_kernel(a_ref, b_ref, added_ref, out_ref):
+    del added_ref
+    out_ref[...] = a_ref[...] + b_ref[...]
 
 
 def final_kernel(
@@ -270,7 +275,7 @@
         (info, fade, back, key_proj, value_proj, states, square), out_specs=(HBM, VMEM),
         scratch_shapes=[pltpu.VMEM((SLOTS_DEV, *row), jnp.float32), pltpu.SemaphoreType.DMA((SLOTS_DEV,))], cost=1_000_000)
     square = square + over_head(square, 1)
-    square = square + over_head(square, 2)
+    square = call(add_kernel, vmem(STEPS, DK), [VMEM, VMEM, ANY], (square, over_head(square, 2), added), out_specs=VMEM)
     other = over_head(square, 6)
     return call(
         final_kernel, (jax.ShapeDtypeStruct(features, jnp.bfloat16), jax.ShapeDtypeStruct((SLOTS_DEV, *row), jnp.float32)),

time: 31.5 us -> 31.4 us (level)
    pallas_call x7 -> x8, Pallas kernels: 4.93 us -> 4.92 us  [call(): pl.pallas_call(kernel, out_shape=outs, in_specs=in_specs, compiler_params...]
where the time goes in v5:
time: 31.4 us; the launch traced here: 31.3 us
  starting transfers between devices  15.6 us (50%)
  waiting for transfers between devices  10.1 us (32%)
  Pallas kernels  4.92 us (16%)
  between operations  0.73 us (2%)
    ppermute x3, starting transfers between devices, over_head(): return lax.ppermute(x, 'head', [(i, i ^ flip) for i in range(N_HEAD)])  8.52 us
    ppermute x4, starting transfers between devices, over_rep(): lax.ppermute(x, 'rep', [(i, (i + distance) % N_REP) for i in range(N_REP)])  7.05 us
    ppermute x4, waiting for transfers between devices, over_rep(): lax.ppermute(x, 'rep', [(i, (i + distance) % N_REP) for i in range(N_REP)])  5.18 us
    pallas_call x8, Pallas kernels, call(): pl.pallas_call(kernel, out_shape=outs, in_specs=in_specs, compiler_params...  4.92 us
    ppermute x3, waiting for transfers between devices, over_head(): return lax.ppermute(x, 'head', [(i, i ^ flip) for i in range(N_HEAD)])  4.91 us
  transfers between devices with their start and end apart: 7, of which 5 were waited for; matrix products, arithmetic and copies ran while one was open for 0% of the time, Pallas kernels for 9%

profile of v5, /device:TPU:32, one launch (start us, length us, event | category | flops | bytes accessed | tf_op | source)
XLA Modules:
  0.0 31.3 jit_solution(4458450186016489483)
XLA Ops:
  0.6 0.0 copy-start
  0.6 1.1 %shard_map.122 = (f32[2,4,512]{2,1,0:T(4,128)S(1)}, f32[4,512]{1,0:T(4,128)S(1)}, f32[4,512]{1,0:T(4,128)S(1)}, f32[4,512]{1,0:T(4,128)S(1)}, s32[25]{0:T(128)S(4)}) custom-call(s32[8]{0:T(128)} %alive_ref.1, s32[3,32]{1,0:T(4,128)} %bitcast.4, s32[3,32]{1,0:T(4,128)} %bitcast.5, s32[32]{0:T(128)} %count_ref.1, f32[4]{0:T(128)} %rate_ref.1, ...), custom_call_target="tpu_custom_call" | custom-call | flops 10000000000 | bytes 10000000000 | tf_op jit(solution)/shard_map/pallas_call | solution.py:227
  1.7 3.3 %collective-permute-start = (f32[2,4,512]{2,1,0:T(4,128)S(1)}, f32[2,4,512]{2,1,0:T(4,128)S(1)}, u32[]{:S(2)}, u32[]{:S(2)}) collective-permute-start(f32[2,4,512]{2,1,0:T(4,128)S(1)} %get-tuple-element.19), channel_id=1, source_target_pairs={{0,128},{8,136},{16,144},{24,152},{32,160},{40,168},{48,176},{56,1... | collective-permute-start | bytes 49160 | tf_op jit(solution)/shard_map/ppermute | solution.py:243
  5.0 0.0 copy-done
  5.0 0.0 copy-start.1
  5.0 0.0 copy-start.2
  5.0 0.0 copy-start.3
  5.0 0.0 copy-start.4
  5.0 0.0 copy-start.5
  5.0 0.1 shard_map.123
  5.1 0.1 collective-permute-start.2
  5.2 1.8 %collective-permute-done.query_ref = f32[2,4,512]{2,1,0:T(4,128)S(1)} collective-permute-done((f32[2,4,512]{2,1,0:T(4,128)S(1)}, f32[2,4,512]{2,1,0:T(4,128)S(1)}, u32[]{:S(2)}, u32[]{:S(2)}) %collective-permute-start) | collective-permute-done | bytes 16416 | tf_op jit(solution)/shard_map/ppermute | solution.py:243
  7.0 0.2 shard_map.124.answer_ref
  7.3 3.3 %collective-permute-start.1 = (f32[2,4,512]{2,1,0:T(4,128)S(1)}, f32[2,4,512]{2,1,0:T(4,128)S(1)}, u32[]{:S(2)}, u32[]{:S(2)}) collective-permute-start(f32[2,4,512]{2,1,0:T(4,128)S(1)} %shard_map.124.answer_ref), channel_id=1, source_target_pairs={{0,128},{8,136},{16,144},{24,152},{32,160},{40,168},{48,176},{56,1... | collective-permute-start | bytes 49160 | tf_op jit(solution)/shard_map/ppermute | solution.py:243
  10.5 0.0 copy-done.1
  10.6 0.0 copy-done.2
  10.6 0.0 copy-done.3
  10.6 0.0 copy-done.4
  10.6 0.0 copy-done.5
  10.6 0.7 %shard_map.125 = (f32[8,4,512]{2,1,0:T(4,128)S(1)}, f32[3,8,4,128]{3,2,1,0:T(4,128)S(1)}, f32[8,4,512]{2,1,0:T(4,128)S(1)}, f32[2,4,128,128]{3,2,1,0:T(8,128)S(1)}) custom-call(s32[25]{0:T(128)S(4)} %get-tuple-element.17.info_ref, f32[4,512]{1,0:T(4,128)S(1)} %get-tuple-element.18.fade_ref, ...), custom_call_target="tpu_custom_call", output_to_operand_aliasing={{3}: (9, {})} | custom-call | flops 10000000000 | bytes 10000000000 | tf_op jit(solution)/shard_map/pallas_call | solution.py:227
  11.2 0.4 %collective-permute-start.6 = (f32[2,4,128,128]{3,2,1,0:T(8,128)S(1)}, f32[2,4,128,128]{3,2,1,0:T(8,128)S(1)}, u32[]{:S(2)}, u32[]{:S(2)}) collective-permute-start(f32[2,4,128,128]{3,2,1,0:T(8,128)S(1)} %get-tuple-element.30), channel_id=1, source_target_pairs={{0,128},{8,136},{16,144},{24,152},{32,160},{40,168},{48,176},{56,1... | collective-permute-start | bytes 1572872 | tf_op jit(solution)/shard_map/ppermute | solution.py:243
  11.7 2.8 %collective-permute-done.1.answer_ref = f32[2,4,512]{2,1,0:T(4,128)S(1)} collective-permute-done((f32[2,4,512]{2,1,0:T(4,128)S(1)}, f32[2,4,512]{2,1,0:T(4,128)S(1)}, u32[]{:S(2)}, u32[]{:S(2)}) %collective-permute-start.1) | collective-permute-done | bytes 16416 | tf_op jit(solution)/shard_map/ppermute | solution.py:243
  14.5 0.6 %collective-permute-done.2.near_ref = f32[1,4,128,128]{3,2,1,0:T(8,128)S(1)} collective-permute-done((f32[1,4,128,128]{3,2,1,0:T(8,128)S(1)}, f32[1,4,128,128]{3,2,1,0:T(8,128)S(1)}, u32[]{:S(2)}, u32[]{:S(2)}) %collective-permute-start.2) | collective-permute-done | bytes 262176 | tf_op jit(solution)/shard_map/ppermute | solution.py:243
  15.0 0.3 shard_map.126
  15.3 0.3 collective-permute-start.3
  15.6 3.3 %collective-permute-done.3 = f32[4,128]{1,0:T(4,128)S(1)} collective-permute-done((f32[4,128]{1,0:T(4,128)S(1)}, f32[4,128]{1,0:T(4,128)S(1)}, u32[]{:S(2)}, u32[]{:S(2)}) %collective-permute-start.3) | collective-permute-done | bytes 2080 | tf_op jit(solution)/shard_map/ppermute | solution.py:247
  18.9 3.3 %collective-permute-start.4 = (f32[4,128]{1,0:T(4,128)S(1)}, f32[4,128]{1,0:T(4,128)S(1)}, u32[]{:S(2)}, u32[]{:S(2)}) collective-permute-start(f32[4,128]{1,0:T(4,128)S(1)} %add.3.a_ref), channel_id=1, source_target_pairs={{0,2},{1,3},{2,0},{3,1},{4,6},{5,7},{6,4},{7,5},{8,10},{9,11},{10,... | collective-permute-start | bytes 6152 | tf_op jit(solution)/shard_map/ppermute | solution.py:247
  22.2 1.6 %shard_map.127 = (f32[8,4,128,128]{3,2,1,0:T(8,128)}, f32[3,4,128,128]{3,2,1,0:T(8,128)S(1)}) custom-call(s32[25]{0:T(128)S(4)} %get-tuple-element.17.info_ref, f32[4,512]{1,0:T(4,128)S(1)} %get-tuple-element.18.fade_ref, f32[4,512]{1,0:T(4,128)S(1)} %get-tuple-element.28.back_ref, bf16[8,4,512]{2,1,0:T(4,128)(2,1)S(1)} %copy-done.1, ...), custom_call_target="tpu_custom_call" | custom-call | flops 1000000 | bytes 1000000 | tf_op jit(solution)/shard_map/pallas_call | solution.py:227
  23.8 0.0 collective-permute-done.4.b_ref
  23.9 5.0 %collective-permute-start.5 = (f32[4,128]{1,0:T(4,128)S(1)}, f32[4,128]{1,0:T(4,128)S(1)}, u32[]{:S(2)}, u32[]{:S(2)}) collective-permute-start(f32[4,128]{1,0:T(4,128)S(1)} %shard_map.128.square_a_ref), channel_id=1, source_target_pairs={{0,6},{1,7},{2,4},{3,5},{4,2},{5,3},{6,0},{7,1},{8,14},{9,15},{10,... | collective-permute-start | bytes 6152 | tf_op jit(solution)/shard_map/ppermute | solution.py:247
  28.8 1.6 %collective-permute-done.5.square_b_ref = f32[4,128]{1,0:T(4,128)S(1)} collective-permute-done((f32[4,128]{1,0:T(4,128)S(1)}, f32[4,128]{1,0:T(4,128)S(1)}, u32[]{:S(2)}, u32[]{:S(2)}) %collective-permute-start.5) | collective-permute-done | bytes 2080 | tf_op jit(solution)/shard_map/ppermute | solution.py:247
  30.4 0.0 collective-permute-done.6.far_ref
  30.4 0.9 %shard_map.129 = (bf16[8,4,512]{2,1,0:T(4,128)(2,1)}, f32[8,4,128,128]{3,2,1,0:T(8,128)}) custom-call(s32[25]{0:T(128)S(4)} %get-tuple-element.17.info_ref, f32[8,4,512]{2,1,0:T(4,128)S(1)} %get-tuple-element.21.gate_ref, f32[8,4,512]{2,1,0:T(4,128)S(1)} %get-tuple-element.26.out_ref, ...), custom_call_target="tpu_custom_call", output_to_operand_aliasing={{1}: (9, {})} | custom-call | flops 100000 | bytes 100000 | tf_op jit(solution)/shard_map/pallas_call | solution.py:227
  (2 shorter events, 0.0 us)
Async XLA Ops:
  0.6 4.4 %copy-start = (f32[8,4,128,128]{3,2,1,0:T(8,128)S(1)}, f32[8,4,128,128]{3,2,1,0:T(8,128)}, u32[]{:S(2)}) copy-start(f32[8,4,128,128]{3,2,1,0:T(8,128)} %states_ref.5) | copy-start | bytes 6291460
  1.7 5.3 %collective-permute-start = (f32[2,4,512]{2,1,0:T(4,128)S(1)}, f32[2,4,512]{2,1,0:T(4,128)S(1)}, u32[]{:S(2)}, u32[]{:S(2)}) collective-permute-start(f32[2,4,512]{2,1,0:T(4,128)S(1)} %get-tuple-element.19), channel_id=1, source_target_pairs={{0,128},{8,136},{16,144},{24,152},{32,160},{40,168},{48,176},{56,1... | collective-permute-start | bytes 49160 | tf_op jit(solution)/shard_map/ppermute | solution.py:243
  5.0 5.6 %copy-start.1 = (bf16[8,4,512]{2,1,0:T(4,128)(2,1)S(1)}, bf16[8,4,512]{2,1,0:T(4,128)(2,1)}, u32[]{:S(2)}) copy-start(bf16[8,4,512]{2,1,0:T(4,128)(2,1)} %key_ref.3) | copy-start | bytes 98308
  5.0 5.6 %copy-start.2 = (bf16[8,4,512]{2,1,0:T(4,128)(2,1)S(1)}, bf16[8,4,512]{2,1,0:T(4,128)(2,1)}, u32[]{:S(2)}) copy-start(bf16[8,4,512]{2,1,0:T(4,128)(2,1)} %value_ref.3) | copy-start | bytes 98308
  5.0 5.6 %copy-start.3 = (bf16[8,4,512]{2,1,0:T(4,128)(2,1)S(1)}, bf16[8,4,512]{2,1,0:T(4,128)(2,1)}, u32[]{:S(2)}) copy-start(bf16[8,4,512]{2,1,0:T(4,128)(2,1)} %query_ref.3) | copy-start | bytes 98308
  5.0 5.6 %copy-start.4 = (bf16[8,4,512]{2,1,0:T(4,128)(2,1)S(1)}, bf16[8,4,512]{2,1,0:T(4,128)(2,1)}, u32[]{:S(2)}) copy-start(bf16[8,4,512]{2,1,0:T(4,128)(2,1)} %gate_ref.1) | copy-start | bytes 98308
  5.0 5.6 %copy-start.5 = (f32[512]{0:T(512)S(1)}, f32[512]{0:T(512)}, u32[]{:S(2)}) copy-start(f32[512]{0:T(512)} %param.21) | copy-start | bytes 6148
  5.1 9.9 %collective-permute-start.2 = (f32[1,4,128,128]{3,2,1,0:T(8,128)S(1)}, f32[1,4,128,128]{3,2,1,0:T(8,128)S(1)}, u32[]{:S(2)}, u32[]{:S(2)}) collective-permute-start(f32[1,4,128,128]{3,2,1,0:T(8,128)S(1)} %get-tuple-element.22), channel_id=1, source_target_pairs={{0,8},{8,16},{16,24},{24,32},{32,40},{40,48},{48,56},{56,64},{64,7... | collective-permute-start | bytes 786440 | tf_op jit(solution)/shard_map/ppermute | solution.py:243
  7.3 7.2 %collective-permute-start.1 = (f32[2,4,512]{2,1,0:T(4,128)S(1)}, f32[2,4,512]{2,1,0:T(4,128)S(1)}, u32[]{:S(2)}, u32[]{:S(2)}) collective-permute-start(f32[2,4,512]{2,1,0:T(4,128)S(1)} %shard_map.124.answer_ref), channel_id=1, source_target_pairs={{0,128},{8,136},{16,144},{24,152},{32,160},{40,168},{48,176},{56,1... | collective-permute-start | bytes 49160 | tf_op jit(solution)/shard_map/ppermute | solution.py:243
  11.2 19.1 %collective-permute-start.6 = (f32[2,4,128,128]{3,2,1,0:T(8,128)S(1)}, f32[2,4,128,128]{3,2,1,0:T(8,128)S(1)}, u32[]{:S(2)}, u32[]{:S(2)}) collective-permute-start(f32[2,4,128,128]{3,2,1,0:T(8,128)S(1)} %get-tuple-element.30), channel_id=1, source_target_pairs={{0,128},{8,136},{16,144},{24,152},{32,160},{40,168},{48,176},{56,1... | collective-permute-start | bytes 1572872 | tf_op jit(solution)/shard_map/ppermute | solution.py:243
  15.3 3.6 %collective-permute-start.3 = (f32[4,128]{1,0:T(4,128)S(1)}, f32[4,128]{1,0:T(4,128)S(1)}, u32[]{:S(2)}, u32[]{:S(2)}) collective-permute-start(f32[4,128]{1,0:T(4,128)S(1)} %get-tuple-element.27.square_ref), channel_id=1, source_target_pairs={{0,1},{1,0},{2,3},{3,2},{4,5},{5,4},{6,7},{7,6},{8,9},{9,8},{10,11... | collective-permute-start | bytes 6152 | tf_op jit(solution)/shard_map/ppermute | solution.py:247
  18.9 4.9 %collective-permute-start.4 = (f32[4,128]{1,0:T(4,128)S(1)}, f32[4,128]{1,0:T(4,128)S(1)}, u32[]{:S(2)}, u32[]{:S(2)}) collective-permute-start(f32[4,128]{1,0:T(4,128)S(1)} %add.3.a_ref), channel_id=1, source_target_pairs={{0,2},{1,3},{2,0},{3,1},{4,6},{5,7},{6,4},{7,5},{8,10},{9,11},{10,... | collective-permute-start | bytes 6152 | tf_op jit(solution)/shard_map/ppermute | solution.py:247
  23.9 6.5 %collective-permute-start.5 = (f32[4,128]{1,0:T(4,128)S(1)}, f32[4,128]{1,0:T(4,128)S(1)}, u32[]{:S(2)}, u32[]{:S(2)}) collective-permute-start(f32[4,128]{1,0:T(4,128)S(1)} %shard_map.128.square_a_ref), channel_id=1, source_target_pairs={{0,6},{1,7},{2,4},{3,5},{4,2},{5,3},{6,0},{7,1},{8,14},{9,15},{10,... | collective-permute-start | bytes 6152 | tf_op jit(solution)/shard_map/ppermute | solution.py:247

commit v6 on v5

--- a/solution.py
+++ b/solution.py
@@ -193,10 +193,7 @@
     out_ref[...] = a_ref[...] + b_ref[...]
 
 
-def final_kernel(
-    info_ref, gate_ref, out_ref, square_a_ref, square_b_ref, fade_ref, added_ref, far_ref, near_ref, old_ref,
-    attended_hbm, new_ref, attended_ref, rows_ref, sems,
-):
+def update_kernel(info_ref, fade_ref, added_ref, far_ref, near_ref, old_ref, new_ref, rows_ref, sems):
     del old_ref
     copies = []
     for move in range(MOVE):
@@ -211,16 +208,17 @@
         def _(copy=copy):
             copy.start()
 
-    scales = lax.rsqrt((square_a_ref[...] + square_b_ref[...]) * (1.0 / (HEADS * DK)) + epsilon)
-    for slot in range(SLOTS_DEV):
-        attended_ref[slot] = (out_ref[slot] * gate_ref[slot] * scales[:, slot:slot + 1]).astype(jnp.bfloat16)
-    out_copy = pltpu.make_async_copy(attended_ref, attended_hbm, sems.at[MOVE])
-    out_copy.start()
-    out_copy.wait()
     for valid, copy in copies:
         @pl.when(valid)
         def _(copy=copy):
             copy.wait()
+
+
+def final_kernel(gate_ref, out_ref, square_a_ref, square_b_ref, new_ref, attended_ref):
+    del new_ref
+    scales = lax.rsqrt((square_a_ref[...] + square_b_ref[...]) * (1.0 / (HEADS * DK)) + epsilon)
+    for slot in range(SLOTS_DEV):
+        attended_ref[slot] = (out_ref[slot] * gate_ref[slot] * scales[:, slot:slot + 1]).astype(jnp.bfloat16)
 
 
 def call(kernel, outs, in_specs, args, cost=100_000, limit=8, **more):
@@ -277,12 +275,14 @@
     square = square + over_head(square, 1)
     square = call(add_kernel, vmem(STEPS, DK), [VMEM, VMEM, ANY], (square, over_head(square, 2), added), out_specs=VMEM)
     other = over_head(square, 6)
-    return call(
-        final_kernel, (jax.ShapeDtypeStruct(features, jnp.bfloat16), jax.ShapeDtypeStruct((SLOTS_DEV, *row), jnp.float32)),
-        [SMEM] + [VMEM] * 8 + [ANY], (info, gate, out, square, other, fade, added, far, near, new_states),
-        out_specs=(ANY, ANY), input_output_aliases={9: 1},
-        scratch_shapes=[
-            pltpu.VMEM(features, jnp.bfloat16), pltpu.VMEM((MOVE, *row), jnp.float32), pltpu.SemaphoreType.DMA((MOVE + 1,))])
+    new_states = call(
+        update_kernel, jax.ShapeDtypeStruct((SLOTS_DEV, *row), jnp.float32), [SMEM] + [VMEM] * 4 + [ANY],
+        (info, fade, added, far, near, new_states), out_specs=ANY, input_output_aliases={5: 0},
+        scratch_shapes=[pltpu.VMEM((MOVE, *row), jnp.float32), pltpu.SemaphoreType.DMA((MOVE,))], cost=100_000)
+    attended = call(
+        final_kernel, jax.ShapeDtypeStruct(features, jnp.bfloat16), [VMEM] * 4 + [HBM], (gate, out, square, other, *in_hbm(new_states)),
+        out_specs=VMEM)
+    return attended, new_states
 
 
 def solution(mesh):

time: 31.4 us -> 31.2 us (level)
  waiting for transfers between devices: 10.1 us -> 9.15 us
  Pallas kernels: 4.92 us -> 5.61 us
    ppermute x3, waiting for transfers between devices: 4.91 us -> 3.97 us  [over_head(): return lax.ppermute(x, 'head', [(i, i ^ flip) for i in range(N_HEAD)])]
    pallas_call x8 -> x9, Pallas kernels: 4.92 us -> 5.61 us  [call(): pl.pallas_call(kernel, out_shape=outs, in_specs=in_specs, compiler_params...]
  transfers between devices with their start and end apart: 7 -> 7, of which waited for: 5 -> 5; matrix products, arithmetic and copies ran while one was open for 0% -> 0% of each run, Pallas kernels for 9% -> 12%
where the time goes in v6:
time: 31.2 us; the launch traced here: 31.1 us
  starting transfers between devices  15.6 us (50%)
  waiting for transfers between devices  9.15 us (29%)
  Pallas kernels  5.61 us (18%)
  between operations  0.74 us (2%)
    ppermute x3, starting transfers between devices, over_head(): return lax.ppermute(x, 'head', [(i, i ^ flip) for i in range(N_HEAD)])  8.52 us
    ppermute x4, starting transfers between devices, over_rep(): lax.ppermute(x, 'rep', [(i, (i + distance) % N_REP) for i in range(N_REP)])  7.05 us
    pallas_call x9, Pallas kernels, call(): pl.pallas_call(kernel, out_shape=outs, in_specs=in_specs, compiler_params...  5.61 us
    ppermute x4, waiting for transfers between devices, over_rep(): lax.ppermute(x, 'rep', [(i, (i + distance) % N_REP) for i in range(N_REP)])  5.18 us
    ppermute x3, waiting for transfers between devices, over_head(): return lax.ppermute(x, 'head', [(i, i ^ flip) for i in range(N_HEAD)])  3.97 us
  transfers between devices with their start and end apart: 7, of which 5 were waited for; matrix products, arithmetic and copies ran while one was open for 0% of the time, Pallas kernels for 12%

profile of v6, /device:TPU:32, one launch (start us, length us, event | category | flops | bytes accessed | tf_op | source)
XLA Modules:
  0.0 31.1 jit_solution(14805229904886117194)
XLA Ops:
  0.6 0.0 copy-start
  0.6 1.1 %shard_map.122 = (f32[2,4,512]{2,1,0:T(4,128)S(1)}, f32[4,512]{1,0:T(4,128)S(1)}, f32[4,512]{1,0:T(4,128)S(1)}, f32[4,512]{1,0:T(4,128)S(1)}, s32[25]{0:T(128)S(4)}) custom-call(s32[8]{0:T(128)} %alive_ref.1, s32[3,32]{1,0:T(4,128)} %bitcast.4, s32[3,32]{1,0:T(4,128)} %bitcast.5, s32[32]{0:T(128)} %count_ref.1, f32[4]{0:T(128)} %rate_ref.1, ...), custom_call_target="tpu_custom_call" | custom-call | flops 10000000000 | bytes 10000000000 | tf_op jit(solution)/shard_map/pallas_call | solution.py:225
  1.7 3.3 %collective-permute-start = (f32[2,4,512]{2,1,0:T(4,128)S(1)}, f32[2,4,512]{2,1,0:T(4,128)S(1)}, u32[]{:S(2)}, u32[]{:S(2)}) collective-permute-start(f32[2,4,512]{2,1,0:T(4,128)S(1)} %get-tuple-element.19), channel_id=1, source_target_pairs={{0,128},{8,136},{16,144},{24,152},{32,160},{40,168},{48,176},{56,1... | collective-permute-start | bytes 49160 | tf_op jit(solution)/shard_map/ppermute | solution.py:241
  5.0 0.0 copy-done
  5.0 0.0 copy-start.1
  5.0 0.0 copy-start.2
  5.0 0.0 copy-start.3
  5.0 0.0 copy-start.4
  5.0 0.0 copy-start.5
  5.0 0.1 shard_map.123
  5.1 0.1 collective-permute-start.2
  5.2 1.8 %collective-permute-done.query_ref = f32[2,4,512]{2,1,0:T(4,128)S(1)} collective-permute-done((f32[2,4,512]{2,1,0:T(4,128)S(1)}, f32[2,4,512]{2,1,0:T(4,128)S(1)}, u32[]{:S(2)}, u32[]{:S(2)}) %collective-permute-start) | collective-permute-done | bytes 16416 | tf_op jit(solution)/shard_map/ppermute | solution.py:241
  7.0 0.2 shard_map.124.answer_ref
  7.3 3.3 %collective-permute-start.1 = (f32[2,4,512]{2,1,0:T(4,128)S(1)}, f32[2,4,512]{2,1,0:T(4,128)S(1)}, u32[]{:S(2)}, u32[]{:S(2)}) collective-permute-start(f32[2,4,512]{2,1,0:T(4,128)S(1)} %shard_map.124.answer_ref), channel_id=1, source_target_pairs={{0,128},{8,136},{16,144},{24,152},{32,160},{40,168},{48,176},{56,1... | collective-permute-start | bytes 49160 | tf_op jit(solution)/shard_map/ppermute | solution.py:241
  10.5 0.0 copy-done.1
  10.6 0.0 copy-done.2
  10.6 0.0 copy-done.3
  10.6 0.0 copy-done.4
  10.6 0.0 copy-done.5
  10.6 0.7 %shard_map.125 = (f32[8,4,512]{2,1,0:T(4,128)S(1)}, f32[3,8,4,128]{3,2,1,0:T(4,128)S(1)}, f32[8,4,512]{2,1,0:T(4,128)S(1)}, f32[2,4,128,128]{3,2,1,0:T(8,128)S(1)}) custom-call(s32[25]{0:T(128)S(4)} %get-tuple-element.17.info_ref, f32[4,512]{1,0:T(4,128)S(1)} %get-tuple-element.18.fade_ref, ...), custom_call_target="tpu_custom_call", output_to_operand_aliasing={{3}: (9, {})} | custom-call | flops 10000000000 | bytes 10000000000 | tf_op jit(solution)/shard_map/pallas_call | solution.py:225
  11.2 0.4 %collective-permute-start.6 = (f32[2,4,128,128]{3,2,1,0:T(8,128)S(1)}, f32[2,4,128,128]{3,2,1,0:T(8,128)S(1)}, u32[]{:S(2)}, u32[]{:S(2)}) collective-permute-start(f32[2,4,128,128]{3,2,1,0:T(8,128)S(1)} %get-tuple-element.30), channel_id=1, source_target_pairs={{0,128},{8,136},{16,144},{24,152},{32,160},{40,168},{48,176},{56,1... | collective-permute-start | bytes 1572872 | tf_op jit(solution)/shard_map/ppermute | solution.py:241
  11.7 2.8 %collective-permute-done.1.answer_ref = f32[2,4,512]{2,1,0:T(4,128)S(1)} collective-permute-done((f32[2,4,512]{2,1,0:T(4,128)S(1)}, f32[2,4,512]{2,1,0:T(4,128)S(1)}, u32[]{:S(2)}, u32[]{:S(2)}) %collective-permute-start.1) | collective-permute-done | bytes 16416 | tf_op jit(solution)/shard_map/ppermute | solution.py:241
  14.5 0.6 %collective-permute-done.2.near_ref = f32[1,4,128,128]{3,2,1,0:T(8,128)S(1)} collective-permute-done((f32[1,4,128,128]{3,2,1,0:T(8,128)S(1)}, f32[1,4,128,128]{3,2,1,0:T(8,128)S(1)}, u32[]{:S(2)}, u32[]{:S(2)}) %collective-permute-start.2) | collective-permute-done | bytes 262176 | tf_op jit(solution)/shard_map/ppermute | solution.py:241
  15.0 0.3 shard_map.126
  15.3 0.3 collective-permute-start.3
  15.6 3.3 %collective-permute-done.3 = f32[4,128]{1,0:T(4,128)S(1)} collective-permute-done((f32[4,128]{1,0:T(4,128)S(1)}, f32[4,128]{1,0:T(4,128)S(1)}, u32[]{:S(2)}, u32[]{:S(2)}) %collective-permute-start.3) | collective-permute-done | bytes 2080 | tf_op jit(solution)/shard_map/ppermute | solution.py:245
  18.9 3.3 %collective-permute-start.4 = (f32[4,128]{1,0:T(4,128)S(1)}, f32[4,128]{1,0:T(4,128)S(1)}, u32[]{:S(2)}, u32[]{:S(2)}) collective-permute-start(f32[4,128]{1,0:T(4,128)S(1)} %add.3.a_ref), channel_id=1, source_target_pairs={{0,2},{1,3},{2,0},{3,1},{4,6},{5,7},{6,4},{7,5},{8,10},{9,11},{10,... | collective-permute-start | bytes 6152 | tf_op jit(solution)/shard_map/ppermute | solution.py:245
  22.2 1.6 %shard_map.127 = (f32[8,4,128,128]{3,2,1,0:T(8,128)}, f32[3,4,128,128]{3,2,1,0:T(8,128)S(1)}) custom-call(s32[25]{0:T(128)S(4)} %get-tuple-element.17.info_ref, f32[4,512]{1,0:T(4,128)S(1)} %get-tuple-element.18.fade_ref, f32[4,512]{1,0:T(4,128)S(1)} %get-tuple-element.28.back_ref, bf16[8,4,512]{2,1,0:T(4,128)(2,1)S(1)} %copy-done.1, ...), custom_call_target="tpu_custom_call" | custom-call | flops 1000000 | bytes 1000000 | tf_op jit(solution)/shard_map/pallas_call | solution.py:225
  23.8 0.0 collective-permute-done.4.b_ref
  23.9 5.0 %collective-permute-start.5 = (f32[4,128]{1,0:T(4,128)S(1)}, f32[4,128]{1,0:T(4,128)S(1)}, u32[]{:S(2)}, u32[]{:S(2)}) collective-permute-start(f32[4,128]{1,0:T(4,128)S(1)} %shard_map.128.square_a_ref), channel_id=1, source_target_pairs={{0,6},{1,7},{2,4},{3,5},{4,2},{5,3},{6,0},{7,1},{8,14},{9,15},{10,... | collective-permute-start | bytes 6152 | tf_op jit(solution)/shard_map/ppermute | solution.py:245
  28.8 0.0 collective-permute-done.6.far_ref
  28.8 0.9 %shard_map.129.new_ref = f32[8,4,128,128]{3,2,1,0:T(8,128)} custom-call(s32[25]{0:T(128)S(4)} %get-tuple-element.17.info_ref, f32[4,512]{1,0:T(4,128)S(1)} %get-tuple-element.18.fade_ref, f32[3,4,128,128]{3,2,1,0:T(8,128)S(1)} %get-tuple-element.29.added_ref, f32[2,4,128,128]{3,2,1,0:T(8,128)S(1)} %collective-permute-done.6.far_ref, ...), custom_call_target="tpu_custom_call", output_to_operand_aliasing={{}: (5, {})} | custom-call | flops 100000 | bytes 100000 | tf_op jit(solution)/shard_map/pallas_call | solution.py:225
  29.8 0.6 %collective-permute-done.5.square_b_ref = f32[4,128]{1,0:T(4,128)S(1)} collective-permute-done((f32[4,128]{1,0:T(4,128)S(1)}, f32[4,128]{1,0:T(4,128)S(1)}, u32[]{:S(2)}, u32[]{:S(2)}) %collective-permute-start.5) | collective-permute-done | bytes 2080 | tf_op jit(solution)/shard_map/ppermute | solution.py:245
  30.4 0.7 %shard_map.130 = bf16[8,4,512]{2,1,0:T(4,128)(2,1)} custom-call(f32[8,4,512]{2,1,0:T(4,128)S(1)} %get-tuple-element.21.gate_ref, f32[8,4,512]{2,1,0:T(4,128)S(1)} %get-tuple-element.26.out_ref, f32[4,128]{1,0:T(4,128)S(1)} %shard_map.128.square_a_ref, f32[4,128]{1,0:T(4,128)S(1)} %collective-permute-done.5.square_b_ref, f32[8,4,128,128]{3,2,1,0:T(8,128)} %shard_map.129.new_ref), custom_call_target="tpu_custom_call" | custom-call | flops 100000 | bytes 100000 | tf_op jit(solution)/shard_map/pallas_call | solution.py:225
  (2 shorter events, 0.0 us)
Async XLA Ops:
  0.6 4.4 %copy-start = (f32[8,4,128,128]{3,2,1,0:T(8,128)S(1)}, f32[8,4,128,128]{3,2,1,0:T(8,128)}, u32[]{:S(2)}) copy-start(f32[8,4,128,128]{3,2,1,0:T(8,128)} %states_ref.5) | copy-start | bytes 6291460
  1.7 5.3 %collective-permute-start = (f32[2,4,512]{2,1,0:T(4,128)S(1)}, f32[2,4,512]{2,1,0:T(4,128)S(1)}, u32[]{:S(2)}, u32[]{:S(2)}) collective-permute-start(f32[2,4,512]{2,1,0:T(4,128)S(1)} %get-tuple-element.19), channel_id=1, source_target_pairs={{0,128},{8,136},{16,144},{24,152},{32,160},{40,168},{48,176},{56,1... | collective-permute-start | bytes 49160 | tf_op jit(solution)/shard_map/ppermute | solution.py:241
  5.0 5.6 %copy-start.1 = (bf16[8,4,512]{2,1,0:T(4,128)(2,1)S(1)}, bf16[8,4,512]{2,1,0:T(4,128)(2,1)}, u32[]{:S(2)}) copy-start(bf16[8,4,512]{2,1,0:T(4,128)(2,1)} %key_ref.3) | copy-start | bytes 98308
  5.0 5.6 %copy-start.2 = (bf16[8,4,512]{2,1,0:T(4,128)(2,1)S(1)}, bf16[8,4,512]{2,1,0:T(4,128)(2,1)}, u32[]{:S(2)}) copy-start(bf16[8,4,512]{2,1,0:T(4,128)(2,1)} %value_ref.3) | copy-start | bytes 98308
  5.0 5.6 %copy-start.3 = (bf16[8,4,512]{2,1,0:T(4,128)(2,1)S(1)}, bf16[8,4,512]{2,1,0:T(4,128)(2,1)}, u32[]{:S(2)}) copy-start(bf16[8,4,512]{2,1,0:T(4,128)(2,1)} %query_ref.3) | copy-start | bytes 98308
  5.0 5.6 %copy-start.4 = (bf16[8,4,512]{2,1,0:T(4,128)(2,1)S(1)}, bf16[8,4,512]{2,1,0:T(4,128)(2,1)}, u32[]{:S(2)}) copy-start(bf16[8,4,512]{2,1,0:T(4,128)(2,1)} %gate_ref.1) | copy-start | bytes 98308
  5.0 5.6 %copy-start.5 = (f32[512]{0:T(512)S(1)}, f32[512]{0:T(512)}, u32[]{:S(2)}) copy-start(f32[512]{0:T(512)} %param.21) | copy-start | bytes 6148
  5.1 9.9 %collective-permute-start.2 = (f32[1,4,128,128]{3,2,1,0:T(8,128)S(1)}, f32[1,4,128,128]{3,2,1,0:T(8,128)S(1)}, u32[]{:S(2)}, u32[]{:S(2)}) collective-permute-start(f32[1,4,128,128]{3,2,1,0:T(8,128)S(1)} %get-tuple-element.22), channel_id=1, source_target_pairs={{0,8},{8,16},{16,24},{24,32},{32,40},{40,48},{48,56},{56,64},{64,7... | collective-permute-start | bytes 786440 | tf_op jit(solution)/shard_map/ppermute | solution.py:241
  7.3 7.2 %collective-permute-start.1 = (f32[2,4,512]{2,1,0:T(4,128)S(1)}, f32[2,4,512]{2,1,0:T(4,128)S(1)}, u32[]{:S(2)}, u32[]{:S(2)}) collective-permute-start(f32[2,4,512]{2,1,0:T(4,128)S(1)} %shard_map.124.answer_ref), channel_id=1, source_target_pairs={{0,128},{8,136},{16,144},{24,152},{32,160},{40,168},{48,176},{56,1... | collective-permute-start | bytes 49160 | tf_op jit(solution)/shard_map/ppermute | solution.py:241
  11.2 17.6 %collective-permute-start.6 = (f32[2,4,128,128]{3,2,1,0:T(8,128)S(1)}, f32[2,4,128,128]{3,2,1,0:T(8,128)S(1)}, u32[]{:S(2)}, u32[]{:S(2)}) collective-permute-start(f32[2,4,128,128]{3,2,1,0:T(8,128)S(1)} %get-tuple-element.30), channel_id=1, source_target_pairs={{0,128},{8,136},{16,144},{24,152},{32,160},{40,168},{48,176},{56,1... | collective-permute-start | bytes 1572872 | tf_op jit(solution)/shard_map/ppermute | solution.py:241
  15.3 3.6 %collective-permute-start.3 = (f32[4,128]{1,0:T(4,128)S(1)}, f32[4,128]{1,0:T(4,128)S(1)}, u32[]{:S(2)}, u32[]{:S(2)}) collective-permute-start(f32[4,128]{1,0:T(4,128)S(1)} %get-tuple-element.27.square_ref), channel_id=1, source_target_pairs={{0,1},{1,0},{2,3},{3,2},{4,5},{5,4},{6,7},{7,6},{8,9},{9,8},{10,11... | collective-permute-start | bytes 6152 | tf_op jit(solution)/shard_map/ppermute | solution.py:245
  18.9 4.9 %collective-permute-start.4 = (f32[4,128]{1,0:T(4,128)S(1)}, f32[4,128]{1,0:T(4,128)S(1)}, u32[]{:S(2)}, u32[]{:S(2)}) collective-permute-start(f32[4,128]{1,0:T(4,128)S(1)} %add.3.a_ref), channel_id=1, source_target_pairs={{0,2},{1,3},{2,0},{3,1},{4,6},{5,7},{6,4},{7,5},{8,10},{9,11},{10,... | collective-permute-start | bytes 6152 | tf_op jit(solution)/shard_map/ppermute | solution.py:245
  23.9 6.5 %collective-permute-start.5 = (f32[4,128]{1,0:T(4,128)S(1)}, f32[4,128]{1,0:T(4,128)S(1)}, u32[]{:S(2)}, u32[]{:S(2)}) collective-permute-start(f32[4,128]{1,0:T(4,128)S(1)} %shard_map.128.square_a_ref), channel_id=1, source_target_pairs={{0,6},{1,7},{2,4},{3,5},{4,2},{5,3},{6,0},{7,1},{8,14},{9,15},{10,... | collective-permute-start | bytes 6152 | tf_op jit(solution)/shard_map/ppermute | solution.py:245

commit v7 on v6

--- a/solution.py
+++ b/solution.py
@@ -35,7 +35,8 @@
     return lax.rem(me + (FAR if move < 2 else N_REP - 1), N_REP)
 
 
-SOURCE, VALID, SLOT, STAYS, LIVE, INFO = 0, MOVE, 2 * MOVE, 3 * MOVE, 3 * MOVE + SLOTS_DEV, 3 * MOVE + 2 * SLOTS_DEV
+SOURCE, VALID, SLOT, INFO = 0, MOVE, 2 * MOVE, 3 * MOVE
+STAYS, LIVE, ROWS = 0, SLOTS_DEV, 2 * SLOTS_DEV
 
 
 def split(x):
@@ -67,30 +68,30 @@
     return lax.broadcasted_iota(jnp.int32, (STEPS, DK), 0).astype(jnp.float32)
 
 
-def ask_kernel(
-    alive_ref, source_ref, target_ref, count_ref, rate_ref, query_ref,
-    out_ref, near_query_ref, fade_ref, back_ref, info_ref,
-):
+def ask_kernel(source_ref, target_ref, count_ref, query_ref, out_ref, info_ref):
     me = lax.axis_index("rep")
     for move in range(MOVE):
         sender = sender_of(move)
         slot = lax.rem(target_ref[move, sender], SLOTS_DEV)
+        if move < 2:
+            out_ref[move] = silu(query_ref[slot])
         info_ref[SOURCE + move] = source_ref[move, me]
         info_ref[VALID + move] = (count_ref[sender] > move).astype(jnp.int32)
         info_ref[SLOT + move] = slot
-        if move < 2:
-            out_ref[move] = silu(query_ref[slot])
-        else:
-            near_query_ref[...] = silu(query_ref[slot])
+
+
+def prepare_kernel(alive_ref, count_ref, rate_ref, info_ref, query_ref, rows_ref, near_query_ref, fade_ref, back_ref):
+    count = count_ref[lax.axis_index("rep")]
+    near_query_ref[...] = silu(query_ref[info_ref[SLOT + 2]])
     for slot in range(SLOTS_DEV):
         stays = alive_ref[slot]
         for move in range(MOVE):
-            stays = jnp.where((count_ref[me] > move) & (source_ref[move, me] == slot), 0, stays)
+            stays = jnp.where((count > move) & (info_ref[SOURCE + move] == slot), 0, stays)
         live = stays
         for move in range(MOVE):
             live = jnp.where((info_ref[VALID + move] == 1) & (info_ref[SLOT + move] == slot), 1, live)
-        info_ref[STAYS + slot] = stays
-        info_ref[LIVE + slot] = live
+        rows_ref[STAYS + slot] = stays
+        rows_ref[LIVE + slot] = live
     for head in range(HEADS_DEV):
         fade_ref[:, head_slice(head)] = jnp.exp(-rate_ref[head] * (times() + 1.0))
         back_ref[:, head_slice(head)] = jnp.exp(-rate_ref[head] * (STEPS - 1.0 - times()))
@@ -107,14 +108,15 @@
         copy.wait()
 
 
-def answer_kernel(query_ref, far_ref, out_ref):
+def answer_kernel(query_ref, far_ref, fade_ref, out_ref):
+    del fade_ref
     for move in range(2):
         for head in range(HEADS_DEV):
             out_ref[move, :, head_slice(head)] = read_out(query_ref[move, :, head_slice(head)], far_ref[move, head])
 
 
 def part_kernel(
-    info_ref, fade_ref, query_ref, key_ref, value_ref, gate_ref, gain_ref, states_ref, answer_ref, far_in_ref,
+    info_ref, flags_ref, fade_ref, query_ref, key_ref, value_ref, gate_ref, gain_ref, states_ref, answer_ref, far_in_ref,
     out_ref, flag_ref, gate_out_ref, far_ref,
 ):
     del answer_ref, far_in_ref, far_ref
@@ -122,8 +124,8 @@
         for move in range(MOVE):
             arrives = info_ref[VALID + move] * (info_ref[SLOT + move] == slot).astype(jnp.int32)
             flag_ref[move, slot] = jnp.full((STEPS, DK), arrives.astype(jnp.float32))
-        live = info_ref[LIVE + slot].astype(jnp.float32)
-        stays = info_ref[STAYS + slot].astype(jnp.float32)
+        live = flags_ref[LIVE + slot].astype(jnp.float32)
+        stays = flags_ref[STAYS + slot].astype(jnp.float32)
         gate_out_ref[slot] = gain_ref[...] * live / (1.0 + jnp.exp(-gate_ref[slot].astype(jnp.float32)))
         queries, keys, values = silu(query_ref[slot]), silu(key_ref[slot]), silu(value_ref[slot])
         inside = [jnp.zeros((STEPS, DK), jnp.float32)] * HEADS_DEV
@@ -141,14 +143,14 @@
 
 
 def state_kernel(
-    info_ref, fade_ref, back_ref, key_ref, value_ref, states_ref, square_ref,
+    info_ref, flags_ref, fade_ref, back_ref, key_ref, value_ref, states_ref, square_ref,
     new_ref, added_ref, rows_ref, sems,
 ):
     del square_ref
     copies = []
     for slot in range(SLOTS_DEV):
-        live = info_ref[LIVE + slot].astype(jnp.float32)
-        stays = info_ref[STAYS + slot].astype(jnp.float32)
+        live = flags_ref[LIVE + slot].astype(jnp.float32)
+        stays = flags_ref[STAYS + slot].astype(jnp.float32)
         keys, values = silu(key_ref[slot]) * (back_ref[...] * live), silu(value_ref[slot])
         for head in range(HEADS_DEV):
             at = head_slice(head)
@@ -248,29 +250,32 @@
 def local(states, alive_flag, plan_source, plan_target, move_count, query_proj, key_proj, value_proj, gate_proj, decay_rate, norm_gain):
     row = (HEADS_DEV, DK, DK)
     features = (SLOTS_DEV, STEPS, WIDTH)
-    asked, near_query, fade, back, info = call(
-        ask_kernel, (vmem(2, STEPS, WIDTH), vmem(STEPS, WIDTH), vmem(STEPS, WIDTH), vmem(STEPS, WIDTH), pltpu.SMEM((INFO,), jnp.int32)),
-        [SMEM] * 5 + [VMEM], in_hbm(alive_flag, plan_source.T, plan_target.T, move_count, decay_rate, query_proj),
-        out_specs=(VMEM,) * 4 + (SMEM,), cost=LONG)
+    source, target = plan_source.T, plan_target.T
+    asked, info = call(
+        ask_kernel, (vmem(2, STEPS, WIDTH), pltpu.SMEM((INFO,), jnp.int32)), [SMEM] * 3 + [VMEM],
+        in_hbm(source, target, move_count, query_proj), out_specs=(VMEM, SMEM), cost=LONG)
     asked = over_rep(asked, FAR)
     far, near = call(
         outbox_kernel, (vmem(2, *row), vmem(1, *row)), [SMEM, ANY], (info, states), out_specs=(VMEM, VMEM),
         scratch_shapes=[pltpu.SemaphoreType.DMA((MOVE,))], cost=LONG)
     near = over_rep(near, 1)
-    answer = call(answer_kernel, vmem(2, STEPS, WIDTH), [VMEM, VMEM], (asked, far), out_specs=VMEM)
+    rows, near_query, fade, back = call(
+        prepare_kernel, (pltpu.SMEM((ROWS,), jnp.int32), vmem(STEPS, WIDTH), vmem(STEPS, WIDTH), vmem(STEPS, WIDTH)),
+        [SMEM] * 4 + [VMEM], (*in_hbm(alive_flag, move_count, decay_rate), info, query_proj), out_specs=(SMEM,) + (VMEM,) * 3)
+    answer = call(answer_kernel, vmem(2, STEPS, WIDTH), [VMEM, VMEM, ANY], (asked, far, fade), out_specs=VMEM)
     part, arrives, gate, far = call(
         part_kernel, (vmem(*features), vmem(MOVE, SLOTS_DEV, STEPS, DK), vmem(*features), vmem(2, *row)),
-        [SMEM] + [VMEM] * 7 + [ANY] * 2,
-        (info, fade, query_proj, key_proj, value_proj, gate_proj, norm_gain.reshape(1, WIDTH), states, answer, far),
-        out_specs=(VMEM,) * 4, input_output_aliases={9: 3}, cost=LONG)
+        [SMEM] * 2 + [VMEM] * 7 + [ANY] * 2,
+        (info, rows, fade, query_proj, key_proj, value_proj, gate_proj, norm_gain.reshape(1, WIDTH), states, answer, far),
+        out_specs=(VMEM,) * 4, input_output_aliases={10: 3}, cost=LONG)
     answer = over_rep(answer, FAR)
     far = over_rep(far, FAR)
     out, square = call(
         combine_kernel, (vmem(*features), vmem(STEPS, DK)), [VMEM] * 6,
         (answer, near, near_query, part, arrives, fade), out_specs=(VMEM, VMEM), cost=LONG)
     new_states, added = call(
-        state_kernel, (pltpu.HBM((SLOTS_DEV, *row), jnp.float32), vmem(MOVE, *row)), [SMEM] + [VMEM] * 5 + [ANY],
-        (info, fade, back, key_proj, value_proj, states, square), out_specs=(HBM, VMEM),
+        state_kernel, (pltpu.HBM((SLOTS_DEV, *row), jnp.float32), vmem(MOVE, *row)), [SMEM] * 2 + [VMEM] * 5 + [ANY],
+        (info, rows, fade, back, key_proj, value_proj, states, square), out_specs=(HBM, VMEM),
         scratch_shapes=[pltpu.VMEM((SLOTS_DEV, *row), jnp.float32), pltpu.SemaphoreType.DMA((SLOTS_DEV,))], cost=1_000_000)
     square = square + over_head(square, 1)
     square = call(add_kernel, vmem(STEPS, DK), [VMEM, VMEM, ANY], (square, over_head(square, 2), added), out_specs=VMEM)

time: 31.2 us -> 31.2 us (level)
  waiting for transfers between devices: 9.15 us -> 7.84 us
  Pallas kernels: 5.61 us -> 6.32 us
  local copies, waits for them, and re-layouts: 0.03 us -> 0.56 us
    ppermute x4, waiting for transfers between devices: 5.18 us -> 3.87 us  [over_rep(): lax.ppermute(x, 'rep', [(i, (i + distance) % N_REP) for i in range(N_REP)])]
    pallas_call x9 -> x10, Pallas kernels: 5.61 us -> 6.32 us  [call(): pl.pallas_call(kernel, out_shape=outs, in_specs=in_specs, compiler_params...]
    unnamed x12, local copies, waits for them, and re-layouts: 0.03 us -> 0.56 us
  transfers between devices with their start and end apart: 7 -> 7, of which waited for: 5 -> 5; matrix products, arithmetic and copies ran while one was open for 0% -> 0% of each run, Pallas kernels for 12% -> 15%
where the time goes in v7:
time: 31.2 us; the launch traced here: 31 us
  starting transfers between devices  15.6 us (50%)
  waiting for transfers between devices  7.84 us (25%)
  Pallas kernels  6.32 us (20%)
  between operations  0.73 us (2%)
  local copies, waits for them, and re-layouts  0.56 us (2%)
    ppermute x3, starting transfers between devices, over_head(): return lax.ppermute(x, 'head', [(i, i ^ flip) for i in range(N_HEAD)])  8.52 us
    ppermute x4, starting transfers between devices, over_rep(): lax.ppermute(x, 'rep', [(i, (i + distance) % N_REP) for i in range(N_REP)])  7.04 us
    pallas_call x10, Pallas kernels, call(): pl.pallas_call(kernel, out_shape=outs, in_specs=in_specs, compiler_params...  6.32 us
    ppermute x3, waiting for transfers between devices, over_head(): return lax.ppermute(x, 'head', [(i, i ^ flip) for i in range(N_HEAD)])  3.97 us
    ppermute x4, waiting for transfers between devices, over_rep(): lax.ppermute(x, 'rep', [(i, (i + distance) % N_REP) for i in range(N_REP)])  3.87 us
  transfers between devices with their start and end apart: 7, of which 5 were waited for; matrix products, arithmetic and copies ran while one was open for 0% of the time, Pallas kernels for 15%

profile of v7, /device:TPU:32, one launch (start us, length us, event | category | flops | bytes accessed | tf_op | source)
XLA Modules:
  0.0 31.0 jit_solution(11142240436929994903)
XLA Ops:
  0.6 0.0 copy-start
  0.6 1.0 %shard_map.122 = (f32[2,4,512]{2,1,0:T(4,128)S(1)}, s32[9]{0:T(128)S(4)}) custom-call(s32[3,32]{1,0:T(4,128)} %bitcast.4, s32[3,32]{1,0:T(4,128)} %bitcast.5, s32[32]{0:T(128)} %count_ref.3, bf16[8,4,512]{2,1,0:T(4,128)(2,1)} %query_ref.5), custom_call_target="tpu_custom_call" | custom-call | flops 10000000000 | bytes 10000000000 | tf_op jit(solution)/shard_map/pallas_call | solution.py:227
  1.6 3.3 %collective-permute-start = (f32[2,4,512]{2,1,0:T(4,128)S(1)}, f32[2,4,512]{2,1,0:T(4,128)S(1)}, u32[]{:S(2)}, u32[]{:S(2)}) collective-permute-start(f32[2,4,512]{2,1,0:T(4,128)S(1)} %get-tuple-element.21), channel_id=1, source_target_pairs={{0,128},{8,136},{16,144},{24,152},{32,160},{40,168},{48,176},{56,1... | collective-permute-start | bytes 49160 | tf_op jit(solution)/shard_map/ppermute | solution.py:243
  4.9 0.0 copy-done
  4.9 0.0 copy-start.3
  4.9 0.0 copy-start.1
  4.9 0.0 copy-start.2
  4.9 0.0 copy-start.4
  4.9 0.0 copy-start.5
  4.9 0.1 shard_map.124
  5.0 0.1 collective-permute-start.2
  5.1 0.5 %copy-done.3 = bf16[8,4,512]{2,1,0:T(4,128)(2,1)S(1)} copy-done((bf16[8,4,512]{2,1,0:T(4,128)(2,1)S(1)}, bf16[8,4,512]{2,1,0:T(4,128)(2,1)}, u32[]{:S(2)}) %copy-start.3) | copy-done | bytes 32792
  5.7 0.8 %shard_map.123 = (s32[16]{0:T(128)S(4)}, f32[4,512]{1,0:T(4,128)S(1)}, f32[4,512]{1,0:T(4,128)S(1)}, f32[4,512]{1,0:T(4,128)S(1)}) custom-call(s32[8]{0:T(128)} %alive_ref.1, s32[32]{0:T(128)} %count_ref.3, f32[4]{0:T(128)} %rate_ref.1, s32[9]{0:T(128)S(4)} %get-tuple-element.18.info_ref, bf16[8,4,512]{2,1,0:T(4,128)(2,1)S(1)} %copy-done.3), custom_call_target="tpu_custom_call" | custom-call | flops 100000 | bytes 100000 | tf_op jit(solution)/shard_map/pallas_call | solution.py:227
  6.4 0.5 %collective-permute-done.query_ref = f32[2,4,512]{2,1,0:T(4,128)S(1)} collective-permute-done((f32[2,4,512]{2,1,0:T(4,128)S(1)}, f32[2,4,512]{2,1,0:T(4,128)S(1)}, u32[]{:S(2)}, u32[]{:S(2)}) %collective-permute-start) | collective-permute-done | bytes 16416 | tf_op jit(solution)/shard_map/ppermute | solution.py:243
  6.9 0.2 shard_map.125.answer_ref
  7.2 3.3 %collective-permute-start.1 = (f32[2,4,512]{2,1,0:T(4,128)S(1)}, f32[2,4,512]{2,1,0:T(4,128)S(1)}, u32[]{:S(2)}, u32[]{:S(2)}) collective-permute-start(f32[2,4,512]{2,1,0:T(4,128)S(1)} %shard_map.125.answer_ref), channel_id=1, source_target_pairs={{0,128},{8,136},{16,144},{24,152},{32,160},{40,168},{48,176},{56,1... | collective-permute-start | bytes 49160 | tf_op jit(solution)/shard_map/ppermute | solution.py:243
  10.5 0.0 copy-done.1
  10.5 0.0 copy-done.2
  10.5 0.0 copy-done.4
  10.5 0.0 copy-done.5
  10.5 0.7 %shard_map.126 = (f32[8,4,512]{2,1,0:T(4,128)S(1)}, f32[3,8,4,128]{3,2,1,0:T(4,128)S(1)}, f32[8,4,512]{2,1,0:T(4,128)S(1)}, f32[2,4,128,128]{3,2,1,0:T(8,128)S(1)}) custom-call(s32[9]{0:T(128)S(4)} %get-tuple-element.18.info_ref, s32[16]{0:T(128)S(4)} %get-tuple-element.19.flags_ref, ...), custom_call_target="tpu_custom_call", output_to_operand_aliasing={{3}: (10, {})} | custom-call | flops 10000000000 | bytes 10000000000 | tf_op jit(solution)/shard_map/pallas_call | solution.py:227
  11.2 0.4 %collective-permute-start.6 = (f32[2,4,128,128]{3,2,1,0:T(8,128)S(1)}, f32[2,4,128,128]{3,2,1,0:T(8,128)S(1)}, u32[]{:S(2)}, u32[]{:S(2)}) collective-permute-start(f32[2,4,128,128]{3,2,1,0:T(8,128)S(1)} %get-tuple-element.32), channel_id=1, source_target_pairs={{0,128},{8,136},{16,144},{24,152},{32,160},{40,168},{48,176},{56,1... | collective-permute-start | bytes 1572872 | tf_op jit(solution)/shard_map/ppermute | solution.py:243
  11.6 2.7 %collective-permute-done.1.answer_ref = f32[2,4,512]{2,1,0:T(4,128)S(1)} collective-permute-done((f32[2,4,512]{2,1,0:T(4,128)S(1)}, f32[2,4,512]{2,1,0:T(4,128)S(1)}, u32[]{:S(2)}, u32[]{:S(2)}) %collective-permute-start.1) | collective-permute-done | bytes 16416 | tf_op jit(solution)/shard_map/ppermute | solution.py:243
  14.3 0.7 %collective-permute-done.2.near_ref = f32[1,4,128,128]{3,2,1,0:T(8,128)S(1)} collective-permute-done((f32[1,4,128,128]{3,2,1,0:T(8,128)S(1)}, f32[1,4,128,128]{3,2,1,0:T(8,128)S(1)}, u32[]{:S(2)}, u32[]{:S(2)}) %collective-permute-start.2) | collective-permute-done | bytes 262176 | tf_op jit(solution)/shard_map/ppermute | solution.py:243
  14.9 0.3 shard_map.127
  15.2 0.3 collective-permute-start.3
  15.5 3.3 %collective-permute-done.3 = f32[4,128]{1,0:T(4,128)S(1)} collective-permute-done((f32[4,128]{1,0:T(4,128)S(1)}, f32[4,128]{1,0:T(4,128)S(1)}, u32[]{:S(2)}, u32[]{:S(2)}) %collective-permute-start.3) | collective-permute-done | bytes 2080 | tf_op jit(solution)/shard_map/ppermute | solution.py:247
  18.9 3.3 %collective-permute-start.4 = (f32[4,128]{1,0:T(4,128)S(1)}, f32[4,128]{1,0:T(4,128)S(1)}, u32[]{:S(2)}, u32[]{:S(2)}) collective-permute-start(f32[4,128]{1,0:T(4,128)S(1)} %add.3.a_ref), channel_id=1, source_target_pairs={{0,2},{1,3},{2,0},{3,1},{4,6},{5,7},{6,4},{7,5},{8,10},{9,11},{10,... | collective-permute-start | bytes 6152 | tf_op jit(solution)/shard_map/ppermute | solution.py:247
  22.1 1.6 %shard_map.128 = (f32[8,4,128,128]{3,2,1,0:T(8,128)}, f32[3,4,128,128]{3,2,1,0:T(8,128)S(1)}) custom-call(s32[9]{0:T(128)S(4)} %get-tuple-element.18.info_ref, s32[16]{0:T(128)S(4)} %get-tuple-element.19.flags_ref, f32[4,512]{1,0:T(4,128)S(1)} %get-tuple-element.20.fade_ref, f32[4,512]{1,0:T(4,128)S(1)} %get-tuple-element.30.back_ref, ...), custom_call_target="tpu_custom_call" | custom-call | flops 1000000 | bytes 1000000 | tf_op jit(solution)/shard_map/pallas_call | solution.py:227
  23.8 0.0 collective-permute-done.4.b_ref
  23.8 5.0 %collective-permute-start.5 = (f32[4,128]{1,0:T(4,128)S(1)}, f32[4,128]{1,0:T(4,128)S(1)}, u32[]{:S(2)}, u32[]{:S(2)}) collective-permute-start(f32[4,128]{1,0:T(4,128)S(1)} %shard_map.129.square_a_ref), channel_id=1, source_target_pairs={{0,6},{1,7},{2,4},{3,5},{4,2},{5,3},{6,0},{7,1},{8,14},{9,15},{10,... | collective-permute-start | bytes 6152 | tf_op jit(solution)/shard_map/ppermute | solution.py:247
  28.7 0.0 collective-permute-done.6.far_ref
  28.8 0.9 %shard_map.130.new_ref = f32[8,4,128,128]{3,2,1,0:T(8,128)} custom-call(s32[9]{0:T(128)S(4)} %get-tuple-element.18.info_ref, f32[4,512]{1,0:T(4,128)S(1)} %get-tuple-element.20.fade_ref, f32[3,4,128,128]{3,2,1,0:T(8,128)S(1)} %get-tuple-element.31.added_ref, f32[2,4,128,128]{3,2,1,0:T(8,128)S(1)} %collective-permute-done.6.far_ref, ...), custom_call_target="tpu_custom_call", output_to_operand_aliasing={{}: (5, {})} | custom-call | flops 100000 | bytes 100000 | tf_op jit(solution)/shard_map/pallas_call | solution.py:227
  29.7 0.6 %collective-permute-done.5.square_b_ref = f32[4,128]{1,0:T(4,128)S(1)} collective-permute-done((f32[4,128]{1,0:T(4,128)S(1)}, f32[4,128]{1,0:T(4,128)S(1)}, u32[]{:S(2)}, u32[]{:S(2)}) %collective-permute-start.5) | collective-permute-done | bytes 2080 | tf_op jit(solution)/shard_map/ppermute | solution.py:247
  30.3 0.7 %shard_map.131 = bf16[8,4,512]{2,1,0:T(4,128)(2,1)} custom-call(f32[8,4,512]{2,1,0:T(4,128)S(1)} %get-tuple-element.23.gate_ref, f32[8,4,512]{2,1,0:T(4,128)S(1)} %get-tuple-element.28.out_ref, f32[4,128]{1,0:T(4,128)S(1)} %shard_map.129.square_a_ref, f32[4,128]{1,0:T(4,128)S(1)} %collective-permute-done.5.square_b_ref, f32[8,4,128,128]{3,2,1,0:T(8,128)} %shard_map.130.new_ref), custom_call_target="tpu_custom_call" | custom-call | flops 100000 | bytes 100000 | tf_op jit(solution)/shard_map/pallas_call | solution.py:227
  (2 shorter events, 0.0 us)
Async XLA Ops:
  0.6 4.3 %copy-start = (f32[8,4,128,128]{3,2,1,0:T(8,128)S(1)}, f32[8,4,128,128]{3,2,1,0:T(8,128)}, u32[]{:S(2)}) copy-start(f32[8,4,128,128]{3,2,1,0:T(8,128)} %states_ref.5) | copy-start | bytes 6291460
  1.6 5.3 %collective-permute-start = (f32[2,4,512]{2,1,0:T(4,128)S(1)}, f32[2,4,512]{2,1,0:T(4,128)S(1)}, u32[]{:S(2)}, u32[]{:S(2)}) collective-permute-start(f32[2,4,512]{2,1,0:T(4,128)S(1)} %get-tuple-element.21), channel_id=1, source_target_pairs={{0,128},{8,136},{16,144},{24,152},{32,160},{40,168},{48,176},{56,1... | collective-permute-start | bytes 49160 | tf_op jit(solution)/shard_map/ppermute | solution.py:243
  4.9 0.8 %copy-start.3 = (bf16[8,4,512]{2,1,0:T(4,128)(2,1)S(1)}, bf16[8,4,512]{2,1,0:T(4,128)(2,1)}, u32[]{:S(2)}) copy-start(bf16[8,4,512]{2,1,0:T(4,128)(2,1)} %query_ref.5) | copy-start | bytes 98308
  4.9 5.6 %copy-start.1 = (bf16[8,4,512]{2,1,0:T(4,128)(2,1)S(1)}, bf16[8,4,512]{2,1,0:T(4,128)(2,1)}, u32[]{:S(2)}) copy-start(bf16[8,4,512]{2,1,0:T(4,128)(2,1)} %key_ref.3) | copy-start | bytes 98308
  4.9 5.6 %copy-start.2 = (bf16[8,4,512]{2,1,0:T(4,128)(2,1)S(1)}, bf16[8,4,512]{2,1,0:T(4,128)(2,1)}, u32[]{:S(2)}) copy-start(bf16[8,4,512]{2,1,0:T(4,128)(2,1)} %value_ref.3) | copy-start | bytes 98308
  4.9 5.6 %copy-start.4 = (bf16[8,4,512]{2,1,0:T(4,128)(2,1)S(1)}, bf16[8,4,512]{2,1,0:T(4,128)(2,1)}, u32[]{:S(2)}) copy-start(bf16[8,4,512]{2,1,0:T(4,128)(2,1)} %gate_ref.1) | copy-start | bytes 98308
  4.9 5.6 %copy-start.5 = (f32[512]{0:T(512)S(1)}, f32[512]{0:T(512)}, u32[]{:S(2)}) copy-start(f32[512]{0:T(512)} %param.21) | copy-start | bytes 6148
  5.0 9.9 %collective-permute-start.2 = (f32[1,4,128,128]{3,2,1,0:T(8,128)S(1)}, f32[1,4,128,128]{3,2,1,0:T(8,128)S(1)}, u32[]{:S(2)}, u32[]{:S(2)}) collective-permute-start(f32[1,4,128,128]{3,2,1,0:T(8,128)S(1)} %get-tuple-element.24), channel_id=1, source_target_pairs={{0,8},{8,16},{16,24},{24,32},{32,40},{40,48},{48,56},{56,64},{64,7... | collective-permute-start | bytes 786440 | tf_op jit(solution)/shard_map/ppermute | solution.py:243
  7.2 7.1 %collective-permute-start.1 = (f32[2,4,512]{2,1,0:T(4,128)S(1)}, f32[2,4,512]{2,1,0:T(4,128)S(1)}, u32[]{:S(2)}, u32[]{:S(2)}) collective-permute-start(f32[2,4,512]{2,1,0:T(4,128)S(1)} %shard_map.125.answer_ref), channel_id=1, source_target_pairs={{0,128},{8,136},{16,144},{24,152},{32,160},{40,168},{48,176},{56,1... | collective-permute-start | bytes 49160 | tf_op jit(solution)/shard_map/ppermute | solution.py:243
  11.2 17.6 %collective-permute-start.6 = (f32[2,4,128,128]{3,2,1,0:T(8,128)S(1)}, f32[2,4,128,128]{3,2,1,0:T(8,128)S(1)}, u32[]{:S(2)}, u32[]{:S(2)}) collective-permute-start(f32[2,4,128,128]{3,2,1,0:T(8,128)S(1)} %get-tuple-element.32), channel_id=1, source_target_pairs={{0,128},{8,136},{16,144},{24,152},{32,160},{40,168},{48,176},{56,1... | collective-permute-start | bytes 1572872 | tf_op jit(solution)/shard_map/ppermute | solution.py:243
  15.2 3.6 %collective-permute-start.3 = (f32[4,128]{1,0:T(4,128)S(1)}, f32[4,128]{1,0:T(4,128)S(1)}, u32[]{:S(2)}, u32[]{:S(2)}) collective-permute-start(f32[4,128]{1,0:T(4,128)S(1)} %get-tuple-element.29.square_ref), channel_id=1, source_target_pairs={{0,1},{1,0},{2,3},{3,2},{4,5},{5,4},{6,7},{7,6},{8,9},{9,8},{10,11... | collective-permute-start | bytes 6152 | tf_op jit(solution)/shard_map/ppermute | solution.py:247
  18.9 4.9 %collective-permute-start.4 = (f32[4,128]{1,0:T(4,128)S(1)}, f32[4,128]{1,0:T(4,128)S(1)}, u32[]{:S(2)}, u32[]{:S(2)}) collective-permute-start(f32[4,128]{1,0:T(4,128)S(1)} %add.3.a_ref), channel_id=1, source_target_pairs={{0,2},{1,3},{2,0},{3,1},{4,6},{5,7},{6,4},{7,5},{8,10},{9,11},{10,... | collective-permute-start | bytes 6152 | tf_op jit(solution)/shard_map/ppermute | solution.py:247
  23.8 6.5 %collective-permute-start.5 = (f32[4,128]{1,0:T(4,128)S(1)}, f32[4,128]{1,0:T(4,128)S(1)}, u32[]{:S(2)}, u32[]{:S(2)}) collective-permute-start(f32[4,128]{1,0:T(4,128)S(1)} %shard_map.129.square_a_ref), channel_id=1, source_target_pairs={{0,6},{1,7},{2,4},{3,5},{4,2},{5,3},{6,0},{7,1},{8,14},{9,15},{10,... | collective-permute-start | bytes 6152 | tf_op jit(solution)/shard_map/ppermute | solution.py:247

commit v8 on v7

--- a/solution.py
+++ b/solution.py
@@ -49,11 +49,11 @@
 
 
 def read_out(query, state):
-    rows = jnp.concatenate(split(query), axis=0)
-    high, low = split(state)
-    by_high = dot(rows, high, ((1,), (0,)))
-    by_low = dot(rows, low, ((1,), (0,)))
-    return by_high[:STEPS] + by_high[STEPS:] + by_low[:STEPS]
+    query_high, query_low = split(query)
+    rows = jnp.concatenate([
+        jnp.concatenate([query_high, query_high], axis=1), jnp.concatenate([query_low, jnp.zeros_like(query_low)], axis=1)], axis=0)
+    both = dot(rows, jnp.concatenate(split(state), axis=0), ((1,), (0,)))
+    return both[:STEPS] + both[STEPS:]
 
 
 def later_by(x, gap):

time: 31.2 us -> 31.2 us (level)
  transfers between devices with their start and end apart: 7 -> 7, of which waited for: 5 -> 5; matrix products, arithmetic and copies ran while one was open for 0% -> 0% of each run, Pallas kernels for 15% -> 14%
where the time goes in v8:
time: 31.2 us; the launch traced here: 31 us
  starting transfers between devices  15.6 us (50%)
  waiting for transfers between devices  7.96 us (26%)
  Pallas kernels  6.09 us (20%)
  between operations  0.73 us (2%)
  local copies, waits for them, and re-layouts  0.56 us (2%)
    ppermute x3, starting transfers between devices, over_head(): return lax.ppermute(x, 'head', [(i, i ^ flip) for i in range(N_HEAD)])  8.59 us
    ppermute x4, starting transfers between devices, over_rep(): lax.ppermute(x, 'rep', [(i, (i + distance) % N_REP) for i in range(N_REP)])  7.05 us
    pallas_call x10, Pallas kernels, call(): pl.pallas_call(kernel, out_shape=outs, in_specs=in_specs, compiler_params...  6.09 us
    ppermute x4, waiting for transfers between devices, over_rep(): lax.ppermute(x, 'rep', [(i, (i + distance) % N_REP) for i in range(N_REP)])  4.07 us
    ppermute x3, waiting for transfers between devices, over_head(): return lax.ppermute(x, 'head', [(i, i ^ flip) for i in range(N_HEAD)])  3.89 us
  transfers between devices with their start and end apart: 7, of which 5 were waited for; matrix products, arithmetic and copies ran while one was open for 0% of the time, Pallas kernels for 14%

profile of v8, /device:TPU:32, one launch (start us, length us, event | category | flops | bytes accessed | tf_op | source)
XLA Modules:
  0.0 31.0 jit_solution(3584763674261230162)
XLA Ops:
  0.6 0.0 copy-start
  0.6 1.0 %shard_map.122 = (f32[2,4,512]{2,1,0:T(4,128)S(1)}, s32[9]{0:T(128)S(4)}) custom-call(s32[3,32]{1,0:T(4,128)} %bitcast.4, s32[3,32]{1,0:T(4,128)} %bitcast.5, s32[32]{0:T(128)} %count_ref.3, bf16[8,4,512]{2,1,0:T(4,128)(2,1)} %query_ref.5), custom_call_target="tpu_custom_call" | custom-call | flops 10000000000 | bytes 10000000000 | tf_op jit(solution)/shard_map/pallas_call | solution.py:227
  1.6 3.3 %collective-permute-start = (f32[2,4,512]{2,1,0:T(4,128)S(1)}, f32[2,4,512]{2,1,0:T(4,128)S(1)}, u32[]{:S(2)}, u32[]{:S(2)}) collective-permute-start(f32[2,4,512]{2,1,0:T(4,128)S(1)} %get-tuple-element.21), channel_id=1, source_target_pairs={{0,128},{8,136},{16,144},{24,152},{32,160},{40,168},{48,176},{56,1... | collective-permute-start | bytes 49160 | tf_op jit(solution)/shard_map/ppermute | solution.py:243
  4.9 0.0 copy-done
  4.9 0.0 copy-start.3
  4.9 0.0 copy-start.1
  4.9 0.0 copy-start.2
  4.9 0.0 copy-start.4
  4.9 0.0 copy-start.5
  4.9 0.1 shard_map.124
  5.0 0.1 collective-permute-start.2
  5.1 0.5 %copy-done.3 = bf16[8,4,512]{2,1,0:T(4,128)(2,1)S(1)} copy-done((bf16[8,4,512]{2,1,0:T(4,128)(2,1)S(1)}, bf16[8,4,512]{2,1,0:T(4,128)(2,1)}, u32[]{:S(2)}) %copy-start.3) | copy-done | bytes 32792
  5.7 0.8 %shard_map.123 = (s32[16]{0:T(128)S(4)}, f32[4,512]{1,0:T(4,128)S(1)}, f32[4,512]{1,0:T(4,128)S(1)}, f32[4,512]{1,0:T(4,128)S(1)}) custom-call(s32[8]{0:T(128)} %alive_ref.1, s32[32]{0:T(128)} %count_ref.3, f32[4]{0:T(128)} %rate_ref.1, s32[9]{0:T(128)S(4)} %get-tuple-element.18.info_ref, bf16[8,4,512]{2,1,0:T(4,128)(2,1)S(1)} %copy-done.3), custom_call_target="tpu_custom_call" | custom-call | flops 100000 | bytes 100000 | tf_op jit(solution)/shard_map/pallas_call | solution.py:227
  6.4 0.5 %collective-permute-done.query_ref = f32[2,4,512]{2,1,0:T(4,128)S(1)} collective-permute-done((f32[2,4,512]{2,1,0:T(4,128)S(1)}, f32[2,4,512]{2,1,0:T(4,128)S(1)}, u32[]{:S(2)}, u32[]{:S(2)}) %collective-permute-start) | collective-permute-done | bytes 16416 | tf_op jit(solution)/shard_map/ppermute | solution.py:243
  6.9 0.2 shard_map.125.answer_ref
  7.1 3.3 %collective-permute-start.1 = (f32[2,4,512]{2,1,0:T(4,128)S(1)}, f32[2,4,512]{2,1,0:T(4,128)S(1)}, u32[]{:S(2)}, u32[]{:S(2)}) collective-permute-start(f32[2,4,512]{2,1,0:T(4,128)S(1)} %shard_map.125.answer_ref), channel_id=1, source_target_pairs={{0,128},{8,136},{16,144},{24,152},{32,160},{40,168},{48,176},{56,1... | collective-permute-start | bytes 49160 | tf_op jit(solution)/shard_map/ppermute | solution.py:243
  10.4 0.0 copy-done.1
  10.4 0.0 copy-done.2
  10.4 0.0 copy-done.4
  10.4 0.0 copy-done.5
  10.4 0.5 %shard_map.126 = (f32[8,4,512]{2,1,0:T(4,128)S(1)}, f32[3,8,4,128]{3,2,1,0:T(4,128)S(1)}, f32[8,4,512]{2,1,0:T(4,128)S(1)}, f32[2,4,128,128]{3,2,1,0:T(8,128)S(1)}) custom-call(s32[9]{0:T(128)S(4)} %get-tuple-element.18.info_ref, s32[16]{0:T(128)S(4)} %get-tuple-element.19.flags_ref, ...), custom_call_target="tpu_custom_call", output_to_operand_aliasing={{3}: (10, {})} | custom-call | flops 10000000000 | bytes 10000000000 | tf_op jit(solution)/shard_map/pallas_call | solution.py:227
  11.0 0.4 %collective-permute-start.6 = (f32[2,4,128,128]{3,2,1,0:T(8,128)S(1)}, f32[2,4,128,128]{3,2,1,0:T(8,128)S(1)}, u32[]{:S(2)}, u32[]{:S(2)}) collective-permute-start(f32[2,4,128,128]{3,2,1,0:T(8,128)S(1)} %get-tuple-element.32), channel_id=1, source_target_pairs={{0,128},{8,136},{16,144},{24,152},{32,160},{40,168},{48,176},{56,1... | collective-permute-start | bytes 1572872 | tf_op jit(solution)/shard_map/ppermute | solution.py:243
  11.4 2.9 %collective-permute-done.1.answer_ref = f32[2,4,512]{2,1,0:T(4,128)S(1)} collective-permute-done((f32[2,4,512]{2,1,0:T(4,128)S(1)}, f32[2,4,512]{2,1,0:T(4,128)S(1)}, u32[]{:S(2)}, u32[]{:S(2)}) %collective-permute-start.1) | collective-permute-done | bytes 16416 | tf_op jit(solution)/shard_map/ppermute | solution.py:243
  14.3 0.7 %collective-permute-done.2.near_ref = f32[1,4,128,128]{3,2,1,0:T(8,128)S(1)} collective-permute-done((f32[1,4,128,128]{3,2,1,0:T(8,128)S(1)}, f32[1,4,128,128]{3,2,1,0:T(8,128)S(1)}, u32[]{:S(2)}, u32[]{:S(2)}) %collective-permute-start.2) | collective-permute-done | bytes 262176 | tf_op jit(solution)/shard_map/ppermute | solution.py:243
  14.9 0.2 shard_map.127
  15.2 0.4 %collective-permute-start.3 = (f32[4,128]{1,0:T(4,128)S(1)}, f32[4,128]{1,0:T(4,128)S(1)}, u32[]{:S(2)}, u32[]{:S(2)}) collective-permute-start(f32[4,128]{1,0:T(4,128)S(1)} %get-tuple-element.29.square_ref), channel_id=1, source_target_pairs={{0,1},{1,0},{2,3},{3,2},{4,5},{5,4},{6,7},{7,6},{8,9},{9,8},{10,11... | collective-permute-start | bytes 6152 | tf_op jit(solution)/shard_map/ppermute | solution.py:247
  15.6 3.3 %collective-permute-done.3 = f32[4,128]{1,0:T(4,128)S(1)} collective-permute-done((f32[4,128]{1,0:T(4,128)S(1)}, f32[4,128]{1,0:T(4,128)S(1)}, u32[]{:S(2)}, u32[]{:S(2)}) %collective-permute-start.3) | collective-permute-done | bytes 2080 | tf_op jit(solution)/shard_map/ppermute | solution.py:247
  18.8 3.3 %collective-permute-start.4 = (f32[4,128]{1,0:T(4,128)S(1)}, f32[4,128]{1,0:T(4,128)S(1)}, u32[]{:S(2)}, u32[]{:S(2)}) collective-permute-start(f32[4,128]{1,0:T(4,128)S(1)} %add.3.a_ref), channel_id=1, source_target_pairs={{0,2},{1,3},{2,0},{3,1},{4,6},{5,7},{6,4},{7,5},{8,10},{9,11},{10,... | collective-permute-start | bytes 6152 | tf_op jit(solution)/shard_map/ppermute | solution.py:247
  22.1 1.6 %shard_map.128 = (f32[8,4,128,128]{3,2,1,0:T(8,128)}, f32[3,4,128,128]{3,2,1,0:T(8,128)S(1)}) custom-call(s32[9]{0:T(128)S(4)} %get-tuple-element.18.info_ref, s32[16]{0:T(128)S(4)} %get-tuple-element.19.flags_ref, f32[4,512]{1,0:T(4,128)S(1)} %get-tuple-element.20.fade_ref, f32[4,512]{1,0:T(4,128)S(1)} %get-tuple-element.30.back_ref, ...), custom_call_target="tpu_custom_call" | custom-call | flops 1000000 | bytes 1000000 | tf_op jit(solution)/shard_map/pallas_call | solution.py:227
  23.7 0.0 collective-permute-done.4.b_ref
  23.8 5.0 %collective-permute-start.5 = (f32[4,128]{1,0:T(4,128)S(1)}, f32[4,128]{1,0:T(4,128)S(1)}, u32[]{:S(2)}, u32[]{:S(2)}) collective-permute-start(f32[4,128]{1,0:T(4,128)S(1)} %shard_map.129.square_a_ref), channel_id=1, source_target_pairs={{0,6},{1,7},{2,4},{3,5},{4,2},{5,3},{6,0},{7,1},{8,14},{9,15},{10,... | collective-permute-start | bytes 6152 | tf_op jit(solution)/shard_map/ppermute | solution.py:247
  28.7 0.0 collective-permute-done.6.far_ref
  28.7 0.9 %shard_map.130.new_ref = f32[8,4,128,128]{3,2,1,0:T(8,128)} custom-call(s32[9]{0:T(128)S(4)} %get-tuple-element.18.info_ref, f32[4,512]{1,0:T(4,128)S(1)} %get-tuple-element.20.fade_ref, f32[3,4,128,128]{3,2,1,0:T(8,128)S(1)} %get-tuple-element.31.added_ref, f32[2,4,128,128]{3,2,1,0:T(8,128)S(1)} %collective-permute-done.6.far_ref, ...), custom_call_target="tpu_custom_call", output_to_operand_aliasing={{}: (5, {})} | custom-call | flops 100000 | bytes 100000 | tf_op jit(solution)/shard_map/pallas_call | solution.py:227
  29.7 0.6 %collective-permute-done.5.square_b_ref = f32[4,128]{1,0:T(4,128)S(1)} collective-permute-done((f32[4,128]{1,0:T(4,128)S(1)}, f32[4,128]{1,0:T(4,128)S(1)}, u32[]{:S(2)}, u32[]{:S(2)}) %collective-permute-start.5) | collective-permute-done | bytes 2080 | tf_op jit(solution)/shard_map/ppermute | solution.py:247
  30.3 0.7 %shard_map.131 = bf16[8,4,512]{2,1,0:T(4,128)(2,1)} custom-call(f32[8,4,512]{2,1,0:T(4,128)S(1)} %get-tuple-element.23.gate_ref, f32[8,4,512]{2,1,0:T(4,128)S(1)} %get-tuple-element.28.out_ref, f32[4,128]{1,0:T(4,128)S(1)} %shard_map.129.square_a_ref, f32[4,128]{1,0:T(4,128)S(1)} %collective-permute-done.5.square_b_ref, f32[8,4,128,128]{3,2,1,0:T(8,128)} %shard_map.130.new_ref), custom_call_target="tpu_custom_call" | custom-call | flops 100000 | bytes 100000 | tf_op jit(solution)/shard_map/pallas_call | solution.py:227
  (2 shorter events, 0.0 us)
Async XLA Ops:
  0.6 4.3 %copy-start = (f32[8,4,128,128]{3,2,1,0:T(8,128)S(1)}, f32[8,4,128,128]{3,2,1,0:T(8,128)}, u32[]{:S(2)}) copy-start(f32[8,4,128,128]{3,2,1,0:T(8,128)} %states_ref.5) | copy-start | bytes 6291460
  1.6 5.3 %collective-permute-start = (f32[2,4,512]{2,1,0:T(4,128)S(1)}, f32[2,4,512]{2,1,0:T(4,128)S(1)}, u32[]{:S(2)}, u32[]{:S(2)}) collective-permute-start(f32[2,4,512]{2,1,0:T(4,128)S(1)} %get-tuple-element.21), channel_id=1, source_target_pairs={{0,128},{8,136},{16,144},{24,152},{32,160},{40,168},{48,176},{56,1... | collective-permute-start | bytes 49160 | tf_op jit(solution)/shard_map/ppermute | solution.py:243
  4.9 0.8 %copy-start.3 = (bf16[8,4,512]{2,1,0:T(4,128)(2,1)S(1)}, bf16[8,4,512]{2,1,0:T(4,128)(2,1)}, u32[]{:S(2)}) copy-start(bf16[8,4,512]{2,1,0:T(4,128)(2,1)} %query_ref.5) | copy-start | bytes 98308
  4.9 5.5 %copy-start.1 = (bf16[8,4,512]{2,1,0:T(4,128)(2,1)S(1)}, bf16[8,4,512]{2,1,0:T(4,128)(2,1)}, u32[]{:S(2)}) copy-start(bf16[8,4,512]{2,1,0:T(4,128)(2,1)} %key_ref.3) | copy-start | bytes 98308
  4.9 5.5 %copy-start.2 = (bf16[8,4,512]{2,1,0:T(4,128)(2,1)S(1)}, bf16[8,4,512]{2,1,0:T(4,128)(2,1)}, u32[]{:S(2)}) copy-start(bf16[8,4,512]{2,1,0:T(4,128)(2,1)} %value_ref.3) | copy-start | bytes 98308
  4.9 5.5 %copy-start.4 = (bf16[8,4,512]{2,1,0:T(4,128)(2,1)S(1)}, bf16[8,4,512]{2,1,0:T(4,128)(2,1)}, u32[]{:S(2)}) copy-start(bf16[8,4,512]{2,1,0:T(4,128)(2,1)} %gate_ref.1) | copy-start | bytes 98308
  4.9 5.5 %copy-start.5 = (f32[512]{0:T(512)S(1)}, f32[512]{0:T(512)}, u32[]{:S(2)}) copy-start(f32[512]{0:T(512)} %param.21) | copy-start | bytes 6148
  5.0 9.9 %collective-permute-start.2 = (f32[1,4,128,128]{3,2,1,0:T(8,128)S(1)}, f32[1,4,128,128]{3,2,1,0:T(8,128)S(1)}, u32[]{:S(2)}, u32[]{:S(2)}) collective-permute-start(f32[1,4,128,128]{3,2,1,0:T(8,128)S(1)} %get-tuple-element.24), channel_id=1, source_target_pairs={{0,8},{8,16},{16,24},{24,32},{32,40},{40,48},{48,56},{56,64},{64,7... | collective-permute-start | bytes 786440 | tf_op jit(solution)/shard_map/ppermute | solution.py:243
  7.1 7.1 %collective-permute-start.1 = (f32[2,4,512]{2,1,0:T(4,128)S(1)}, f32[2,4,512]{2,1,0:T(4,128)S(1)}, u32[]{:S(2)}, u32[]{:S(2)}) collective-permute-start(f32[2,4,512]{2,1,0:T(4,128)S(1)} %shard_map.125.answer_ref), channel_id=1, source_target_pairs={{0,128},{8,136},{16,144},{24,152},{32,160},{40,168},{48,176},{56,1... | collective-permute-start | bytes 49160 | tf_op jit(solution)/shard_map/ppermute | solution.py:243
  11.0 17.8 %collective-permute-start.6 = (f32[2,4,128,128]{3,2,1,0:T(8,128)S(1)}, f32[2,4,128,128]{3,2,1,0:T(8,128)S(1)}, u32[]{:S(2)}, u32[]{:S(2)}) collective-permute-start(f32[2,4,128,128]{3,2,1,0:T(8,128)S(1)} %get-tuple-element.32), channel_id=1, source_target_pairs={{0,128},{8,136},{16,144},{24,152},{32,160},{40,168},{48,176},{56,1... | collective-permute-start | bytes 1572872 | tf_op jit(solution)/shard_map/ppermute | solution.py:243
  15.2 3.6 %collective-permute-start.3 = (f32[4,128]{1,0:T(4,128)S(1)}, f32[4,128]{1,0:T(4,128)S(1)}, u32[]{:S(2)}, u32[]{:S(2)}) collective-permute-start(f32[4,128]{1,0:T(4,128)S(1)} %get-tuple-element.29.square_ref), channel_id=1, source_target_pairs={{0,1},{1,0},{2,3},{3,2},{4,5},{5,4},{6,7},{7,6},{8,9},{9,8},{10,11... | collective-permute-start | bytes 6152 | tf_op jit(solution)/shard_map/ppermute | solution.py:247
  18.8 4.9 %collective-permute-start.4 = (f32[4,128]{1,0:T(4,128)S(1)}, f32[4,128]{1,0:T(4,128)S(1)}, u32[]{:S(2)}, u32[]{:S(2)}) collective-permute-start(f32[4,128]{1,0:T(4,128)S(1)} %add.3.a_ref), channel_id=1, source_target_pairs={{0,2},{1,3},{2,0},{3,1},{4,6},{5,7},{6,4},{7,5},{8,10},{9,11},{10,... | collective-permute-start | bytes 6152 | tf_op jit(solution)/shard_map/ppermute | solution.py:247
  23.8 6.5 %collective-permute-start.5 = (f32[4,128]{1,0:T(4,128)S(1)}, f32[4,128]{1,0:T(4,128)S(1)}, u32[]{:S(2)}, u32[]{:S(2)}) collective-permute-start(f32[4,128]{1,0:T(4,128)S(1)} %shard_map.129.square_a_ref), channel_id=1, source_target_pairs={{0,6},{1,7},{2,4},{3,5},{4,2},{5,3},{6,0},{7,1},{8,14},{9,15},{10,... | collective-permute-start | bytes 6152 | tf_op jit(solution)/shard_map/ppermute | solution.py:247

commit v9 on v8

--- a/solution.py
+++ b/solution.py
@@ -183,7 +183,7 @@
             at = head_slice(head)
             row = part_ref[slot, :, at]
             for move in range(MOVE):
-                row = jnp.where(flag_ref[move, slot] > 0.0, row + moved[move][:, at], row)
+                row += flag_ref[move, slot] * moved[move][:, at]
             out_ref[slot, :, at] = row
             total += row * row
         squares = jnp.where(lanes == slot, jnp.sum(total, axis=1, keepdims=True), squares)

time: 31.2 us -> 31.1 us (level)
  no operation moved by 1% of the time
where the time goes in v9:
time: 31.1 us; the launch traced here: 31 us
  starting transfers between devices  15.6 us (50%)
  waiting for transfers between devices  7.96 us (26%)
  Pallas kernels  6.09 us (20%)
  between operations  0.73 us (2%)
  local copies, waits for them, and re-layouts  0.56 us (2%)
    ppermute x3, starting transfers between devices, over_head(): return lax.ppermute(x, 'head', [(i, i ^ flip) for i in range(N_HEAD)])  8.56 us
    ppermute x4, starting transfers between devices, over_rep(): lax.ppermute(x, 'rep', [(i, (i + distance) % N_REP) for i in range(N_REP)])  7.05 us
    pallas_call x10, Pallas kernels, call(): pl.pallas_call(kernel, out_shape=outs, in_specs=in_specs, compiler_params...  6.09 us
    ppermute x4, waiting for transfers between devices, over_rep(): lax.ppermute(x, 'rep', [(i, (i + distance) % N_REP) for i in range(N_REP)])  4.07 us
    ppermute x3, waiting for transfers between devices, over_head(): return lax.ppermute(x, 'head', [(i, i ^ flip) for i in range(N_HEAD)])  3.89 us
  transfers between devices with their start and end apart: 7, of which 5 were waited for; matrix products, arithmetic and copies ran while one was open for 0% of the time, Pallas kernels for 14%

profile of v9, /device:TPU:32, one launch (start us, length us, event | category | flops | bytes accessed | tf_op | source)
XLA Modules:
  0.0 31.0 jit_solution(1653550959948483913)
XLA Ops:
  0.6 0.0 copy-start
  0.6 1.0 %shard_map.122 = (f32[2,4,512]{2,1,0:T(4,128)S(1)}, s32[9]{0:T(128)S(4)}) custom-call(s32[3,32]{1,0:T(4,128)} %bitcast.4, s32[3,32]{1,0:T(4,128)} %bitcast.5, s32[32]{0:T(128)} %count_ref.3, bf16[8,4,512]{2,1,0:T(4,128)(2,1)} %query_ref.5), custom_call_target="tpu_custom_call" | custom-call | flops 10000000000 | bytes 10000000000 | tf_op jit(solution)/shard_map/pallas_call | solution.py:227
  1.6 3.3 %collective-permute-start = (f32[2,4,512]{2,1,0:T(4,128)S(1)}, f32[2,4,512]{2,1,0:T(4,128)S(1)}, u32[]{:S(2)}, u32[]{:S(2)}) collective-permute-start(f32[2,4,512]{2,1,0:T(4,128)S(1)} %get-tuple-element.21), channel_id=1, source_target_pairs={{0,128},{8,136},{16,144},{24,152},{32,160},{40,168},{48,176},{56,1... | collective-permute-start | bytes 49160 | tf_op jit(solution)/shard_map/ppermute | solution.py:243
  4.9 0.0 copy-done
  4.9 0.0 copy-start.3
  4.9 0.0 copy-start.1
  4.9 0.0 copy-start.2
  4.9 0.0 copy-start.4
  4.9 0.0 copy-start.5
  4.9 0.1 shard_map.124
  5.0 0.1 collective-permute-start.2
  5.1 0.5 %copy-done.3 = bf16[8,4,512]{2,1,0:T(4,128)(2,1)S(1)} copy-done((bf16[8,4,512]{2,1,0:T(4,128)(2,1)S(1)}, bf16[8,4,512]{2,1,0:T(4,128)(2,1)}, u32[]{:S(2)}) %copy-start.3) | copy-done | bytes 32792
  5.7 0.8 %shard_map.123 = (s32[16]{0:T(128)S(4)}, f32[4,512]{1,0:T(4,128)S(1)}, f32[4,512]{1,0:T(4,128)S(1)}, f32[4,512]{1,0:T(4,128)S(1)}) custom-call(s32[8]{0:T(128)} %alive_ref.1, s32[32]{0:T(128)} %count_ref.3, f32[4]{0:T(128)} %rate_ref.1, s32[9]{0:T(128)S(4)} %get-tuple-element.18.info_ref, bf16[8,4,512]{2,1,0:T(4,128)(2,1)S(1)} %copy-done.3), custom_call_target="tpu_custom_call" | custom-call | flops 100000 | bytes 100000 | tf_op jit(solution)/shard_map/pallas_call | solution.py:227
  6.4 0.5 %collective-permute-done.query_ref = f32[2,4,512]{2,1,0:T(4,128)S(1)} collective-permute-done((f32[2,4,512]{2,1,0:T(4,128)S(1)}, f32[2,4,512]{2,1,0:T(4,128)S(1)}, u32[]{:S(2)}, u32[]{:S(2)}) %collective-permute-start) | collective-permute-done | bytes 16416 | tf_op jit(solution)/shard_map/ppermute | solution.py:243
  6.9 0.2 shard_map.125.answer_ref
  7.1 3.3 %collective-permute-start.1 = (f32[2,4,512]{2,1,0:T(4,128)S(1)}, f32[2,4,512]{2,1,0:T(4,128)S(1)}, u32[]{:S(2)}, u32[]{:S(2)}) collective-permute-start(f32[2,4,512]{2,1,0:T(4,128)S(1)} %shard_map.125.answer_ref), channel_id=1, source_target_pairs={{0,128},{8,136},{16,144},{24,152},{32,160},{40,168},{48,176},{56,1... | collective-permute-start | bytes 49160 | tf_op jit(solution)/shard_map/ppermute | solution.py:243
  10.4 0.0 copy-done.1
  10.4 0.0 copy-done.2
  10.4 0.0 copy-done.4
  10.4 0.0 copy-done.5
  10.4 0.5 %shard_map.126 = (f32[8,4,512]{2,1,0:T(4,128)S(1)}, f32[3,8,4,128]{3,2,1,0:T(4,128)S(1)}, f32[8,4,512]{2,1,0:T(4,128)S(1)}, f32[2,4,128,128]{3,2,1,0:T(8,128)S(1)}) custom-call(s32[9]{0:T(128)S(4)} %get-tuple-element.18.info_ref, s32[16]{0:T(128)S(4)} %get-tuple-element.19.flags_ref, ...), custom_call_target="tpu_custom_call", output_to_operand_aliasing={{3}: (10, {})} | custom-call | flops 10000000000 | bytes 10000000000 | tf_op jit(solution)/shard_map/pallas_call | solution.py:227
  11.0 0.4 %collective-permute-start.6 = (f32[2,4,128,128]{3,2,1,0:T(8,128)S(1)}, f32[2,4,128,128]{3,2,1,0:T(8,128)S(1)}, u32[]{:S(2)}, u32[]{:S(2)}) collective-permute-start(f32[2,4,128,128]{3,2,1,0:T(8,128)S(1)} %get-tuple-element.32), channel_id=1, source_target_pairs={{0,128},{8,136},{16,144},{24,152},{32,160},{40,168},{48,176},{56,1... | collective-permute-start | bytes 1572872 | tf_op jit(solution)/shard_map/ppermute | solution.py:243
  11.4 2.9 %collective-permute-done.1.answer_ref = f32[2,4,512]{2,1,0:T(4,128)S(1)} collective-permute-done((f32[2,4,512]{2,1,0:T(4,128)S(1)}, f32[2,4,512]{2,1,0:T(4,128)S(1)}, u32[]{:S(2)}, u32[]{:S(2)}) %collective-permute-start.1) | collective-permute-done | bytes 16416 | tf_op jit(solution)/shard_map/ppermute | solution.py:243
  14.3 0.7 %collective-permute-done.2.near_ref = f32[1,4,128,128]{3,2,1,0:T(8,128)S(1)} collective-permute-done((f32[1,4,128,128]{3,2,1,0:T(8,128)S(1)}, f32[1,4,128,128]{3,2,1,0:T(8,128)S(1)}, u32[]{:S(2)}, u32[]{:S(2)}) %collective-permute-start.2) | collective-permute-done | bytes 262176 | tf_op jit(solution)/shard_map/ppermute | solution.py:243
  14.9 0.2 shard_map.127
  15.2 0.3 %collective-permute-start.3 = (f32[4,128]{1,0:T(4,128)S(1)}, f32[4,128]{1,0:T(4,128)S(1)}, u32[]{:S(2)}, u32[]{:S(2)}) collective-permute-start(f32[4,128]{1,0:T(4,128)S(1)} %get-tuple-element.29.square_ref), channel_id=1, source_target_pairs={{0,1},{1,0},{2,3},{3,2},{4,5},{5,4},{6,7},{7,6},{8,9},{9,8},{10,11... | collective-permute-start | bytes 6152 | tf_op jit(solution)/shard_map/ppermute | solution.py:247
  15.5 3.3 %collective-permute-done.3 = f32[4,128]{1,0:T(4,128)S(1)} collective-permute-done((f32[4,128]{1,0:T(4,128)S(1)}, f32[4,128]{1,0:T(4,128)S(1)}, u32[]{:S(2)}, u32[]{:S(2)}) %collective-permute-start.3) | collective-permute-done | bytes 2080 | tf_op jit(solution)/shard_map/ppermute | solution.py:247
  18.8 3.3 %collective-permute-start.4 = (f32[4,128]{1,0:T(4,128)S(1)}, f32[4,128]{1,0:T(4,128)S(1)}, u32[]{:S(2)}, u32[]{:S(2)}) collective-permute-start(f32[4,128]{1,0:T(4,128)S(1)} %add.3.a_ref), channel_id=1, source_target_pairs={{0,2},{1,3},{2,0},{3,1},{4,6},{5,7},{6,4},{7,5},{8,10},{9,11},{10,... | collective-permute-start | bytes 6152 | tf_op jit(solution)/shard_map/ppermute | solution.py:247
  22.1 1.6 %shard_map.128 = (f32[8,4,128,128]{3,2,1,0:T(8,128)}, f32[3,4,128,128]{3,2,1,0:T(8,128)S(1)}) custom-call(s32[9]{0:T(128)S(4)} %get-tuple-element.18.info_ref, s32[16]{0:T(128)S(4)} %get-tuple-element.19.flags_ref, f32[4,512]{1,0:T(4,128)S(1)} %get-tuple-element.20.fade_ref, f32[4,512]{1,0:T(4,128)S(1)} %get-tuple-element.30.back_ref, ...), custom_call_target="tpu_custom_call" | custom-call | flops 1000000 | bytes 1000000 | tf_op jit(solution)/shard_map/pallas_call | solution.py:227
  23.7 0.0 collective-permute-done.4.b_ref
  23.7 5.0 %collective-permute-start.5 = (f32[4,128]{1,0:T(4,128)S(1)}, f32[4,128]{1,0:T(4,128)S(1)}, u32[]{:S(2)}, u32[]{:S(2)}) collective-permute-start(f32[4,128]{1,0:T(4,128)S(1)} %shard_map.129.square_a_ref), channel_id=1, source_target_pairs={{0,6},{1,7},{2,4},{3,5},{4,2},{5,3},{6,0},{7,1},{8,14},{9,15},{10,... | collective-permute-start | bytes 6152 | tf_op jit(solution)/shard_map/ppermute | solution.py:247
  28.7 0.0 collective-permute-done.6.far_ref
  28.7 0.9 %shard_map.130.new_ref = f32[8,4,128,128]{3,2,1,0:T(8,128)} custom-call(s32[9]{0:T(128)S(4)} %get-tuple-element.18.info_ref, f32[4,512]{1,0:T(4,128)S(1)} %get-tuple-element.20.fade_ref, f32[3,4,128,128]{3,2,1,0:T(8,128)S(1)} %get-tuple-element.31.added_ref, f32[2,4,128,128]{3,2,1,0:T(8,128)S(1)} %collective-permute-done.6.far_ref, ...), custom_call_target="tpu_custom_call", output_to_operand_aliasing={{}: (5, {})} | custom-call | flops 100000 | bytes 100000 | tf_op jit(solution)/shard_map/pallas_call | solution.py:227
  29.6 0.6 %collective-permute-done.5.square_b_ref = f32[4,128]{1,0:T(4,128)S(1)} collective-permute-done((f32[4,128]{1,0:T(4,128)S(1)}, f32[4,128]{1,0:T(4,128)S(1)}, u32[]{:S(2)}, u32[]{:S(2)}) %collective-permute-start.5) | collective-permute-done | bytes 2080 | tf_op jit(solution)/shard_map/ppermute | solution.py:247
  30.3 0.7 %shard_map.131 = bf16[8,4,512]{2,1,0:T(4,128)(2,1)} custom-call(f32[8,4,512]{2,1,0:T(4,128)S(1)} %get-tuple-element.23.gate_ref, f32[8,4,512]{2,1,0:T(4,128)S(1)} %get-tuple-element.28.out_ref, f32[4,128]{1,0:T(4,128)S(1)} %shard_map.129.square_a_ref, f32[4,128]{1,0:T(4,128)S(1)} %collective-permute-done.5.square_b_ref, f32[8,4,128,128]{3,2,1,0:T(8,128)} %shard_map.130.new_ref), custom_call_target="tpu_custom_call" | custom-call | flops 100000 | bytes 100000 | tf_op jit(solution)/shard_map/pallas_call | solution.py:227
  (2 shorter events, 0.0 us)
Async XLA Ops:
  0.6 4.3 %copy-start = (f32[8,4,128,128]{3,2,1,0:T(8,128)S(1)}, f32[8,4,128,128]{3,2,1,0:T(8,128)}, u32[]{:S(2)}) copy-start(f32[8,4,128,128]{3,2,1,0:T(8,128)} %states_ref.5) | copy-start | bytes 6291460
  1.6 5.3 %collective-permute-start = (f32[2,4,512]{2,1,0:T(4,128)S(1)}, f32[2,4,512]{2,1,0:T(4,128)S(1)}, u32[]{:S(2)}, u32[]{:S(2)}) collective-permute-start(f32[2,4,512]{2,1,0:T(4,128)S(1)} %get-tuple-element.21), channel_id=1, source_target_pairs={{0,128},{8,136},{16,144},{24,152},{32,160},{40,168},{48,176},{56,1... | collective-permute-start | bytes 49160 | tf_op jit(solution)/shard_map/ppermute | solution.py:243
  4.9 0.8 %copy-start.3 = (bf16[8,4,512]{2,1,0:T(4,128)(2,1)S(1)}, bf16[8,4,512]{2,1,0:T(4,128)(2,1)}, u32[]{:S(2)}) copy-start(bf16[8,4,512]{2,1,0:T(4,128)(2,1)} %query_ref.5) | copy-start | bytes 98308
  4.9 5.5 %copy-start.1 = (bf16[8,4,512]{2,1,0:T(4,128)(2,1)S(1)}, bf16[8,4,512]{2,1,0:T(4,128)(2,1)}, u32[]{:S(2)}) copy-start(bf16[8,4,512]{2,1,0:T(4,128)(2,1)} %key_ref.3) | copy-start | bytes 98308
  4.9 5.5 %copy-start.2 = (bf16[8,4,512]{2,1,0:T(4,128)(2,1)S(1)}, bf16[8,4,512]{2,1,0:T(4,128)(2,1)}, u32[]{:S(2)}) copy-start(bf16[8,4,512]{2,1,0:T(4,128)(2,1)} %value_ref.3) | copy-start | bytes 98308
  4.9 5.5 %copy-start.4 = (bf16[8,4,512]{2,1,0:T(4,128)(2,1)S(1)}, bf16[8,4,512]{2,1,0:T(4,128)(2,1)}, u32[]{:S(2)}) copy-start(bf16[8,4,512]{2,1,0:T(4,128)(2,1)} %gate_ref.1) | copy-start | bytes 98308
  4.9 5.5 %copy-start.5 = (f32[512]{0:T(512)S(1)}, f32[512]{0:T(512)}, u32[]{:S(2)}) copy-start(f32[512]{0:T(512)} %param.21) | copy-start | bytes 6148
  5.0 9.9 %collective-permute-start.2 = (f32[1,4,128,128]{3,2,1,0:T(8,128)S(1)}, f32[1,4,128,128]{3,2,1,0:T(8,128)S(1)}, u32[]{:S(2)}, u32[]{:S(2)}) collective-permute-start(f32[1,4,128,128]{3,2,1,0:T(8,128)S(1)} %get-tuple-element.24), channel_id=1, source_target_pairs={{0,8},{8,16},{16,24},{24,32},{32,40},{40,48},{48,56},{56,64},{64,7... | collective-permute-start | bytes 786440 | tf_op jit(solution)/shard_map/ppermute | solution.py:243
  7.1 7.1 %collective-permute-start.1 = (f32[2,4,512]{2,1,0:T(4,128)S(1)}, f32[2,4,512]{2,1,0:T(4,128)S(1)}, u32[]{:S(2)}, u32[]{:S(2)}) collective-permute-start(f32[2,4,512]{2,1,0:T(4,128)S(1)} %shard_map.125.answer_ref), channel_id=1, source_target_pairs={{0,128},{8,136},{16,144},{24,152},{32,160},{40,168},{48,176},{56,1... | collective-permute-start | bytes 49160 | tf_op jit(solution)/shard_map/ppermute | solution.py:243
  11.0 17.7 %collective-permute-start.6 = (f32[2,4,128,128]{3,2,1,0:T(8,128)S(1)}, f32[2,4,128,128]{3,2,1,0:T(8,128)S(1)}, u32[]{:S(2)}, u32[]{:S(2)}) collective-permute-start(f32[2,4,128,128]{3,2,1,0:T(8,128)S(1)} %get-tuple-element.32), channel_id=1, source_target_pairs={{0,128},{8,136},{16,144},{24,152},{32,160},{40,168},{48,176},{56,1... | collective-permute-start | bytes 1572872 | tf_op jit(solution)/shard_map/ppermute | solution.py:243
  15.2 3.6 %collective-permute-start.3 = (f32[4,128]{1,0:T(4,128)S(1)}, f32[4,128]{1,0:T(4,128)S(1)}, u32[]{:S(2)}, u32[]{:S(2)}) collective-permute-start(f32[4,128]{1,0:T(4,128)S(1)} %get-tuple-element.29.square_ref), channel_id=1, source_target_pairs={{0,1},{1,0},{2,3},{3,2},{4,5},{5,4},{6,7},{7,6},{8,9},{9,8},{10,11... | collective-permute-start | bytes 6152 | tf_op jit(solution)/shard_map/ppermute | solution.py:247
  18.8 4.9 %collective-permute-start.4 = (f32[4,128]{1,0:T(4,128)S(1)}, f32[4,128]{1,0:T(4,128)S(1)}, u32[]{:S(2)}, u32[]{:S(2)}) collective-permute-start(f32[4,128]{1,0:T(4,128)S(1)} %add.3.a_ref), channel_id=1, source_target_pairs={{0,2},{1,3},{2,0},{3,1},{4,6},{5,7},{6,4},{7,5},{8,10},{9,11},{10,... | collective-permute-start | bytes 6152 | tf_op jit(solution)/shard_map/ppermute | solution.py:247
  23.7 6.5 %collective-permute-start.5 = (f32[4,128]{1,0:T(4,128)S(1)}, f32[4,128]{1,0:T(4,128)S(1)}, u32[]{:S(2)}, u32[]{:S(2)}) collective-permute-start(f32[4,128]{1,0:T(4,128)S(1)} %shard_map.129.square_a_ref), channel_id=1, source_target_pairs={{0,6},{1,7},{2,4},{3,5},{4,2},{5,3},{6,0},{7,1},{8,14},{9,15},{10,... | collective-permute-start | bytes 6152 | tf_op jit(solution)/shard_map/ppermute | solution.py:247
